TPU v7x, 128 devices: a whole 4x4x4 slice. The times are simulated.
128 devices in a mesh: ex: 16 (over z, y), ey: 8 (over x, core).
Axes of the slice: x: 4, y: 4, z: 4, core: 2. Of those that a mesh axis runs over, the one named last changes fastest.
Arguments:
- fields: float32 [65536, 3, 512], P(('ex', 'ey')), may hold values from -6 to 6
- particles: float32 [65536, 128], P(('ex', 'ey')), as said below
- counts: int32 [65536], P(('ex', 'ey')), may hold values from 1 to 16
- new_place: int32 [65536], P(('ex', 'ey')), may hold values from 0 to 65535, as said below
Outputs:
- velocity_next: float32 [65536, 3, 512], P(('ex', 'ey'))
- particles_next: float32 [65536, 128], P(('ex', 'ey'))
Inputs may be any that keep to these rules, and one draw needn't show every extreme that they name: new_place is a permutation of all elements; each device sends either none or exactly 4 of its elements to any other device, keeps the rest in place, and receives as many as it sends. `particles`: coordinates lie in [-1, 1], ratios in [0.1, 0.9], masses in [0.5, 2].
All inputs are finite; a program needn't handle non-finite values.
Results may differ from a plain program's by a relative error of at most 0.0003.
Values sent between devices are 32-bit elements; how exact they have to be, the bound alone decides.
No kernel may reach another device: no remote copies, remote signals or barrier semaphores. Data moves between devices by JAX's collectives and lax.ppermute only.
A program may use at most 128 MiB of HBM per device.

v0:
```python
import functools

import jax
import jax.numpy as jnp
import numpy as np
from jax import lax
from jax.experimental import pallas as pl
from jax.experimental.pallas import tpu as pltpu
from jax.sharding import PartitionSpec as P

NP = 8
SLOTS = 16
CAP = 4
BX = 4
BY = 8
BZ = 16
NODES = NP**3
EL = BX * BY * BZ
LANES = 128
PARTS = 8 * SLOTS
HEAD = 8
COMP = 16
AXES = ("ex", "ey")
POINTS = [
    -1.0,
    -0.8717401485096066,
    -0.5917001814331423,
    -0.2092992179024789,
    0.2092992179024789,
    0.5917001814331423,
    0.8717401485096066,
    1.0,
]
F32 = jnp.float32
BF16 = jnp.bfloat16
VMEM_LIMIT = 56 * 1024 * 1024


def iota(shape, axis):
    return lax.broadcasted_iota(jnp.int32, shape, axis)


def split(x):
    high = x.astype(BF16)
    return high, (x - high.astype(F32)).astype(BF16)


def picked(onehot, x):
    high, low = split(x)
    return jnp.dot(onehot, high, preferred_element_type=F32) + jnp.dot(
        onehot, low, preferred_element_type=F32
    )


def as_column(row):
    return jnp.broadcast_to(row, (LANES, EL)).T


def pack_positions(place, rank):
    target = place // EL
    moving = target != rank
    key = jnp.where(moving, target, -1).astype(F32)
    key_col = as_column(key)
    order = []
    for j in range(EL // LANES):
        piece = key[:, j * LANES : (j + 1) * LANES]
        earlier = iota((EL, LANES), 0) < iota((EL, LANES), 1) + j * LANES
        same = (key_col == piece) & earlier
        order.append(jnp.sum(same.astype(F32), axis=0, keepdims=True))
    order = jnp.concatenate(order, axis=1).astype(jnp.int32)
    return jnp.where(moving, target * CAP + order, -1)


def interleave(first, second):
    devices = first.shape[0] // CAP
    low = iota((devices // 2, 8, LANES), 1) < CAP
    first = first.reshape(devices // 2, 8, LANES)
    second = second.reshape(devices // 2, 8, LANES)
    even = jnp.where(low, first, pltpu.roll(second, CAP, 1))
    odd = jnp.where(low, pltpu.roll(first, CAP, 1), second)
    return jnp.stack([even, odd], axis=1).reshape(devices, 8, LANES)


def deinterleave(blocks):
    devices = blocks.shape[0]
    pairs = blocks.reshape(devices // 2, 2, 8, LANES)
    even, odd = pairs[:, 0], pairs[:, 1]
    low = iota((devices // 2, 8, LANES), 1) < CAP
    first = jnp.where(low, even, pltpu.roll(odd, CAP, 1))
    second = jnp.where(low, pltpu.roll(even, CAP, 1), odd)
    return first.reshape(devices * CAP, LANES), second.reshape(devices * CAP, LANES)


def pack_kernel(rank_ref, place_ref, count_ref, fields_ref, part_ref, out_ref):
    devices = out_ref.shape[0]
    place = place_ref[...]
    position = pack_positions(place, rank_ref[0])
    onehot = (iota((devices * CAP, EL), 0) == position).astype(BF16)
    extra = jnp.concatenate(
        [count_ref[...], place % EL + 1, jnp.zeros((LANES - 2, EL), jnp.int32)], axis=0
    )
    extra = extra.astype(F32).T
    rows = picked(onehot, jnp.concatenate([part_ref[...], extra], axis=1))
    out_ref[:, 0:HEAD, :] = interleave(rows[:, :LANES], rows[:, LANES:])
    for f in range(3):
        rows = picked(onehot, fields_ref[f])
        for h in range(2):
            at = HEAD + COMP * f + 8 * h
            left = 2 * h * LANES
            out_ref[:, at : at + 8, :] = interleave(
                rows[:, left : left + LANES], rows[:, left + LANES : left + 2 * LANES]
            )


def lagrange_rows(coord):
    diffs = [coord - p for p in POINTS]
    left = [None] * NP
    right = [None] * NP
    for i in range(1, NP):
        left[i] = diffs[i - 1] if i == 1 else left[i - 1] * diffs[i - 1]
    for i in range(NP - 2, -1, -1):
        right[i] = diffs[i + 1] if i == NP - 2 else right[i + 1] * diffs[i + 1]
    out = []
    for i in range(NP):
        scale = 1.0
        for m in range(NP):
            if m != i:
                scale /= POINTS[i] - POINTS[m]
        if i == 0:
            term = right[0]
        elif i == NP - 1:
            term = left[i]
        else:
            term = left[i] * right[i]
        out.append(term * float(scale))
    return out


def gaussian_rows(coord):
    return [jnp.exp(-((p - coord) ** 2) * (0.5 / 0.35**2)) for p in POINTS]


def shift_z(x):
    n = x.shape[0] // NP
    x = x.reshape(n, NP, LANES)
    node = iota((n, NP, LANES), 1)
    bz = iota((n, NP, LANES), 2) % BZ
    down = pltpu.roll(pltpu.roll(x, 1, 1), 1, 2)
    up = pltpu.roll(pltpu.roll(x, NP - 1, 1), LANES - 1, 2)
    x = x + jnp.where((node == 0) & (bz > 0), down, 0.0)
    x = x + jnp.where((node == NP - 1) & (bz < BZ - 1), up, 0.0)
    return x.reshape(n * NP, LANES)


def section_kernel(
    rank_ref,
    place_ref,
    count_ref,
    fields_ref,
    part_ref,
    recv_ref,
    z_ref,
    xup_ref,
    xdn_ref,
    yup_ref,
    ydn_ref,
    part_out_ref,
    onehot_ref,
    stay_ref,
    tp_ref,
    basis_ref,
    t_ref,
    force_ref,
    work_ref,
    push_ref,
    live_ref,
):
    tiles = EL // LANES
    particles, extra = deinterleave(recv_ref[:, 0:HEAD, :])
    slot_row = extra.T[1:2, :]
    onehot = (iota((EL, EL), 0) + 1 == slot_row.astype(jnp.int32)).astype(BF16)
    onehot_ref[...] = onehot
    stay = (place_ref[...] // EL == rank_ref[0]).astype(F32)
    stay_col = as_column(stay)
    stay_ref[...] = stay_col
    both = picked(onehot, jnp.concatenate([particles, extra], axis=1))
    moved_part = jnp.where(stay_col > 0, part_ref[...], both[:, :LANES]).T
    moved_count = jnp.where(stay > 0, count_ref[...].astype(F32), both[:, LANES:].T[0:1, :])
    for t in range(tiles):
        tp_ref[t] = moved_part[:, t * LANES : (t + 1) * LANES]
        slot = iota((SLOTS, LANES), 0).astype(F32)
        live_ref[t] = (slot < moved_count[:, t * LANES : (t + 1) * LANES]).astype(F32)

    def make_basis(t, carry):
        for d in range(3):
            coord = tp_ref[t, d * SLOTS : (d + 1) * SLOTS, :]
            for kind, rows in ((0, lagrange_rows(coord)), (1, gaussian_rows(coord))):
                for n in range(NP):
                    basis_ref[t, 2 * d + kind, n * SLOTS : (n + 1) * SLOTS, :] = rows[n]
        return carry

    lax.fori_loop(0, tiles, make_basis, 0)

    for f in range(3):
        pieces = []
        for h in range(2):
            at = HEAD + COMP * f + 8 * h
            pieces += list(deinterleave(recv_ref[:, at : at + 8, :]))
        rows = picked(onehot_ref[...], jnp.concatenate(pieces, axis=1))
        for j in range(NODES // LANES):
            cols = slice(j * LANES, (j + 1) * LANES)
            moved = jnp.where(stay_ref[...] > 0, fields_ref[f, :, cols], rows[:, cols]).T
            for t in range(tiles):
                t_ref[f, t, cols, :] = moved[:, t * LANES : (t + 1) * LANES]

    def step(index, carry):
        f = index // tiles
        t = index % tiles

        def basis(which, n, p):
            return basis_ref[t, which, pl.ds(n * SLOTS + p, 1), :]

        total = [None] * SLOTS
        for pair in range(NP // 2):
            nodes = [
                [t_ref[f, t, pl.ds(a * 64 + (2 * pair + i) * 8, 8), :] for a in range(NP)]
                for i in range(2)
            ]
            for p in range(SLOTS):
                sums = [None, None]
                for a in range(NP):
                    weight = basis(0, a, p)
                    for i in range(2):
                        term = nodes[i][a] * weight
                        sums[i] = term if sums[i] is None else sums[i] + term
                for i in range(2):
                    term = sums[i] * basis(2, 2 * pair + i, p)
                    total[p] = term if total[p] is None else total[p] + term
        for p in range(SLOTS):
            along_z = basis_ref[t, 4, pl.ds(p, NP, stride=SLOTS), :]
            work_ref[p * NP : (p + 1) * NP, :] = total[p] * along_z
        fluid = work_ref[pl.ds(0, SLOTS, stride=NP), :]
        for c in range(1, NP):
            fluid = fluid + work_ref[pl.ds(c, SLOTS, stride=NP), :]
        where = pl.ds(pl.multiple_of((3 + f) * SLOTS, SLOTS), SLOTS)
        velocity = tp_ref[t, where, :]
        ratio = tp_ref[t, 6 * SLOTS : 7 * SLOTS, :]
        mass = tp_ref[t, 7 * SLOTS : 8 * SLOTS, :]
        drag = live_ref[t] * ratio * (fluid - velocity)
        tp_ref[t, where, :] = velocity + drag
        push_ref[...] = -(mass * drag)
        for p in range(SLOTS):
            along_z = basis_ref[t, 5, pl.ds(p, NP, stride=SLOTS), :]
            work_ref[p * NP : (p + 1) * NP, :] = push_ref[pl.ds(p, 1), :] * along_z
        for pair in range(NP // 2):
            acc = [[None] * NP for _ in range(2)]
            for p in range(SLOTS):
                base = work_ref[p * NP : (p + 1) * NP, :]
                lines = [base * basis(3, 2 * pair + i, p) for i in range(2)]
                for a in range(NP):
                    weight = basis(1, a, p)
                    for i in range(2):
                        term = lines[i] * weight
                        acc[i][a] = term if acc[i][a] is None else acc[i][a] + term
            for i in range(2):
                for a in range(NP):
                    force_ref[f, t, pl.ds(a * 64 + (2 * pair + i) * 8, 8), :] = acc[i][a]
        return carry

    lax.fori_loop(0, 3 * tiles, step, 0)

    lane = iota((NP, LANES), 1)
    for f in range(3):
        xup_ref[f] = force_ref[f, tiles - 1, 448:512, :]
        xdn_ref[f] = force_ref[f, 0, 0:64, :]
        for t in range(tiles - 1):
            summed = force_ref[f, t, 448:512, :] + force_ref[f, t + 1, 0:64, :]
            force_ref[f, t, 448:512, :] = summed
            force_ref[f, t + 1, 0:64, :] = summed
        for a in range(NP):
            first = slice(a * 64, a * 64 + 8)
            last = slice(a * 64 + 56, a * 64 + 64)
            up_line = jnp.zeros((NP, LANES), F32)
            down_line = jnp.zeros((NP, LANES), F32)
            for t in range(tiles):
                upper = force_ref[f, t, last, :]
                lower = force_ref[f, t, first, :]
                take = lane // BZ == t
                up_line = jnp.where(take, pltpu.roll(upper, (16 * t + 16) % LANES, 1), up_line)
                down_line = jnp.where(take, pltpu.roll(lower, (16 * t) % LANES, 1) if t else lower, down_line)
                force_ref[f, t, first, :] = lower + jnp.where(lane >= BZ, pltpu.roll(upper, BZ, 1), 0.0)
                force_ref[f, t, last, :] = upper + jnp.where(
                    lane < LANES - BZ, pltpu.roll(lower, LANES - BZ, 1), 0.0
                )
            yup_ref[f, a * 8 : a * 8 + 8, :] = up_line
            ydn_ref[f, a * 8 : a * 8 + 8, :] = down_line
        bz = iota((64, LANES), 1) % BZ
        for t in range(tiles):
            lower = force_ref[f, t, pl.ds(0, 64, stride=NP), :]
            upper = force_ref[f, t, pl.ds(NP - 1, 64, stride=NP), :]
            force_ref[f, t, pl.ds(0, 64, stride=NP), :] = lower + jnp.where(
                bz > 0, pltpu.roll(upper, 1, 1), 0.0
            )
            force_ref[f, t, pl.ds(NP - 1, 64, stride=NP), :] = upper + jnp.where(
                bz < BZ - 1, pltpu.roll(lower, LANES - 1, 1), 0.0
            )
            z_ref[f, t] = t_ref[f, t] + 0.5 * force_ref[f, t]
    for t in range(tiles):
        part_out_ref[t * LANES : (t + 1) * LANES, :] = tp_ref[t].T


def edge_kernel(below_ref, above_ref, yup_ref, ydn_ref, up_ref, down_ref):
    lane = iota((NP, LANES), 1)
    first = lane < BZ
    last = (lane >= 3 * BZ) & (lane < 4 * BZ)
    for f in range(3):
        up_ref[f] = yup_ref[f]
        down_ref[f] = ydn_ref[f]
        up_ref[f, 0:8, :] += jnp.where(first, pltpu.roll(below_ref[f, 56:64, :], BZ, 1), 0.0)
        up_ref[f, 56:64, :] += jnp.where(last, pltpu.roll(above_ref[f, 56:64, :], 4 * BZ, 1), 0.0)
        down_ref[f, 0:8, :] += jnp.where(first, below_ref[f, 0:8, :], 0.0)
        down_ref[f, 56:64, :] += jnp.where(last, pltpu.roll(above_ref[f, 0:8, :], 3 * BZ, 1), 0.0)


def face_delta(face):
    lane = iota((NP, LANES), 1)
    upper = face[56:64]
    lower = face[0:8]
    new_lower = lower + jnp.where(lane >= BZ, pltpu.roll(upper, BZ, 1), 0.0)
    new_upper = upper + jnp.where(lane < LANES - BZ, pltpu.roll(lower, LANES - BZ, 1), 0.0)
    return shift_z(0.5 * jnp.concatenate([new_lower, face[8:56], new_upper], axis=0))


def finish_kernel(z_ref, xb_ref, xa_ref, yb_ref, ya_ref, out_ref, zs_ref):
    tiles = EL // LANES
    zs_ref[...] = z_ref[0]
    zs_ref[0, 0:64, :] += face_delta(xb_ref[0])
    zs_ref[tiles - 1, 448:512, :] += face_delta(xa_ref[0])
    lane = iota((64, LANES), 1)
    for t in range(tiles):
        moved = pltpu.roll(yb_ref[0], LANES - BZ * t, 1) if t else yb_ref[0]
        below = shift_z(0.5 * jnp.where(lane < BZ, moved, 0.0))
        moved = pltpu.roll(ya_ref[0], LANES - BZ - BZ * t, 1)
        above = shift_z(0.5 * jnp.where(lane >= LANES - BZ, moved, 0.0))
        for a in range(NP):
            zs_ref[t, a * 64 : a * 64 + 8, :] += below[a * 8 : a * 8 + 8]
            zs_ref[t, a * 64 + 56 : a * 64 + 64, :] += above[a * 8 : a * 8 + 8]
        out_ref[0, t * LANES : (t + 1) * LANES, :] = zs_ref[t].T


def passed_along(x, axis, by):
    size = lax.axis_size(axis)
    pairs = [(i, i + by) for i in range(size) if 0 <= i + by < size]
    return lax.ppermute(x, axis, pairs)


def whole(n):
    return [pl.BlockSpec(memory_space=pltpu.VMEM)] * n


def params():
    return pltpu.CompilerParams(vmem_limit_bytes=VMEM_LIMIT)


def body(fields, particles, counts, new_place):
    devices = lax.axis_size(AXES)
    rank = lax.axis_index(AXES).astype(jnp.int32).reshape(1)
    fields = jnp.transpose(fields, (1, 0, 2))
    place = new_place.reshape(1, EL)
    counts = counts.reshape(1, EL)
    smem = [pl.BlockSpec(memory_space=pltpu.SMEM)]
    rows = HEAD + 3 * COMP
    struct = jax.ShapeDtypeStruct
    send = pl.pallas_call(
        pack_kernel,
        out_shape=struct((devices, rows, LANES), F32),
        in_specs=smem + whole(4),
        out_specs=whole(1)[0],
        compiler_params=params(),
        name="pack",
    )(rank, place, counts, fields, particles)
    recv = lax.all_to_all(send, AXES, split_axis=0, concat_axis=0, tiled=True)
    tiles = EL // LANES
    face = struct((3, 64, LANES), F32)
    z, xup, xdn, yup, ydn, particles_next = pl.pallas_call(
        section_kernel,
        out_shape=(struct((3, tiles, NODES, LANES), F32), face, face, face, face, struct((EL, PARTS), F32)),
        in_specs=smem + whole(5),
        out_specs=tuple(whole(6)),
        scratch_shapes=[
            pltpu.VMEM((EL, EL), BF16),
            pltpu.VMEM((EL, LANES), F32),
            pltpu.VMEM((tiles, LANES, LANES), F32),
            pltpu.VMEM((tiles, 6, LANES, LANES), F32),
            pltpu.VMEM((3, tiles, NODES, LANES), F32),
            pltpu.VMEM((3, tiles, NODES, LANES), F32),
            pltpu.VMEM((LANES, LANES), F32),
            pltpu.VMEM((SLOTS, LANES), F32),
            pltpu.VMEM((tiles, SLOTS, LANES), F32),
        ],
        compiler_params=params(),
        name="section",
    )(rank, place, counts, fields, particles, recv)
    below_x = passed_along(xup, "ex", 1)
    above_x = passed_along(xdn, "ex", -1)
    up, down = pl.pallas_call(
        edge_kernel,
        out_shape=(face, face),
        in_specs=whole(4),
        out_specs=tuple(whole(2)),
        compiler_params=params(),
        name="edge",
    )(below_x, above_x, yup, ydn)
    below_y = passed_along(up, "ey", 1)
    above_y = passed_along(down, "ey", -1)
    halo = pl.BlockSpec((1, 64, LANES), lambda f: (f, 0, 0))
    out = pl.pallas_call(
        finish_kernel,
        grid=(3,),
        out_shape=struct((3, EL, NODES), F32),
        in_specs=[pl.BlockSpec((1, tiles, NODES, LANES), lambda f: (f, 0, 0, 0)), halo, halo, halo, halo],
        out_specs=pl.BlockSpec((1, EL, NODES), lambda f: (f, 0, 0)),
        scratch_shapes=[pltpu.VMEM((tiles, NODES, LANES), F32)],
        compiler_params=params(),
        name="finish",
    )(z, below_x, above_x, below_y, above_y)
    return jnp.transpose(out, (1, 0, 2)), particles_next


def solution(mesh):
    return jax.shard_map(
        body,
        mesh=mesh,
        in_specs=(P(AXES, None, None), P(AXES, None), P(AXES), P(AXES)),
        out_specs=(P(AXES, None, None), P(AXES, None)),
        check_vma=False,
    )
```

profile of v0, /device:TPU:27, one launch (start us, length us, event | category | flops | bytes accessed | tf_op | source)
XLA Modules:
  0.0 109.4 jit_solution(6324592245693074502)
XLA Ops:
  0.6 6.0 %pack.1 = f32[128,56,128]{2,1,0:T(8,128)} custom-call(s32[1]{0:T(128)} %bitcast.rank_ref, s32[1,512]{1,0:T(1,128)} %bitcast.8, s32[1,512]{1,0:T(1,128)} %bitcast.10, f32[3,512,512]{2,1,0:T(8,128)} %bitcast.5, f32[512,128]{1,0:T(8,128)} %part_ref.3), custom_call_target="tpu_custom_call" | custom-call | tf_op jit(solution)/shard_map/pack/pallas_call | solution.py:374
  6.7 54.7 %all_to_all.5.recv_ref = f32[128,56,128]{2,1,0:T(8,128)} all-to-all(f32[128,56,128]{2,1,0:T(8,128)} %pack.1), channel_id=1, replica_groups=mesh['ex'=16,'ey'=8] {'ex','ey'}, dimensions={0} | all-to-all | bytes 7340032 | tf_op jit(solution)/shard_map/all_to_all | solution.py:382
  61.3 16.8 %section.1 = (f32[3,4,512,128]{3,2,1,0:T(8,128)}, f32[3,64,128]{2,1,0:T(8,128)}, f32[3,64,128]{2,1,0:T(8,128)}, f32[3,64,128]{2,1,0:T(8,128)}, f32[3,64,128]{2,1,0:T(8,128)}, /*index=5*/f32[512,128]{1,0:T(8,128)}) custom-call(s32[1]{0:T(128)} %bitcast.rank_ref, s32[1,512]{1,0:T(1,128)} %bitcast.9, s32[1,512]{1,0:T(1,128)} %bitcast.11, ...), custom_call_target="tpu_custom_call" | custom-call | tf_op jit(solution)/shard_map/section/pallas_call | solution.py:385
  78.1 2.8 %collective-permute-start = (f32[3,64,128]{2,1,0:T(8,128)}, f32[3,64,128]{2,1,0:T(8,128)S(1)}, u32[]{:S(2)}, u32[]{:S(2)}) collective-permute-start(f32[3,64,128]{2,1,0:T(8,128)} %get-tuple-element.11), channel_id=1, source_target_pairs={{0,8},{8,16},{16,24},{24,32},{32,40},{40,48},{48,56},{56,64},{64,7... | collective-permute-start | bytes 294920 | tf_op jit(solution)/shard_map/ppermute | solution.py:354
  80.9 2.5 %collective-permute-start.1 = (f32[3,64,128]{2,1,0:T(8,128)}, f32[3,64,128]{2,1,0:T(8,128)S(1)}, u32[]{:S(2)}, u32[]{:S(2)}) collective-permute-start(f32[3,64,128]{2,1,0:T(8,128)} %get-tuple-element.12), channel_id=1, source_target_pairs={{8,0},{16,8},{24,16},{32,24},{40,32},{48,40},{56,48},{64,56},{72,6... | collective-permute-start | bytes 294920 | tf_op jit(solution)/shard_map/ppermute | solution.py:354
  83.4 0.3 collective-permute-done.below_ref.xb_ref
  83.6 0.0 copy-start
  83.6 4.9 %collective-permute-done.1.above_ref.xa_ref = f32[3,64,128]{2,1,0:T(8,128)S(1)} collective-permute-done((f32[3,64,128]{2,1,0:T(8,128)}, f32[3,64,128]{2,1,0:T(8,128)S(1)}, u32[]{:S(2)}, u32[]{:S(2)}) %collective-permute-start.1) | collective-permute-done | bytes 98336 | tf_op jit(solution)/shard_map/ppermute | solution.py:354
  88.5 0.0 copy-start.1
  88.5 0.0 copy-done
  88.5 0.6 copy-done.1
  89.2 1.8 %edge.1 = (f32[3,64,128]{2,1,0:T(8,128)}, f32[3,64,128]{2,1,0:T(8,128)}) custom-call(f32[3,64,128]{2,1,0:T(8,128)} %copy-done, f32[3,64,128]{2,1,0:T(8,128)} %copy-done.1, f32[3,64,128]{2,1,0:T(8,128)} %get-tuple-element.13.yup_ref, f32[3,64,128]{2,1,0:T(8,128)} %get-tuple-element.14.ydn_ref), custom_call_target="tpu_custom_call" | custom-call | tf_op jit(solution)/shard_map/edge/pallas_call | solution.py:406
  90.9 5.7 %collective-permute-start.2 = (f32[3,64,128]{2,1,0:T(8,128)}, f32[3,64,128]{2,1,0:T(8,128)S(1)}, u32[]{:S(2)}, u32[]{:S(2)}) collective-permute-start(f32[3,64,128]{2,1,0:T(8,128)} %get-tuple-element.15), channel_id=1, source_target_pairs={{0,1},{1,2},{2,3},{3,4},{4,5},{5,6},{6,7},{8,9},{9,10},{10,11},{11... | collective-permute-start | bytes 294920 | tf_op jit(solution)/shard_map/ppermute | solution.py:354
  96.7 1.9 %collective-permute-start.3 = (f32[3,64,128]{2,1,0:T(8,128)}, f32[3,64,128]{2,1,0:T(8,128)S(1)}, u32[]{:S(2)}, u32[]{:S(2)}) collective-permute-start(f32[3,64,128]{2,1,0:T(8,128)} %get-tuple-element.16), channel_id=1, source_target_pairs={{1,0},{2,1},{3,2},{4,3},{5,4},{6,5},{7,6},{9,8},{10,9},{11,10},{12... | collective-permute-start | bytes 294920 | tf_op jit(solution)/shard_map/ppermute | solution.py:354
  98.6 0.0 collective-permute-done.2.yb_ref
  98.6 0.0 copy-start.2
  98.6 4.2 %collective-permute-done.3.ya_ref = f32[3,64,128]{2,1,0:T(8,128)S(1)} collective-permute-done((f32[3,64,128]{2,1,0:T(8,128)}, f32[3,64,128]{2,1,0:T(8,128)S(1)}, u32[]{:S(2)}, u32[]{:S(2)}) %collective-permute-start.3) | collective-permute-done | bytes 98336 | tf_op jit(solution)/shard_map/ppermute | solution.py:354
  102.8 0.0 copy-start.3
  102.8 0.0 copy-done.2
  102.8 0.6 copy-done.3
  103.5 5.9 %finish.1 = f32[3,512,512]{2,1,0:T(8,128)} custom-call(f32[3,4,512,128]{3,2,1,0:T(8,128)} %get-tuple-element.10.z_ref, f32[3,64,128]{2,1,0:T(8,128)} %copy-done, f32[3,64,128]{2,1,0:T(8,128)} %copy-done.1, f32[3,64,128]{2,1,0:T(8,128)} %copy-done.2, f32[3,64,128]{2,1,0:T(8,128)} %copy-done.3), custom_call_target="tpu_custom_call" | custom-call | tf_op jit(solution)/shard_map/finish/pallas_call | solution.py:417
Async XLA Ops:
  78.1 5.6 %collective-permute-start = (f32[3,64,128]{2,1,0:T(8,128)}, f32[3,64,128]{2,1,0:T(8,128)S(1)}, u32[]{:S(2)}, u32[]{:S(2)}) collective-permute-start(f32[3,64,128]{2,1,0:T(8,128)} %get-tuple-element.11), channel_id=1, source_target_pairs={{0,8},{8,16},{16,24},{24,32},{32,40},{40,48},{48,56},{56,64},{64,7... | collective-permute-start | bytes 294920 | tf_op jit(solution)/shard_map/ppermute | solution.py:354
  80.9 7.7 %collective-permute-start.1 = (f32[3,64,128]{2,1,0:T(8,128)}, f32[3,64,128]{2,1,0:T(8,128)S(1)}, u32[]{:S(2)}, u32[]{:S(2)}) collective-permute-start(f32[3,64,128]{2,1,0:T(8,128)} %get-tuple-element.12), channel_id=1, source_target_pairs={{8,0},{16,8},{24,16},{32,24},{40,32},{48,40},{56,48},{64,56},{72,6... | collective-permute-start | bytes 294920 | tf_op jit(solution)/shard_map/ppermute | solution.py:354
  83.6 4.9 %copy-start = (f32[3,64,128]{2,1,0:T(8,128)}, f32[3,64,128]{2,1,0:T(8,128)S(1)}, u32[]{:S(2)}) copy-start(f32[3,64,128]{2,1,0:T(8,128)S(1)} %collective-permute-done.below_ref.xb_ref) | copy-start | bytes 294916
  88.5 0.6 copy-start.1
  90.9 7.7 %collective-permute-start.2 = (f32[3,64,128]{2,1,0:T(8,128)}, f32[3,64,128]{2,1,0:T(8,128)S(1)}, u32[]{:S(2)}, u32[]{:S(2)}) collective-permute-start(f32[3,64,128]{2,1,0:T(8,128)} %get-tuple-element.15), channel_id=1, source_target_pairs={{0,1},{1,2},{2,3},{3,4},{4,5},{5,6},{6,7},{8,9},{9,10},{10,11},{11... | collective-permute-start | bytes 294920 | tf_op jit(solution)/shard_map/ppermute | solution.py:354
  96.7 6.1 %collective-permute-start.3 = (f32[3,64,128]{2,1,0:T(8,128)}, f32[3,64,128]{2,1,0:T(8,128)S(1)}, u32[]{:S(2)}, u32[]{:S(2)}) collective-permute-start(f32[3,64,128]{2,1,0:T(8,128)} %get-tuple-element.16), channel_id=1, source_target_pairs={{1,0},{2,1},{3,2},{4,3},{5,4},{6,5},{7,6},{9,8},{10,9},{11,10},{12... | collective-permute-start | bytes 294920 | tf_op jit(solution)/shard_map/ppermute | solution.py:354
  98.6 4.2 %copy-start.2 = (f32[3,64,128]{2,1,0:T(8,128)}, f32[3,64,128]{2,1,0:T(8,128)S(1)}, u32[]{:S(2)}) copy-start(f32[3,64,128]{2,1,0:T(8,128)S(1)} %collective-permute-done.2.yb_ref) | copy-start | bytes 294916
  102.8 0.6 copy-start.3
where the time goes:
time: 110 us; the launch traced here: 109 us
  blocking collectives  54.7 us (50%)
  Pallas kernels  30.5 us (28%)
  starting transfers between devices  12.9 us (12%)
  waiting for transfers between devices  9.38 us (9%)
  local copies, waits for them, and re-layouts  1.27 us (1%)
    all_to_all x1, blocking collectives, body(): recv = lax.all_to_all(send, AXES, split_axis=0, concat_axis=0, tiled=True)  54.7 us
    pallas_call x1, Pallas kernels, body(): pl.pallas_call(section_kernel, out_shape=(struct((3, tiles, NODES, LANES)...  16.8 us
    ppermute x4, starting transfers between devices, passed_along(): return lax.ppermute(x, axis, pairs)  12.9 us
    ppermute x4, waiting for transfers between devices, passed_along(): return lax.ppermute(x, axis, pairs)  9.38 us
    pallas_call x1, Pallas kernels, body(): pl.pallas_call(pack_kernel, out_shape=struct((devices, rows, LANES), F32)...  6.03 us
    pallas_call x1, Pallas kernels, body(): pl.pallas_call(finish_kernel, grid=(3,), out_shape=struct((3, EL, NODES),...  5.91 us
  transfers between devices with their start and end apart: 4, of which 3 were waited for; matrix products, arithmetic and copies ran while one was open for 0% of the time, Pallas kernels for 0%

commit v1 on v0

v1 whole, which is shorter than its diff:
```python
import functools

import jax
import jax.numpy as jnp
import numpy as np
from jax import lax
from jax.experimental import pallas as pl
from jax.experimental.pallas import tpu as pltpu
from jax.sharding import PartitionSpec as P

NP = 8
SLOTS = 16
CAP = 4
PEERS = 64
BX = 4
BY = 8
BZ = 16
NODES = NP**3
EL = BX * BY * BZ
MOVERS = PEERS * CAP
LANES = 128
PARTS = 8 * SLOTS
HEAD = 8
COMP = 16
AXES = ("ex", "ey")
POINTS = [
    -1.0,
    -0.8717401485096066,
    -0.5917001814331423,
    -0.2092992179024789,
    0.2092992179024789,
    0.5917001814331423,
    0.8717401485096066,
    1.0,
]
F32 = jnp.float32
BF16 = jnp.bfloat16
MIB = 1024 * 1024


def iota(shape, axis):
    return lax.broadcasted_iota(jnp.int32, shape, axis)


def split(x):
    high = x.astype(BF16)
    return high, (x - high.astype(F32)).astype(BF16)


def picked(onehot, x):
    high, low = split(x)
    return jnp.dot(onehot, high, preferred_element_type=F32) + jnp.dot(
        onehot, low, preferred_element_type=F32
    )


def as_column(row):
    return jnp.broadcast_to(row, (LANES, EL)).T


def pack_positions(place, rank):
    target = place // EL
    moving = target != rank
    key = jnp.where(moving, target, -1).astype(F32)
    key_col = as_column(key)
    order = []
    for j in range(EL // LANES):
        piece = key[:, j * LANES : (j + 1) * LANES]
        earlier = iota((EL, LANES), 0) < iota((EL, LANES), 1) + j * LANES
        same = (key_col == piece) & earlier
        order.append(jnp.sum(same.astype(F32), axis=0, keepdims=True))
    order = jnp.concatenate(order, axis=1).astype(jnp.int32)
    return jnp.where(moving, target * CAP + order, -1)


def interleave(first, second):
    devices = first.shape[0] // CAP
    low = iota((devices // 2, 8, LANES), 1) < CAP
    first = first.reshape(devices // 2, 8, LANES)
    second = second.reshape(devices // 2, 8, LANES)
    even = jnp.where(low, first, pltpu.roll(second, CAP, 1))
    odd = jnp.where(low, pltpu.roll(first, CAP, 1), second)
    return jnp.stack([even, odd], axis=1).reshape(devices, 8, LANES)


def deinterleave(blocks):
    devices = blocks.shape[0]
    pairs = blocks.reshape(devices // 2, 2, 8, LANES)
    even, odd = pairs[:, 0], pairs[:, 1]
    low = iota((devices // 2, 8, LANES), 1) < CAP
    first = jnp.where(low, even, pltpu.roll(odd, CAP, 1))
    second = jnp.where(low, pltpu.roll(even, CAP, 1), odd)
    return first.reshape(devices * CAP, LANES), second.reshape(devices * CAP, LANES)


def picked_row(row, onehot):
    high, low = split(jnp.broadcast_to(row.astype(F32), (8, row.shape[1])))
    dims = (((1,), (1,)), ((), ()))
    out = lax.dot_general(high, onehot, dims, preferred_element_type=F32)
    out = out + lax.dot_general(low, onehot, dims, preferred_element_type=F32)
    return out[0:1]


def interp_kernel(moves, *refs):
    rank_ref, place_ref, count_ref, fields_ref, part_ref = refs[:5]
    out_refs = refs[5:7]
    tp_ref, push_ref, basis_ref, t_ref, work_ref, count_row_ref, held_ref = refs[7:14]
    place_held, count_held, part_held, arrived = refs[14:]
    tiles = MOVERS // LANES
    pairs = [(place_ref, place_held), (count_ref, count_held), (part_ref, part_held)]
    pairs += [(fields_ref.at[f], held_ref.at[f]) for f in range(3)]
    copies = [pltpu.make_async_copy(*pair, arrived.at[i]) for i, pair in enumerate(pairs)]
    for copy in copies:
        copy.start()
    earlier = (iota((EL, EL), 0) < iota((EL, EL), 1)).astype(BF16)
    copies[0].wait()
    place = place_held[...]
    moving = place // EL != rank_ref[0]
    chosen = moving if moves else jnp.logical_not(moving)
    order = jnp.dot(
        jnp.broadcast_to(chosen.astype(F32), (8, EL)).astype(BF16),
        earlier,
        preferred_element_type=F32,
    )[0:1]
    key = jnp.where(chosen, order.astype(jnp.int32), -1)
    onehot = (iota((MOVERS, EL), 0) == key).astype(BF16)
    slot_row = picked_row(place % EL + 1, onehot)
    copies[1].wait()
    count_row_ref[...] = picked_row(count_held[...], onehot).astype(jnp.int32)
    copies[2].wait()
    records = picked(onehot, part_held[...])
    for t in range(tiles):
        tp_ref[t] = records[t * LANES : (t + 1) * LANES, :].T

    def make_basis(t, carry):
        for d in range(3):
            rows = lagrange_rows(tp_ref[t, d * SLOTS : (d + 1) * SLOTS, :])
            for n in range(NP):
                basis_ref[t, d, n * SLOTS : (n + 1) * SLOTS, :] = rows[n]
        return carry

    lax.fori_loop(0, tiles, make_basis, 0)

    def step(t, f):
        def basis(which, n, p):
            return basis_ref[t, which, pl.ds(n * SLOTS + p, 1), :]

        total = [None] * SLOTS
        for pair in range(NP // 2):
            nodes = [
                [t_ref[f, t, pl.ds(a * 64 + (2 * pair + i) * 8, 8), :] for a in range(NP)]
                for i in range(2)
            ]
            for p in range(SLOTS):
                sums = [None, None]
                for a in range(NP):
                    weight = basis(0, a, p)
                    for i in range(2):
                        term = nodes[i][a] * weight
                        sums[i] = term if sums[i] is None else sums[i] + term
                for i in range(2):
                    term = sums[i] * basis(1, 2 * pair + i, p)
                    total[p] = term if total[p] is None else total[p] + term
        for p in range(SLOTS):
            along_z = basis_ref[t, 2, pl.ds(p, NP, stride=SLOTS), :]
            work_ref[p * NP : (p + 1) * NP, :] = total[p] * along_z
        fluid = work_ref[pl.ds(0, SLOTS, stride=NP), :]
        for c in range(1, NP):
            fluid = fluid + work_ref[pl.ds(c, SLOTS, stride=NP), :]
        where = pl.ds(pl.multiple_of((3 + f) * SLOTS, SLOTS), SLOTS)
        velocity = tp_ref[t, where, :]
        ratio = tp_ref[t, 6 * SLOTS : 7 * SLOTS, :]
        mass = tp_ref[t, 7 * SLOTS : 8 * SLOTS, :]
        count = count_row_ref[:, pl.ds(pl.multiple_of(t * LANES, LANES), LANES)]
        drag = jnp.where(iota((SLOTS, LANES), 0) < count, ratio * (fluid - velocity), 0.0)
        tp_ref[t, where, :] = velocity + drag
        push_ref[t, pl.ds(pl.multiple_of((1 + f) * SLOTS, SLOTS), SLOTS), :] = -(mass * drag)
        return f

    for f in range(3):
        copies[3 + f].wait()
        rows = picked(onehot, held_ref[f])
        for t in range(tiles):
            for j in range(NODES // LANES):
                cols = slice(j * LANES, (j + 1) * LANES)
                t_ref[f, t, cols, :] = rows[t * LANES : (t + 1) * LANES, cols].T
        lax.fori_loop(0, tiles, step, f)

    heads = []
    for t in range(tiles):
        rows = slice(t * LANES, (t + 1) * LANES)
        push_ref[t, 0:SLOTS, :] = jnp.broadcast_to(slot_row[:, rows], (SLOTS, LANES))
        push_ref[t, 4 * SLOTS :, :] = jnp.zeros((LANES - 4 * SLOTS, LANES), F32)
        heads.append(jnp.concatenate([tp_ref[t].T, push_ref[t].T], axis=1))
    head = jnp.concatenate(heads, axis=0)
    if moves:
        send_ref, position_ref = out_refs
        devices = send_ref.shape[0]
        position = pack_positions(place, rank_ref[0])
        position_ref[...] = position
        goes_to = picked_row(position, onehot).astype(jnp.int32)
        scatter = (iota((devices * CAP, MOVERS), 0) == goes_to).astype(BF16)
        rows = picked(scatter, head)
        send_ref[...] = interleave(rows[:, :LANES], rows[:, LANES:])
    else:
        head_ref, slot_ref = out_refs
        head_ref[...] = head
        slot_ref[...] = slot_row.astype(jnp.int32)


def pack_kernel(position_ref, fields_ref, out_ref):
    devices = out_ref.shape[0]
    onehot = (iota((devices * CAP, EL), 0) == position_ref[...]).astype(BF16)
    for f in range(3):
        rows = picked(onehot, fields_ref[f])
        for h in range(2):
            at = COMP * f + 8 * h
            left = 2 * h * LANES
            out_ref[:, at : at + 8, :] = interleave(
                rows[:, left : left + LANES], rows[:, left + LANES : left + 2 * LANES]
            )


def lagrange_rows(coord):
    diffs = [coord - p for p in POINTS]
    left = [None] * NP
    right = [None] * NP
    for i in range(1, NP):
        left[i] = diffs[i - 1] if i == 1 else left[i - 1] * diffs[i - 1]
    for i in range(NP - 2, -1, -1):
        right[i] = diffs[i + 1] if i == NP - 2 else right[i + 1] * diffs[i + 1]
    out = []
    for i in range(NP):
        scale = 1.0
        for m in range(NP):
            if m != i:
                scale /= POINTS[i] - POINTS[m]
        if i == 0:
            term = right[0]
        elif i == NP - 1:
            term = left[i]
        else:
            term = left[i] * right[i]
        out.append(term * float(scale))
    return out


def gaussian_rows(coord):
    return [jnp.exp(-((p - coord) ** 2) * (0.5 / 0.35**2)) for p in POINTS]


def shift_z(x):
    n = x.shape[0] // NP
    x = x.reshape(n, NP, LANES)
    node = iota((n, NP, LANES), 1)
    bz = iota((n, NP, LANES), 2) % BZ
    down = pltpu.roll(pltpu.roll(x, 1, 1), 1, 2)
    up = pltpu.roll(pltpu.roll(x, NP - 1, 1), LANES - 1, 2)
    x = x + jnp.where((node == 0) & (bz > 0), down, 0.0)
    x = x + jnp.where((node == NP - 1) & (bz < BZ - 1), up, 0.0)
    return x.reshape(n * NP, LANES)


def force_kernel(
    head_ref,
    stay_slot_ref,
    recv_ref,
    force_ref,
    xup_ref,
    xdn_ref,
    yup_ref,
    ydn_ref,
    part_ref,
    slot_ref,
    tp_ref,
    push_ref,
    basis_ref,
    work_ref,
):
    tiles = EL // LANES
    particles, extra = deinterleave(recv_ref[...])
    slot_row = extra.T[0:1, :].astype(jnp.int32)
    slot_ref[...] = slot_row
    slots = jnp.concatenate([slot_row, stay_slot_ref[...]], axis=1)
    onehot = (iota((EL, EL + MOVERS), 0) + 1 == slots).astype(BF16)
    arrived = jnp.concatenate([particles, extra], axis=1)
    both = picked(onehot, jnp.concatenate([arrived, head_ref[...]], axis=0))
    record = both[:, :LANES]
    push = both[:, LANES:]
    part_ref[...] = record
    for t in range(tiles):
        rows = slice(t * LANES, (t + 1) * LANES)
        tp_ref[t] = record[rows].T
        push_ref[t] = push[rows].T

    def make_basis(t, carry):
        for d in range(3):
            rows = gaussian_rows(tp_ref[t, d * SLOTS : (d + 1) * SLOTS, :])
            for n in range(NP):
                basis_ref[t, d, n * SLOTS : (n + 1) * SLOTS, :] = rows[n]
        return carry

    lax.fori_loop(0, tiles, make_basis, 0)

    def step(index, carry):
        f = index // tiles
        t = index % tiles

        def basis(which, n, p):
            return basis_ref[t, which, pl.ds(n * SLOTS + p, 1), :]

        for p in range(SLOTS):
            along_z = basis_ref[t, 2, pl.ds(p, NP, stride=SLOTS), :]
            value = push_ref[t, pl.ds((1 + f) * SLOTS + p, 1), :]
            work_ref[p * NP : (p + 1) * NP, :] = (0.5 * value) * along_z
        for pair in range(NP // 2):
            acc = [[None] * NP for _ in range(2)]
            for p in range(SLOTS):
                base = work_ref[p * NP : (p + 1) * NP, :]
                lines = [base * basis(1, 2 * pair + i, p) for i in range(2)]
                for a in range(NP):
                    weight = basis(0, a, p)
                    for i in range(2):
                        term = lines[i] * weight
                        acc[i][a] = term if acc[i][a] is None else acc[i][a] + term
            for i in range(2):
                for a in range(NP):
                    force_ref[f, t, pl.ds(a * 64 + (2 * pair + i) * 8, 8), :] = acc[i][a]
        return carry

    lax.fori_loop(0, 3 * tiles, step, 0)

    lane = iota((NP, LANES), 1)
    bz = iota((64, LANES), 1) % BZ
    for f in range(3):
        xup_ref[f] = force_ref[f, tiles - 1, 448:512, :]
        xdn_ref[f] = force_ref[f, 0, 0:64, :]
        for t in range(tiles - 1):
            summed = force_ref[f, t, 448:512, :] + force_ref[f, t + 1, 0:64, :]
            force_ref[f, t, 448:512, :] = summed
            force_ref[f, t + 1, 0:64, :] = summed
        for a in range(NP):
            first = slice(a * 64, a * 64 + 8)
            last = slice(a * 64 + 56, a * 64 + 64)
            up_line = jnp.zeros((NP, LANES), F32)
            down_line = jnp.zeros((NP, LANES), F32)
            for t in range(tiles):
                upper = force_ref[f, t, last, :]
                lower = force_ref[f, t, first, :]
                take = lane // BZ == t
                up_line = jnp.where(take, pltpu.roll(upper, 16 * t + 16, 1), up_line)
                moved = pltpu.roll(lower, 16 * t, 1) if t else lower
                down_line = jnp.where(take, moved, down_line)
                force_ref[f, t, first, :] = lower + jnp.where(
                    lane >= BZ, pltpu.roll(upper, BZ, 1), 0.0
                )
                force_ref[f, t, last, :] = upper + jnp.where(
                    lane < LANES - BZ, pltpu.roll(lower, LANES - BZ, 1), 0.0
                )
            yup_ref[f, a * 8 : a * 8 + 8, :] = up_line
            ydn_ref[f, a * 8 : a * 8 + 8, :] = down_line
        for t in range(tiles):
            lower = force_ref[f, t, pl.ds(0, 64, stride=NP), :]
            upper = force_ref[f, t, pl.ds(NP - 1, 64, stride=NP), :]
            force_ref[f, t, pl.ds(0, 64, stride=NP), :] = lower + jnp.where(
                bz > 0, pltpu.roll(upper, 1, 1), 0.0
            )
            force_ref[f, t, pl.ds(NP - 1, 64, stride=NP), :] = upper + jnp.where(
                bz < BZ - 1, pltpu.roll(lower, LANES - 1, 1), 0.0
            )


def edge_kernel(below_ref, above_ref, yup_ref, ydn_ref, token_ref, up_ref, down_ref):
    lane = iota((NP, LANES), 1)
    first = lane < BZ
    last = (lane >= 3 * BZ) & (lane < 4 * BZ)
    for f in range(3):
        up_ref[f] = yup_ref[f]
        down_ref[f] = ydn_ref[f]
        up_ref[f, 0:8, :] += jnp.where(first, pltpu.roll(below_ref[f, 56:64, :], BZ, 1), 0.0)
        up_ref[f, 56:64, :] += jnp.where(last, pltpu.roll(above_ref[f, 56:64, :], 4 * BZ, 1), 0.0)
        down_ref[f, 0:8, :] += jnp.where(first, below_ref[f, 0:8, :], 0.0)
        down_ref[f, 56:64, :] += jnp.where(last, pltpu.roll(above_ref[f, 0:8, :], 3 * BZ, 1), 0.0)


def face_delta(face):
    lane = iota((NP, LANES), 1)
    upper = face[56:64]
    lower = face[0:8]
    new_lower = lower + jnp.where(lane >= BZ, pltpu.roll(upper, BZ, 1), 0.0)
    new_upper = upper + jnp.where(lane < LANES - BZ, pltpu.roll(lower, LANES - BZ, 1), 0.0)
    return shift_z(0.5 * jnp.concatenate([new_lower, face[8:56], new_upper], axis=0))


def face_delta(face):
    lane = iota((NP, LANES), 1)
    upper = face[56:64]
    lower = face[0:8]
    new_lower = lower + jnp.where(lane >= BZ, pltpu.roll(upper, BZ, 1), 0.0)
    new_upper = upper + jnp.where(lane < LANES - BZ, pltpu.roll(lower, LANES - BZ, 1), 0.0)
    return shift_z(jnp.concatenate([new_lower, face[8:56], new_upper], axis=0))


def base_kernel(rank_ref, place_ref, fields_ref, force_ref, out_ref, token_ref):
    tiles = EL // LANES
    stay_col = as_column((place_ref[...] // EL == rank_ref[0]).astype(F32)) > 0
    for f in range(3):
        for t in range(tiles):
            rows = slice(t * LANES, (t + 1) * LANES)
            for j in range(NODES // LANES):
                cols = slice(j * LANES, (j + 1) * LANES)
                own = jnp.where(stay_col[rows], fields_ref[f, rows, cols], 0.0)
                out_ref[f, rows, cols] = own + force_ref[f, t, cols, :].T
    token_ref[...] = jnp.zeros((8, LANES), F32)


def place_kernel(
    slot_ref,
    recv_ref,
    base_ref,
    xb_ref,
    xa_ref,
    out_ref,
    ends_ref,
    recv_held,
    held_ref,
    arrived,
    left,
):
    devices = recv_ref.shape[0]
    tiles = EL // LANES
    loads = []
    for f in range(3):
        part = (pl.ds(0, devices), pl.ds(COMP * f, COMP))
        loads.append(
            (
                pltpu.make_async_copy(recv_ref.at[part], recv_held.at[f], arrived.at[f, 0]),
                pltpu.make_async_copy(base_ref.at[f], held_ref.at[f], arrived.at[f, 1]),
            )
        )
        for load in loads[f]:
            load.start()
    onehot = (iota((EL, EL), 0) + 1 == slot_ref[...]).astype(BF16)
    blank = jnp.zeros((64, LANES), F32)
    copies = []
    for f in range(3):
        loads[f][0].wait()
        pieces = []
        for h in range(2):
            pieces += list(deinterleave(recv_held[f, :, 8 * h : 8 * h + 8, :]))
        rows = picked(onehot, jnp.concatenate(pieces, axis=1))
        loads[f][1].wait()
        held_ref[f] += rows
        delta = jnp.concatenate([face_delta(xb_ref[f]), blank], axis=0)
        held_ref[f, 0:LANES, 0:LANES] += delta.T
        delta = jnp.concatenate([blank, face_delta(xa_ref[f])], axis=0)
        held_ref[f, EL - LANES :, NODES - LANES :] += delta.T
        for t in range(tiles):
            inner = pl.ds(t * LANES + BZ, LANES - 2 * BZ)
            copies.append(
                pltpu.make_async_copy(held_ref.at[f, inner], out_ref.at[f, inner], left.at[f, t])
            )
            copies[-1].start()
            ends_ref[f, 0, t * BZ : (t + 1) * BZ, :] = held_ref[f, t * LANES : t * LANES + BZ, :]
            last = (t + 1) * LANES
            ends_ref[f, 1, t * BZ : (t + 1) * BZ, :] = held_ref[f, last - BZ : last, :]
    for copy in copies:
        copy.wait()


def lines_kernel(ends_ref, yb_ref, ya_ref, inner_ref, out_ref, line_ref, held_ref, left):
    tiles = EL // LANES
    lane = iota((64, LANES), 1)
    line_ref[...] = jnp.zeros((NODES, LANES), F32)
    copies = []
    for f in range(3):
        low = shift_z(jnp.where(lane < tiles * BZ, yb_ref[f], 0.0))
        high = shift_z(jnp.where(lane < tiles * BZ, ya_ref[f], 0.0))
        high = pltpu.roll(high, LANES // 2, 1)
        for a in range(NP):
            line_ref[a * 64 : a * 64 + 8, :] = low[a * 8 : a * 8 + 8]
            line_ref[a * 64 + 56 : a * 64 + 64, :] = high[a * 8 : a * 8 + 8]
        for j in range(NODES // LANES):
            cols = slice(j * LANES, (j + 1) * LANES)
            lines = line_ref[cols, :].T
            held_ref[f, 0, :, cols] = ends_ref[f, 0, :, cols] + lines[:64]
            held_ref[f, 1, :, cols] = ends_ref[f, 1, :, cols] + lines[64:]
        for side in range(2):
            for t in range(tiles):
                at = pl.ds(t * LANES + side * (LANES - BZ), BZ)
                copies.append(
                    pltpu.make_async_copy(
                        held_ref.at[f, side, pl.ds(t * BZ, BZ)],
                        out_ref.at[f, at],
                        left.at[f, side, t],
                    )
                )
                copies[-1].start()
    for copy in copies:
        copy.wait()


def passed_along(x, along_ex, along_ey):
    rows, cols = lax.axis_size("ex"), lax.axis_size("ey")
    pairs = []
    for i in range(rows):
        for j in range(cols):
            to_i, to_j = i + along_ex, j + along_ey
            if 0 <= to_i < rows and 0 <= to_j < cols:
                pairs.append((i * cols + j, to_i * cols + to_j))
    return lax.ppermute(x, AXES, pairs)


def whole(n):
    return [pl.BlockSpec(memory_space=pltpu.VMEM)] * n


def params(mib):
    return pltpu.CompilerParams(vmem_limit_bytes=mib * MIB)


def cost(micros):
    return pl.CostEstimate(flops=0, bytes_accessed=int(micros * 3_000_000), transcendentals=0)


def body(fields, particles, counts, new_place):
    devices = lax.axis_size(AXES)
    rank = lax.axis_index(AXES).astype(jnp.int32).reshape(1)
    fields = jnp.transpose(fields, (1, 0, 2))
    place = new_place.reshape(1, EL)
    counts = counts.reshape(1, EL)
    smem = [pl.BlockSpec(memory_space=pltpu.SMEM)]
    anywhere = pl.BlockSpec(memory_space=pl.ANY)
    in_hbm = pl.BlockSpec(memory_space=pltpu.HBM)
    struct = jax.ShapeDtypeStruct
    tiles = EL // LANES
    tile_scratch = pltpu.VMEM((tiles, LANES, LANES), F32)
    basis_scratch = pltpu.VMEM((tiles, 3, LANES, LANES), F32)
    work_scratch = pltpu.VMEM((LANES, LANES), F32)
    half = MOVERS // LANES

    def interp(moves, out_shape, mib, name):
        return pl.pallas_call(
            functools.partial(interp_kernel, moves),
            out_shape=out_shape,
            in_specs=smem + [anywhere] * 4,
            out_specs=tuple(whole(2)),
            scratch_shapes=[
                pltpu.VMEM((half, LANES, LANES), F32),
                pltpu.VMEM((half, LANES, LANES), F32),
                pltpu.VMEM((half, 3, LANES, LANES), F32),
                pltpu.VMEM((3, half, NODES, LANES), F32),
                work_scratch,
                pltpu.VMEM((1, MOVERS), jnp.int32),
                pltpu.VMEM((3, EL, NODES), F32),
                pltpu.VMEM((1, EL), jnp.int32),
                pltpu.VMEM((1, EL), jnp.int32),
                pltpu.VMEM((EL, PARTS), F32),
                pltpu.SemaphoreType.DMA((6,)),
            ],
            compiler_params=params(mib),
            cost_estimate=cost(6),
            name=name,
        )(rank, place, counts, fields, particles)

    send_head, position = interp(
        True, (struct((devices, HEAD, LANES), F32), struct((1, EL), jnp.int32)), 58, "moving"
    )
    head, stay_slots = interp(
        False, (struct((MOVERS, 2 * LANES), F32), struct((1, MOVERS), jnp.int32)), 40, "staying"
    )
    recv_head = lax.all_to_all(send_head, AXES, split_axis=0, concat_axis=0, tiled=True)
    send = pl.pallas_call(
        pack_kernel,
        out_shape=struct((devices, 3 * COMP, LANES), F32),
        in_specs=whole(2),
        out_specs=whole(1)[0],
        compiler_params=params(58),
        cost_estimate=cost(5),
        name="pack",
    )(position, fields)
    recv = lax.all_to_all(send, AXES, split_axis=0, concat_axis=0, tiled=True)
    face = struct((3, 64, LANES), F32)
    force, xup, xdn, yup, ydn, particles_next, slots = pl.pallas_call(
        force_kernel,
        out_shape=(
            struct((3, tiles, NODES, LANES), F32),
            face,
            face,
            face,
            face,
            struct((EL, PARTS), F32),
            struct((1, EL), jnp.int32),
        ),
        in_specs=whole(3),
        out_specs=tuple(whole(7)),
        scratch_shapes=[tile_scratch, tile_scratch, basis_scratch, work_scratch],
        compiler_params=params(40),
        cost_estimate=cost(8),
        name="force",
    )(head, stay_slots, recv_head)
    base, token = pl.pallas_call(
        base_kernel,
        out_shape=(pltpu.HBM((3, EL, NODES), F32), struct((8, LANES), F32)),
        in_specs=smem + whole(3),
        out_specs=tuple(whole(2)),
        compiler_params=params(20),
        cost_estimate=cost(5),
        name="base",
    )(rank, place, fields, force)
    below_x = passed_along(xup, 1, 0)
    above_x = passed_along(xdn, -1, 0)
    up, down = pl.pallas_call(
        edge_kernel,
        out_shape=(face, face),
        in_specs=whole(5),
        out_specs=tuple(whole(2)),
        compiler_params=params(8),
        cost_estimate=cost(1),
        name="edge",
    )(below_x, above_x, yup, ydn, token)
    below_y = passed_along(up, 0, 1)
    above_y = passed_along(down, 0, -1)
    ends = (3, 2, tiles * BZ, NODES)
    inner, ends_out = pl.pallas_call(
        place_kernel,
        out_shape=(struct((3, EL, NODES), F32), struct(ends, F32)),
        in_specs=whole(1) + [in_hbm, in_hbm] + whole(2),
        out_specs=(in_hbm, whole(1)[0]),
        scratch_shapes=[
            pltpu.VMEM((3, devices, COMP, LANES), F32),
            pltpu.VMEM((3, EL, NODES), F32),
            pltpu.SemaphoreType.DMA((3, 2)),
            pltpu.SemaphoreType.DMA((3, tiles)),
        ],
        compiler_params=params(20),
        cost_estimate=cost(3),
        name="place",
    )(slots, recv, pltpu.with_memory_space_constraint(base, pltpu.HBM), below_x, above_x)
    out = pl.pallas_call(
        lines_kernel,
        out_shape=struct((3, EL, NODES), F32),
        in_specs=whole(3) + [anywhere],
        out_specs=anywhere,
        scratch_shapes=[
            pltpu.VMEM((NODES, LANES), F32),
            pltpu.VMEM(ends, F32),
            pltpu.SemaphoreType.DMA((3, 2, tiles)),
        ],
        input_output_aliases={3: 0},
        compiler_params=params(10),
        cost_estimate=cost(1),
        name="lines",
    )(ends_out, below_y, above_y, inner)
    return jnp.transpose(out, (1, 0, 2)), particles_next


def solution(mesh):
    return jax.shard_map(
        body,
        mesh=mesh,
        in_specs=(P(AXES, None, None), P(AXES, None), P(AXES), P(AXES)),
        out_specs=(P(AXES, None, None), P(AXES, None)),
        check_vma=False,
    )
```

time: 110 us -> 89.5 us (0.81)
  the two profiles are of different devices: /device:TPU:27 before, /device:TPU:33 now
where the time goes in v1:
time: 89.5 us; the launch traced here: 89.1 us
  Pallas kernels  35.7 us (40%)
  starting transfers between devices  32.9 us (37%)
  waiting for transfers between devices  19.6 us (22%)
  between operations  0.93 us (1%)
    ppermute x4, starting transfers between devices, passed_along(): return lax.ppermute(x, AXES, pairs)  14.5 us
    ppermute x4, waiting for transfers between devices, passed_along(): return lax.ppermute(x, AXES, pairs)  13.6 us
    pallas_call x2, Pallas kernels, interp(): pl.pallas_call(functools.partial(interp_kernel, moves), out_shape=out_sha...  13.2 us
    all_to_all x1, starting transfers between devices, body(): lax.all_to_all(send_head, AXES, split_axis=0, concat_axis=0, tiled=True)  11 us
    all_to_all x1, starting transfers between devices, body(): recv = lax.all_to_all(send, AXES, split_axis=0, concat_axis=0, tiled=True)  7.4 us
    pallas_call x1, Pallas kernels, body(): pl.pallas_call(force_kernel, out_shape=(struct((3, tiles, NODES, LANES),...  7.38 us
    all_to_all x1, waiting for transfers between devices, body(): lax.all_to_all(send_head, AXES, split_axis=0, concat_axis=0, tiled=True)  6.02 us
    pallas_call x1, Pallas kernels, body(): pl.pallas_call(pack_kernel, out_shape=struct((devices, 3 * COMP, LANES),...  5.42 us
  transfers between devices with their start and end apart: 6, of which 3 were waited for; matrix products, arithmetic and copies ran while one was open for 0% of the time, Pallas kernels for 30%

profile of v1, /device:TPU:33, one launch (start us, length us, event | category | flops | bytes accessed | tf_op | source)
XLA Modules:
  0.0 89.1 jit_solution(15325175598528051927)
XLA Ops:
  0.6 7.6 %moving.1 = (f32[128,8,128]{2,1,0:T(8,128)}, s32[1,512]{1,0:T(1,128)}) custom-call(s32[1]{0:T(128)} %bitcast.refs_0_.rank_ref, s32[1,512]{1,0:T(1,128)} %bitcast.9, s32[1,512]{1,0:T(1,128)} %bitcast.12, f32[3,512,512]{2,1,0:T(8,128)} %bitcast.5, f32[512,128]{1,0:T(8,128)} %refs_4_.3), custom_call_target="tpu_custom_call" | custom-call | bytes 18000000 | tf_op jit(solution)/shard_map/moving/pallas_call | solution.py:543
  8.2 11.0 %all-to-all-start = ((f32[128,8,128]{2,1,0:T(8,128)}), f32[128,8,128]{2,1,0:T(8,128)}, u32[]{:S(2)}, u32[]{:S(2)}) async-start(f32[128,8,128]{2,1,0:T(8,128)} %get-tuple-element.21), calls=%async_computation | async-start | bytes 1048576 | tf_op jit(solution)/shard_map/all_to_all | solution.py:572
  19.2 5.4 %pack.1 = f32[128,48,128]{2,1,0:T(8,128)} custom-call(s32[1,512]{1,0:T(1,128)} %get-tuple-element.23.position_ref, f32[3,512,512]{2,1,0:T(8,128)} %bitcast.6), custom_call_target="tpu_custom_call" | custom-call | bytes 15000000 | tf_op jit(solution)/shard_map/pack/pallas_call | solution.py:573
  24.7 0.0 copy-start
  24.7 0.0 copy-start.1
  24.7 0.0 copy-start.2
  24.7 0.0 copy-start.3
  24.7 6.0 %all-to-all-done.recv_ref = f32[128,8,128]{2,1,0:T(8,128)} async-done(((f32[128,8,128]{2,1,0:T(8,128)}), f32[128,8,128]{2,1,0:T(8,128)}, u32[]{:S(2)}, u32[]{:S(2)}) %all-to-all-start) | async-done | bytes 524320 | tf_op jit(solution)/shard_map/all_to_all | solution.py:572
  30.7 7.4 %all-to-all-start.1 = ((f32[128,48,128]{2,1,0:T(8,128)}), f32[128,48,128]{2,1,0:T(8,128)}, u32[]{:S(2)}, u32[]{:S(2)}) async-start(f32[128,48,128]{2,1,0:T(8,128)} %pack.1), calls=%async_computation.1 | async-start | bytes 6291456 | tf_op jit(solution)/shard_map/all_to_all | solution.py:582
  38.1 0.0 copy-done
  38.1 0.0 copy-done.1
  38.1 0.0 copy-done.2
  38.1 0.0 copy-done.3
  38.1 5.6 %staying.1 = (f32[256,256]{1,0:T(8,128)S(1)}, s32[1,256]{1,0:T(1,128)S(1)}) custom-call(s32[1]{0:T(128)} %bitcast.refs_0_.rank_ref, s32[1,512]{1,0:T(1,128)S(1)} %bitcast.10, s32[1,512]{1,0:T(1,128)S(1)} %bitcast.13, f32[3,512,512]{2,1,0:T(8,128)S(1)} %bitcast.7, f32[512,128]{1,0:T(8,128)S(1)} %copy-done.1), custom_call_target="tpu_custom_call" | custom-call | bytes 18000000 | tf_op jit(solution)/shard_map/staying/pallas_call | solution.py:543
  43.8 7.4 %force.1 = (f32[3,4,512,128]{3,2,1,0:T(8,128)S(1)}, f32[3,64,128]{2,1,0:T(8,128)S(1)}, f32[3,64,128]{2,1,0:T(8,128)S(1)}, f32[3,64,128]{2,1,0:T(8,128)S(1)}, f32...) custom-call(f32[256,256]{1,0:T(8,128)S(1)} %get-tuple-element.19.head_ref, ...), custom_call_target="tpu_custom_call" | custom-call | bytes 24000000 | tf_op jit(solution)/shard_map/force/pallas_call | solution.py:584
  51.1 3.1 %collective-permute-start = (f32[3,64,128]{2,1,0:T(8,128)S(1)}, f32[3,64,128]{2,1,0:T(8,128)S(1)}, u32[]{:S(2)}, u32[]{:S(2)}) collective-permute-start(f32[3,64,128]{2,1,0:T(8,128)S(1)} %get-tuple-element.26), channel_id=1, source_target_pairs={{0,8},{1,9},{2,10},{3,11},{4,12},{5,13},{6,14},{7,15},{8,16},{9,17... | collective-permute-start | bytes 294920 | tf_op jit(solution)/shard_map/ppermute | solution.py:511
  54.3 4.4 %collective-permute-start.1 = (f32[3,64,128]{2,1,0:T(8,128)S(1)}, f32[3,64,128]{2,1,0:T(8,128)S(1)}, u32[]{:S(2)}, u32[]{:S(2)}) collective-permute-start(f32[3,64,128]{2,1,0:T(8,128)S(1)} %get-tuple-element.27), channel_id=1, source_target_pairs={{8,0},{9,1},{10,2},{11,3},{12,4},{13,5},{14,6},{15,7},{16,8},{17,9... | collective-permute-start | bytes 294920 | tf_op jit(solution)/shard_map/ppermute | solution.py:511
  58.7 2.7 %base.1 = (f32[3,512,512]{2,1,0:T(8,128)}, f32[8,128]{1,0:T(8,128)S(1)}) custom-call(s32[1]{0:T(128)} %bitcast.refs_0_.rank_ref, s32[1,512]{1,0:T(1,128)S(1)} %bitcast.11, f32[3,512,512]{2,1,0:T(8,128)S(1)} %bitcast.8, f32[3,4,512,128]{3,2,1,0:T(8,128)S(1)} %get-tuple-element.24.force_ref), custom_call_target="tpu_custom_call" | custom-call | bytes 15000000 | tf_op jit(solution)/shard_map/base/pallas_call | solution.py:602
  61.4 12.9 %collective-permute-done.xb_ref.below_ref = f32[3,64,128]{2,1,0:T(8,128)S(1)} collective-permute-done((f32[3,64,128]{2,1,0:T(8,128)S(1)}, f32[3,64,128]{2,1,0:T(8,128)S(1)}, u32[]{:S(2)}, u32[]{:S(2)}) %collective-permute-start) | collective-permute-done | bytes 98336 | tf_op jit(solution)/shard_map/ppermute | solution.py:511
  74.3 0.7 collective-permute-done.1.xa_ref.above_ref
  75.0 0.1 edge.1
  75.1 5.0 %collective-permute-start.2 = (f32[3,64,128]{2,1,0:T(8,128)S(1)}, f32[3,64,128]{2,1,0:T(8,128)S(1)}, u32[]{:S(2)}, u32[]{:S(2)}) collective-permute-start(f32[3,64,128]{2,1,0:T(8,128)S(1)} %get-tuple-element.32), channel_id=1, source_target_pairs={{0,1},{1,2},{2,3},{3,4},{4,5},{5,6},{6,7},{8,9},{9,10},{10,11},{11... | collective-permute-start | bytes 294920 | tf_op jit(solution)/shard_map/ppermute | solution.py:511
  80.1 1.9 %collective-permute-start.3 = (f32[3,64,128]{2,1,0:T(8,128)S(1)}, f32[3,64,128]{2,1,0:T(8,128)S(1)}, u32[]{:S(2)}, u32[]{:S(2)}) collective-permute-start(f32[3,64,128]{2,1,0:T(8,128)S(1)} %get-tuple-element.33), channel_id=1, source_target_pairs={{1,0},{2,1},{3,2},{4,3},{5,4},{6,5},{7,6},{9,8},{10,9},{11,10},{12... | collective-permute-start | bytes 294920 | tf_op jit(solution)/shard_map/ppermute | solution.py:511
  82.0 0.0 all-to-all-done.1.recv_ref
  82.0 5.4 %place.1 = (f32[3,512,512]{2,1,0:T(8,128)}, f32[3,2,64,512]{3,2,1,0:T(8,128)S(1)}) custom-call(s32[1,512]{1,0:T(1,128)S(1)} %get-tuple-element.22.slot_ref, f32[128,48,128]{2,1,0:T(8,128)} %all-to-all-done.1.recv_ref, f32[3,512,512]{2,1,0:T(8,128)} %get-tuple-element.25.base_ref, f32[3,64,128]{2,1,0:T(8,128)S(1)} %collective-permute-done.xb_ref.below_ref, ...), custom_call_target="tpu_custom_call" | custom-call | bytes 9000000 | tf_op jit(solution)/shard_map/place/pallas_call | solution.py:625
  87.4 0.0 collective-permute-done.2.yb_ref
  87.4 0.0 collective-permute-done.3.ya_ref
  87.4 1.5 %lines.1 = f32[3,512,512]{2,1,0:T(8,128)} custom-call(f32[3,2,64,512]{3,2,1,0:T(8,128)S(1)} %get-tuple-element.28.ends_ref, f32[3,64,128]{2,1,0:T(8,128)S(1)} %collective-permute-done.2.yb_ref, f32[3,64,128]{2,1,0:T(8,128)S(1)} %collective-permute-done.3.ya_ref, f32[3,512,512]{2,1,0:T(8,128)} %get-tuple-element.34.inner_ref), custom_call_target="tpu_custom_call", output_to_operand_aliasing={{}: (3, {})} | custom-call | bytes 3000000 | tf_op jit(solution)/shard_map/lines/pallas_call | solution.py:640
Async XLA Ops:
  8.2 22.5 %all-to-all-start = ((f32[128,8,128]{2,1,0:T(8,128)}), f32[128,8,128]{2,1,0:T(8,128)}, u32[]{:S(2)}, u32[]{:S(2)}) async-start(f32[128,8,128]{2,1,0:T(8,128)} %get-tuple-element.21), calls=%async_computation | async-start | bytes 1048576 | tf_op jit(solution)/shard_map/all_to_all | solution.py:572
  24.7 13.4 %copy-start = (f32[512,3,512]{2,0,1:T(8,128)S(1)}, f32[512,3,512]{2,0,1:T(8,128)}, u32[]{:S(2)}) copy-start(f32[512,3,512]{2,0,1:T(8,128)} %param.4) | copy-start | bytes 9437188
  24.7 13.5 %copy-start.1 = (f32[512,128]{1,0:T(8,128)S(1)}, f32[512,128]{1,0:T(8,128)}, u32[]{:S(2)}) copy-start(f32[512,128]{1,0:T(8,128)} %refs_4_.3) | copy-start | bytes 786436
  24.7 13.5 %copy-start.2 = (s32[512]{0:T(512)S(1)}, s32[512]{0:T(512)}, u32[]{:S(2)}) copy-start(s32[512]{0:T(512)} %param.7) | copy-start | bytes 6148
  24.7 13.5 %copy-start.3 = (s32[512]{0:T(512)S(1)}, s32[512]{0:T(512)}, u32[]{:S(2)}) copy-start(s32[512]{0:T(512)} %param.6) | copy-start | bytes 6148
  30.7 51.3 %all-to-all-start.1 = ((f32[128,48,128]{2,1,0:T(8,128)}), f32[128,48,128]{2,1,0:T(8,128)}, u32[]{:S(2)}, u32[]{:S(2)}) async-start(f32[128,48,128]{2,1,0:T(8,128)} %pack.1), calls=%async_computation.1 | async-start | bytes 6291456 | tf_op jit(solution)/shard_map/all_to_all | solution.py:582
  51.1 23.1 %collective-permute-start = (f32[3,64,128]{2,1,0:T(8,128)S(1)}, f32[3,64,128]{2,1,0:T(8,128)S(1)}, u32[]{:S(2)}, u32[]{:S(2)}) collective-permute-start(f32[3,64,128]{2,1,0:T(8,128)S(1)} %get-tuple-element.26), channel_id=1, source_target_pairs={{0,8},{1,9},{2,10},{3,11},{4,12},{5,13},{6,14},{7,15},{8,16},{9,17... | collective-permute-start | bytes 294920 | tf_op jit(solution)/shard_map/ppermute | solution.py:511
  54.3 20.7 %collective-permute-start.1 = (f32[3,64,128]{2,1,0:T(8,128)S(1)}, f32[3,64,128]{2,1,0:T(8,128)S(1)}, u32[]{:S(2)}, u32[]{:S(2)}) collective-permute-start(f32[3,64,128]{2,1,0:T(8,128)S(1)} %get-tuple-element.27), channel_id=1, source_target_pairs={{8,0},{9,1},{10,2},{11,3},{12,4},{13,5},{14,6},{15,7},{16,8},{17,9... | collective-permute-start | bytes 294920 | tf_op jit(solution)/shard_map/ppermute | solution.py:511
  75.1 12.4 %collective-permute-start.2 = (f32[3,64,128]{2,1,0:T(8,128)S(1)}, f32[3,64,128]{2,1,0:T(8,128)S(1)}, u32[]{:S(2)}, u32[]{:S(2)}) collective-permute-start(f32[3,64,128]{2,1,0:T(8,128)S(1)} %get-tuple-element.32), channel_id=1, source_target_pairs={{0,1},{1,2},{2,3},{3,4},{4,5},{5,6},{6,7},{8,9},{9,10},{10,11},{11... | collective-permute-start | bytes 294920 | tf_op jit(solution)/shard_map/ppermute | solution.py:511
  80.1 7.4 %collective-permute-start.3 = (f32[3,64,128]{2,1,0:T(8,128)S(1)}, f32[3,64,128]{2,1,0:T(8,128)S(1)}, u32[]{:S(2)}, u32[]{:S(2)}) collective-permute-start(f32[3,64,128]{2,1,0:T(8,128)S(1)} %get-tuple-element.33), channel_id=1, source_target_pairs={{1,0},{2,1},{3,2},{4,3},{5,4},{6,5},{7,6},{9,8},{10,9},{11,10},{12... | collective-permute-start | bytes 294920 | tf_op jit(solution)/shard_map/ppermute | solution.py:511

commit v2 on v1

--- a/solution.py
+++ b/solution.py
@@ -20,7 +20,7 @@
 MOVERS = PEERS * CAP
 LANES = 128
 PARTS = 8 * SLOTS
-HEAD = 8
+HEAD = 6
 COMP = 16
 AXES = ("ex", "ey")
 POINTS = [
@@ -195,13 +195,21 @@
     head = jnp.concatenate(heads, axis=0)
     if moves:
         send_ref, position_ref = out_refs
-        devices = send_ref.shape[0]
+        devices = send_ref.shape[0] // HEAD
         position = pack_positions(place, rank_ref[0])
         position_ref[...] = position
         goes_to = picked_row(position, onehot).astype(jnp.int32)
+        goes_to = goes_to % CAP * devices + goes_to // CAP
         scatter = (iota((devices * CAP, MOVERS), 0) == goes_to).astype(BF16)
         rows = picked(scatter, head)
-        send_ref[...] = interleave(rows[:, :LANES], rows[:, LANES:])
+        lane = iota((devices, LANES), 1)
+        for q in range(CAP):
+            mine = slice(q * devices, (q + 1) * devices)
+            send_ref[pl.ds(q, devices, stride=HEAD), :] = rows[mine, :LANES]
+            if q % 2:
+                both = jnp.where(lane < LANES // 2, before, pltpu.roll(rows[mine, LANES:], LANES // 2, 1))
+                send_ref[pl.ds(CAP + q // 2, devices, stride=HEAD), :] = both
+            before = rows[mine, LANES:]
     else:
         head_ref, slot_ref = out_refs
         head_ref[...] = head
@@ -278,9 +286,22 @@
     work_ref,
 ):
     tiles = EL // LANES
-    particles, extra = deinterleave(recv_ref[...])
+    devices = recv_ref.shape[0] // HEAD
+    particles, extra = [], []
+    for q in range(CAP):
+        particles.append(recv_ref[pl.ds(q, devices, stride=HEAD), :])
+        both = recv_ref[pl.ds(CAP + q // 2, devices, stride=HEAD), :]
+        extra.append(pltpu.roll(both, LANES // 2, 1) if q % 2 else both)
+    particles = jnp.concatenate(particles, axis=0)
+    extra = jnp.concatenate(extra, axis=0)
     slot_row = extra.T[0:1, :].astype(jnp.int32)
-    slot_ref[...] = slot_row
+    at = iota((devices * CAP, devices * CAP), 0)
+    turned = at // devices + at % devices * CAP == iota((devices * CAP, devices * CAP), 1)
+    high, low = split(jnp.broadcast_to(slot_row.astype(F32), (8, devices * CAP)))
+    order = turned.astype(BF16)
+    row = jnp.dot(high, order, preferred_element_type=F32)
+    row = row + jnp.dot(low, order, preferred_element_type=F32)
+    slot_ref[...] = row[0:1].astype(jnp.int32)
     slots = jnp.concatenate([slot_row, stay_slot_ref[...]], axis=1)
     onehot = (iota((EL, EL + MOVERS), 0) + 1 == slots).astype(BF16)
     arrived = jnp.concatenate([particles, extra], axis=1)
@@ -564,12 +585,13 @@
         )(rank, place, counts, fields, particles)
 
     send_head, position = interp(
-        True, (struct((devices, HEAD, LANES), F32), struct((1, EL), jnp.int32)), 58, "moving"
+        True, (struct((devices * HEAD, LANES), F32), struct((1, EL), jnp.int32)), 58, "moving"
     )
     head, stay_slots = interp(
         False, (struct((MOVERS, 2 * LANES), F32), struct((1, MOVERS), jnp.int32)), 40, "staying"
     )
-    recv_head = lax.all_to_all(send_head, AXES, split_axis=0, concat_axis=0, tiled=True)
+    recv_head = lax.all_to_all(send_head.reshape(-1), AXES, split_axis=0, concat_axis=0, tiled=True)
+    recv_head = recv_head.reshape(devices * HEAD, LANES)
     send = pl.pallas_call(
         pack_kernel,
         out_shape=struct((devices, 3 * COMP, LANES), F32),

time: 89.5 us -> 88 us (0.983)
  waiting for transfers between devices: 19.6 us -> 18.3 us
  local copies, waits for them, and re-layouts: 0.01 us -> 0.96 us
    all_to_all x1, waiting for transfers between devices: 6.02 us -> 5 us  [body(): lax.all_to_all(send_head.reshape(-1), AXES, split_axis=0, concat_axis=0,...]
    unnamed x8, local copies, waits for them, and re-layouts: 0.01 us -> 0.96 us
where the time goes in v2:
time: 88 us; the launch traced here: 87.6 us
  Pallas kernels  35.1 us (40%)
  starting transfers between devices  32.4 us (37%)
  waiting for transfers between devices  18.3 us (21%)
  local copies, waits for them, and re-layouts  0.96 us (1%)
  between operations  0.93 us (1%)
    ppermute x4, starting transfers between devices, passed_along(): return lax.ppermute(x, AXES, pairs)  14.5 us
    ppermute x4, waiting for transfers between devices, passed_along(): return lax.ppermute(x, AXES, pairs)  13.3 us
    pallas_call x2, Pallas kernels, interp(): pl.pallas_call(functools.partial(interp_kernel, moves), out_shape=out_sha...  13.2 us
    all_to_all x1, starting transfers between devices, body(): lax.all_to_all(send_head.reshape(-1), AXES, split_axis=0, concat_axis=0,...  10.5 us
    all_to_all x1, starting transfers between devices, body(): recv = lax.all_to_all(send, AXES, split_axis=0, concat_axis=0, tiled=True)  7.38 us
    pallas_call x1, Pallas kernels, body(): pl.pallas_call(force_kernel, out_shape=(struct((3, tiles, NODES, LANES),...  6.74 us
    pallas_call x1, Pallas kernels, body(): pl.pallas_call(pack_kernel, out_shape=struct((devices, 3 * COMP, LANES),...  5.42 us
    pallas_call x1, Pallas kernels, body(): pl.pallas_call(place_kernel, out_shape=(struct((3, EL, NODES), F32), stru...  5.41 us
  transfers between devices with their start and end apart: 6, of which 3 were waited for; matrix products, arithmetic and copies ran while one was open for 0% of the time, Pallas kernels for 30%

profile of v2, /device:TPU:33, one launch (start us, length us, event | category | flops | bytes accessed | tf_op | source)
XLA Modules:
  0.0 87.6 jit_solution(9356202083000765232)
XLA Ops:
  0.6 7.6 %moving.1 = (f32[768,128]{1,0:T(8,128)}, s32[1,512]{1,0:T(1,128)}) custom-call(s32[1]{0:T(128)} %bitcast.refs_0_.rank_ref, s32[1,512]{1,0:T(1,128)} %bitcast.12, s32[1,512]{1,0:T(1,128)} %bitcast.15, f32[3,512,512]{2,1,0:T(8,128)} %bitcast.7, f32[512,128]{1,0:T(8,128)} %refs_4_.3), custom_call_target="tpu_custom_call" | custom-call | bytes 18000000 | tf_op jit(solution)/shard_map/moving/pallas_call | solution.py:564
  8.3 10.5 %all-to-all-start = ((f32[128,768,1]{1,2,0:T(1,128)}), f32[128,768,1]{1,2,0:T(1,128)S(1)}, u32[]{:S(2)}, u32[]{:S(2)}) async-start(f32[128,768,1]{1,2,0:T(1,128)} %bitcast.18), calls=%async_computation | async-start | bytes 786432 | tf_op jit(solution)/shard_map/all_to_all | solution.py:593
  18.8 5.4 %pack.1 = f32[128,48,128]{2,1,0:T(8,128)} custom-call(s32[1,512]{1,0:T(1,128)} %get-tuple-element.23.position_ref, f32[3,512,512]{2,1,0:T(8,128)} %bitcast.8), custom_call_target="tpu_custom_call" | custom-call | bytes 15000000 | tf_op jit(solution)/shard_map/pack/pallas_call | solution.py:595
  24.2 0.0 copy-start
  24.2 0.0 copy-start.2
  24.2 0.0 copy-start.3
  24.2 5.0 %all-to-all-done = f32[128,768,1]{1,2,0:T(1,128)S(1)} async-done(((f32[128,768,1]{1,2,0:T(1,128)}), f32[128,768,1]{1,2,0:T(1,128)S(1)}, u32[]{:S(2)}, u32[]{:S(2)}) %all-to-all-start) | async-done | bytes 393248 | tf_op jit(solution)/shard_map/all_to_all | solution.py:593
  29.2 7.4 %all-to-all-start.1 = ((f32[128,48,128]{2,1,0:T(8,128)}), f32[128,48,128]{2,1,0:T(8,128)}, u32[]{:S(2)}, u32[]{:S(2)}) async-start(f32[128,48,128]{2,1,0:T(8,128)} %pack.1), calls=%async_computation.1 | async-start | bytes 6291456 | tf_op jit(solution)/shard_map/all_to_all | solution.py:604
  36.6 0.0 copy-done
  36.6 0.0 copy-done.2
  36.7 0.0 copy-done.3
  36.7 0.0 copy-start.1
  36.7 0.9 %copy-done.1 = f32[512,128]{1,0:T(8,128)S(1)} copy-done((f32[512,128]{1,0:T(8,128)S(1)}, f32[512,128]{1,0:T(8,128)}, u32[]{:S(2)}) %copy-start.1) | copy-done | bytes 262168
  37.6 5.6 %staying.1 = (f32[256,256]{1,0:T(8,128)S(1)}, s32[1,256]{1,0:T(1,128)S(1)}) custom-call(s32[1]{0:T(128)} %bitcast.refs_0_.rank_ref, s32[1,512]{1,0:T(1,128)S(1)} %bitcast.13, s32[1,512]{1,0:T(1,128)S(1)} %bitcast.16, f32[3,512,512]{2,1,0:T(8,128)S(1)} %bitcast.9, f32[512,128]{1,0:T(8,128)S(1)} %copy-done.1), custom_call_target="tpu_custom_call" | custom-call | bytes 18000000 | tf_op jit(solution)/shard_map/staying/pallas_call | solution.py:564
  43.2 6.7 %force.1 = (f32[3,4,512,128]{3,2,1,0:T(8,128)S(1)}, f32[3,64,128]{2,1,0:T(8,128)S(1)}, f32[3,64,128]{2,1,0:T(8,128)S(1)}, f32[3,64,128]{2,1,0:T(8,128)S(1)}, f32...) custom-call(f32[256,256]{1,0:T(8,128)S(1)} %get-tuple-element.19.head_ref, ...), custom_call_target="tpu_custom_call" | custom-call | bytes 24000000 | tf_op jit(solution)/shard_map/force/pallas_call | solution.py:606
  50.0 3.1 %collective-permute-start = (f32[3,64,128]{2,1,0:T(8,128)S(1)}, f32[3,64,128]{2,1,0:T(8,128)S(1)}, u32[]{:S(2)}, u32[]{:S(2)}) collective-permute-start(f32[3,64,128]{2,1,0:T(8,128)S(1)} %get-tuple-element.26), channel_id=1, source_target_pairs={{0,8},{1,9},{2,10},{3,11},{4,12},{5,13},{6,14},{7,15},{8,16},{9,17... | collective-permute-start | bytes 294920 | tf_op jit(solution)/shard_map/ppermute | solution.py:532
  53.1 4.4 %collective-permute-start.1 = (f32[3,64,128]{2,1,0:T(8,128)S(1)}, f32[3,64,128]{2,1,0:T(8,128)S(1)}, u32[]{:S(2)}, u32[]{:S(2)}) collective-permute-start(f32[3,64,128]{2,1,0:T(8,128)S(1)} %get-tuple-element.27), channel_id=1, source_target_pairs={{8,0},{9,1},{10,2},{11,3},{12,4},{13,5},{14,6},{15,7},{16,8},{17,9... | collective-permute-start | bytes 294920 | tf_op jit(solution)/shard_map/ppermute | solution.py:532
  57.5 2.7 %base.1 = (f32[3,512,512]{2,1,0:T(8,128)}, f32[8,128]{1,0:T(8,128)S(1)}) custom-call(s32[1]{0:T(128)} %bitcast.refs_0_.rank_ref, s32[1,512]{1,0:T(1,128)S(1)} %bitcast.14, f32[3,512,512]{2,1,0:T(8,128)S(1)} %bitcast.10, f32[3,4,512,128]{3,2,1,0:T(8,128)S(1)} %get-tuple-element.24.force_ref), custom_call_target="tpu_custom_call" | custom-call | bytes 15000000 | tf_op jit(solution)/shard_map/base/pallas_call | solution.py:624
  60.2 12.6 %collective-permute-done.xb_ref.below_ref = f32[3,64,128]{2,1,0:T(8,128)S(1)} collective-permute-done((f32[3,64,128]{2,1,0:T(8,128)S(1)}, f32[3,64,128]{2,1,0:T(8,128)S(1)}, u32[]{:S(2)}, u32[]{:S(2)}) %collective-permute-start) | collective-permute-done | bytes 98336 | tf_op jit(solution)/shard_map/ppermute | solution.py:532
  72.8 0.7 collective-permute-done.1.xa_ref.above_ref
  73.5 0.1 edge.1
  73.6 5.0 %collective-permute-start.2 = (f32[3,64,128]{2,1,0:T(8,128)S(1)}, f32[3,64,128]{2,1,0:T(8,128)S(1)}, u32[]{:S(2)}, u32[]{:S(2)}) collective-permute-start(f32[3,64,128]{2,1,0:T(8,128)S(1)} %get-tuple-element.32), channel_id=1, source_target_pairs={{0,1},{1,2},{2,3},{3,4},{4,5},{5,6},{6,7},{8,9},{9,10},{10,11},{11... | collective-permute-start | bytes 294920 | tf_op jit(solution)/shard_map/ppermute | solution.py:532
  78.6 1.9 %collective-permute-start.3 = (f32[3,64,128]{2,1,0:T(8,128)S(1)}, f32[3,64,128]{2,1,0:T(8,128)S(1)}, u32[]{:S(2)}, u32[]{:S(2)}) collective-permute-start(f32[3,64,128]{2,1,0:T(8,128)S(1)} %get-tuple-element.33), channel_id=1, source_target_pairs={{1,0},{2,1},{3,2},{4,3},{5,4},{6,5},{7,6},{9,8},{10,9},{11,10},{12... | collective-permute-start | bytes 294920 | tf_op jit(solution)/shard_map/ppermute | solution.py:532
  80.5 0.0 all-to-all-done.1.recv_ref
  80.5 5.4 %place.1 = (f32[3,512,512]{2,1,0:T(8,128)}, f32[3,2,64,512]{3,2,1,0:T(8,128)S(1)}) custom-call(s32[1,512]{1,0:T(1,128)S(1)} %get-tuple-element.22.slot_ref, f32[128,48,128]{2,1,0:T(8,128)} %all-to-all-done.1.recv_ref, f32[3,512,512]{2,1,0:T(8,128)} %get-tuple-element.25.base_ref, f32[3,64,128]{2,1,0:T(8,128)S(1)} %collective-permute-done.xb_ref.below_ref, ...), custom_call_target="tpu_custom_call" | custom-call | bytes 9000000 | tf_op jit(solution)/shard_map/place/pallas_call | solution.py:647
  85.9 0.0 collective-permute-done.2.yb_ref
  86.0 0.0 collective-permute-done.3.ya_ref
  86.0 1.5 %lines.1 = f32[3,512,512]{2,1,0:T(8,128)} custom-call(f32[3,2,64,512]{3,2,1,0:T(8,128)S(1)} %get-tuple-element.28.ends_ref, f32[3,64,128]{2,1,0:T(8,128)S(1)} %collective-permute-done.2.yb_ref, f32[3,64,128]{2,1,0:T(8,128)S(1)} %collective-permute-done.3.ya_ref, f32[3,512,512]{2,1,0:T(8,128)} %get-tuple-element.34.inner_ref), custom_call_target="tpu_custom_call", output_to_operand_aliasing={{}: (3, {})} | custom-call | bytes 3000000 | tf_op jit(solution)/shard_map/lines/pallas_call | solution.py:662
Async XLA Ops:
  8.3 21.0 %all-to-all-start = ((f32[128,768,1]{1,2,0:T(1,128)}), f32[128,768,1]{1,2,0:T(1,128)S(1)}, u32[]{:S(2)}, u32[]{:S(2)}) async-start(f32[128,768,1]{1,2,0:T(1,128)} %bitcast.18), calls=%async_computation | async-start | bytes 786432 | tf_op jit(solution)/shard_map/all_to_all | solution.py:593
  24.2 12.4 %copy-start = (f32[512,3,512]{2,0,1:T(8,128)S(1)}, f32[512,3,512]{2,0,1:T(8,128)}, u32[]{:S(2)}) copy-start(f32[512,3,512]{2,0,1:T(8,128)} %param.4) | copy-start | bytes 9437188
  24.2 12.4 %copy-start.2 = (s32[512]{0:T(512)S(1)}, s32[512]{0:T(512)}, u32[]{:S(2)}) copy-start(s32[512]{0:T(512)} %param.7) | copy-start | bytes 6148
  24.2 12.4 %copy-start.3 = (s32[512]{0:T(512)S(1)}, s32[512]{0:T(512)}, u32[]{:S(2)}) copy-start(s32[512]{0:T(512)} %param.6) | copy-start | bytes 6148
  29.2 51.3 %all-to-all-start.1 = ((f32[128,48,128]{2,1,0:T(8,128)}), f32[128,48,128]{2,1,0:T(8,128)}, u32[]{:S(2)}, u32[]{:S(2)}) async-start(f32[128,48,128]{2,1,0:T(8,128)} %pack.1), calls=%async_computation.1 | async-start | bytes 6291456 | tf_op jit(solution)/shard_map/all_to_all | solution.py:604
  36.7 1.0 %copy-start.1 = (f32[512,128]{1,0:T(8,128)S(1)}, f32[512,128]{1,0:T(8,128)}, u32[]{:S(2)}) copy-start(f32[512,128]{1,0:T(8,128)} %refs_4_.3) | copy-start | bytes 786436
  50.0 22.8 %collective-permute-start = (f32[3,64,128]{2,1,0:T(8,128)S(1)}, f32[3,64,128]{2,1,0:T(8,128)S(1)}, u32[]{:S(2)}, u32[]{:S(2)}) collective-permute-start(f32[3,64,128]{2,1,0:T(8,128)S(1)} %get-tuple-element.26), channel_id=1, source_target_pairs={{0,8},{1,9},{2,10},{3,11},{4,12},{5,13},{6,14},{7,15},{8,16},{9,17... | collective-permute-start | bytes 294920 | tf_op jit(solution)/shard_map/ppermute | solution.py:532
  53.1 20.4 %collective-permute-start.1 = (f32[3,64,128]{2,1,0:T(8,128)S(1)}, f32[3,64,128]{2,1,0:T(8,128)S(1)}, u32[]{:S(2)}, u32[]{:S(2)}) collective-permute-start(f32[3,64,128]{2,1,0:T(8,128)S(1)} %get-tuple-element.27), channel_id=1, source_target_pairs={{8,0},{9,1},{10,2},{11,3},{12,4},{13,5},{14,6},{15,7},{16,8},{17,9... | collective-permute-start | bytes 294920 | tf_op jit(solution)/shard_map/ppermute | solution.py:532
  73.6 12.4 %collective-permute-start.2 = (f32[3,64,128]{2,1,0:T(8,128)S(1)}, f32[3,64,128]{2,1,0:T(8,128)S(1)}, u32[]{:S(2)}, u32[]{:S(2)}) collective-permute-start(f32[3,64,128]{2,1,0:T(8,128)S(1)} %get-tuple-element.32), channel_id=1, source_target_pairs={{0,1},{1,2},{2,3},{3,4},{4,5},{5,6},{6,7},{8,9},{9,10},{10,11},{11... | collective-permute-start | bytes 294920 | tf_op jit(solution)/shard_map/ppermute | solution.py:532
  78.6 7.4 %collective-permute-start.3 = (f32[3,64,128]{2,1,0:T(8,128)S(1)}, f32[3,64,128]{2,1,0:T(8,128)S(1)}, u32[]{:S(2)}, u32[]{:S(2)}) collective-permute-start(f32[3,64,128]{2,1,0:T(8,128)S(1)} %get-tuple-element.33), channel_id=1, source_target_pairs={{1,0},{2,1},{3,2},{4,3},{5,4},{6,5},{7,6},{9,8},{10,9},{11,10},{12... | collective-permute-start | bytes 294920 | tf_op jit(solution)/shard_map/ppermute | solution.py:532

commit v3 on v2

--- a/solution.py
+++ b/solution.py
@@ -278,6 +278,8 @@
     xdn_ref,
     yup_ref,
     ydn_ref,
+    left_ref,
+    right_ref,
     part_ref,
     slot_ref,
     tp_ref,
@@ -356,6 +358,8 @@
     for f in range(3):
         xup_ref[f] = force_ref[f, tiles - 1, 448:512, :]
         xdn_ref[f] = force_ref[f, 0, 0:64, :]
+        left_ref[f] = pltpu.roll(force_ref[f, tiles - 1, 504:512, :], BZ, 1)
+        right_ref[f] = pltpu.roll(force_ref[f, 0, 56:64, :], BZ, 1)
         for t in range(tiles - 1):
             summed = force_ref[f, t, 448:512, :] + force_ref[f, t + 1, 0:64, :]
             force_ref[f, t, 448:512, :] = summed
@@ -391,17 +395,17 @@
             )
 
 
-def edge_kernel(below_ref, above_ref, yup_ref, ydn_ref, token_ref, up_ref, down_ref):
+def edge_kernel(below_ref, above_ref, ydn_ref, yb_ref, cb_ref, ca_ref, token_ref, down_ref, low_ref):
     lane = iota((NP, LANES), 1)
     first = lane < BZ
     last = (lane >= 3 * BZ) & (lane < 4 * BZ)
     for f in range(3):
-        up_ref[f] = yup_ref[f]
         down_ref[f] = ydn_ref[f]
-        up_ref[f, 0:8, :] += jnp.where(first, pltpu.roll(below_ref[f, 56:64, :], BZ, 1), 0.0)
-        up_ref[f, 56:64, :] += jnp.where(last, pltpu.roll(above_ref[f, 56:64, :], 4 * BZ, 1), 0.0)
         down_ref[f, 0:8, :] += jnp.where(first, below_ref[f, 0:8, :], 0.0)
         down_ref[f, 56:64, :] += jnp.where(last, pltpu.roll(above_ref[f, 0:8, :], 3 * BZ, 1), 0.0)
+        low_ref[f] = yb_ref[f]
+        low_ref[f, 0:8, :] += jnp.where(first, cb_ref[f], 0.0)
+        low_ref[f, 56:64, :] += jnp.where(last, pltpu.roll(ca_ref[f], 3 * BZ, 1), 0.0)
 
 
 def face_delta(face):
@@ -435,16 +439,28 @@
     token_ref[...] = jnp.zeros((8, LANES), F32)
 
 
+def lines_of(values, node, line_ref):
+    values = shift_z(jnp.where(iota((64, LANES), 1) < BX * BZ, values, 0.0))
+    for a in range(NP):
+        at = a * 64 + node * 8
+        line_ref[at : at + 8, :] = values[a * 8 : a * 8 + 8]
+    cols = [line_ref[j * LANES : (j + 1) * LANES, :].T for j in range(NODES // LANES)]
+    return jnp.concatenate(cols, axis=1)[: BX * BZ]
+
+
 def place_kernel(
     slot_ref,
     recv_ref,
     base_ref,
     xb_ref,
     xa_ref,
+    low_ref,
     out_ref,
     ends_ref,
     recv_held,
     held_ref,
+    line_ref,
+    lows_ref,
     arrived,
     left,
 ):
@@ -463,6 +479,9 @@
             load.start()
     onehot = (iota((EL, EL), 0) + 1 == slot_ref[...]).astype(BF16)
     blank = jnp.zeros((64, LANES), F32)
+    line_ref[...] = jnp.zeros((NODES, LANES), F32)
+    for f in range(3):
+        lows_ref[f] = lines_of(low_ref[f], 0, line_ref)
     copies = []
     for f in range(3):
         loads[f][0].wait()
@@ -477,46 +496,32 @@
         delta = jnp.concatenate([blank, face_delta(xa_ref[f])], axis=0)
         held_ref[f, EL - LANES :, NODES - LANES :] += delta.T
         for t in range(tiles):
-            inner = pl.ds(t * LANES + BZ, LANES - 2 * BZ)
+            mine = slice(t * BZ, (t + 1) * BZ)
+            held_ref[f, t * LANES : t * LANES + BZ, :] += lows_ref[f, mine, :]
+            inner = pl.ds(t * LANES, LANES - BZ)
             copies.append(
                 pltpu.make_async_copy(held_ref.at[f, inner], out_ref.at[f, inner], left.at[f, t])
             )
             copies[-1].start()
-            ends_ref[f, 0, t * BZ : (t + 1) * BZ, :] = held_ref[f, t * LANES : t * LANES + BZ, :]
             last = (t + 1) * LANES
-            ends_ref[f, 1, t * BZ : (t + 1) * BZ, :] = held_ref[f, last - BZ : last, :]
+            ends_ref[f, mine, :] = held_ref[f, last - BZ : last, :]
     for copy in copies:
         copy.wait()
 
 
-def lines_kernel(ends_ref, yb_ref, ya_ref, inner_ref, out_ref, line_ref, held_ref, left):
+def lines_kernel(ends_ref, ya_ref, inner_ref, out_ref, line_ref, held_ref, left):
     tiles = EL // LANES
-    lane = iota((64, LANES), 1)
     line_ref[...] = jnp.zeros((NODES, LANES), F32)
     copies = []
     for f in range(3):
-        low = shift_z(jnp.where(lane < tiles * BZ, yb_ref[f], 0.0))
-        high = shift_z(jnp.where(lane < tiles * BZ, ya_ref[f], 0.0))
-        high = pltpu.roll(high, LANES // 2, 1)
-        for a in range(NP):
-            line_ref[a * 64 : a * 64 + 8, :] = low[a * 8 : a * 8 + 8]
-            line_ref[a * 64 + 56 : a * 64 + 64, :] = high[a * 8 : a * 8 + 8]
-        for j in range(NODES // LANES):
-            cols = slice(j * LANES, (j + 1) * LANES)
-            lines = line_ref[cols, :].T
-            held_ref[f, 0, :, cols] = ends_ref[f, 0, :, cols] + lines[:64]
-            held_ref[f, 1, :, cols] = ends_ref[f, 1, :, cols] + lines[64:]
-        for side in range(2):
-            for t in range(tiles):
-                at = pl.ds(t * LANES + side * (LANES - BZ), BZ)
-                copies.append(
-                    pltpu.make_async_copy(
-                        held_ref.at[f, side, pl.ds(t * BZ, BZ)],
-                        out_ref.at[f, at],
-                        left.at[f, side, t],
-                    )
-                )
-                copies[-1].start()
+        held_ref[f] = ends_ref[f] + lines_of(ya_ref[f], NP - 1, line_ref)
+        for t in range(tiles):
+            at = pl.ds((t + 1) * LANES - BZ, BZ)
+            mine = pl.ds(t * BZ, BZ)
+            copies.append(
+                pltpu.make_async_copy(held_ref.at[f, mine], out_ref.at[f, at], left.at[f, t])
+            )
+            copies[-1].start()
     for copy in copies:
         copy.wait()
 
@@ -603,7 +608,8 @@
     )(position, fields)
     recv = lax.all_to_all(send, AXES, split_axis=0, concat_axis=0, tiled=True)
     face = struct((3, 64, LANES), F32)
-    force, xup, xdn, yup, ydn, particles_next, slots = pl.pallas_call(
+    corner = struct((3, NP, LANES), F32)
+    force, xup, xdn, yup, ydn, left, right, particles_next, slots = pl.pallas_call(
         force_kernel,
         out_shape=(
             struct((3, tiles, NODES, LANES), F32),
@@ -611,11 +617,13 @@
             face,
             face,
             face,
+            corner,
+            corner,
             struct((EL, PARTS), F32),
             struct((1, EL), jnp.int32),
         ),
         in_specs=whole(3),
-        out_specs=tuple(whole(7)),
+        out_specs=tuple(whole(9)),
         scratch_shapes=[tile_scratch, tile_scratch, basis_scratch, work_scratch],
         compiler_params=params(40),
         cost_estimate=cost(8),
@@ -632,48 +640,59 @@
     )(rank, place, fields, force)
     below_x = passed_along(xup, 1, 0)
     above_x = passed_along(xdn, -1, 0)
-    up, down = pl.pallas_call(
+    below_y = passed_along(yup, 0, 1)
+    corner_below = passed_along(left, 1, 1)
+    corner_above = passed_along(right, -1, 1)
+    down, low = pl.pallas_call(
         edge_kernel,
         out_shape=(face, face),
-        in_specs=whole(5),
+        in_specs=whole(7),
         out_specs=tuple(whole(2)),
         compiler_params=params(8),
         cost_estimate=cost(1),
         name="edge",
-    )(below_x, above_x, yup, ydn, token)
-    below_y = passed_along(up, 0, 1)
+    )(below_x, above_x, ydn, below_y, corner_below, corner_above, token)
     above_y = passed_along(down, 0, -1)
-    ends = (3, 2, tiles * BZ, NODES)
+    ends = (3, tiles * BZ, NODES)
     inner, ends_out = pl.pallas_call(
         place_kernel,
         out_shape=(struct((3, EL, NODES), F32), struct(ends, F32)),
-        in_specs=whole(1) + [in_hbm, in_hbm] + whole(2),
+        in_specs=whole(1) + [in_hbm, in_hbm] + whole(3),
         out_specs=(in_hbm, whole(1)[0]),
         scratch_shapes=[
             pltpu.VMEM((3, devices, COMP, LANES), F32),
             pltpu.VMEM((3, EL, NODES), F32),
+            pltpu.VMEM((NODES, LANES), F32),
+            pltpu.VMEM(ends, F32),
             pltpu.SemaphoreType.DMA((3, 2)),
             pltpu.SemaphoreType.DMA((3, tiles)),
         ],
         compiler_params=params(20),
         cost_estimate=cost(3),
         name="place",
-    )(slots, recv, pltpu.with_memory_space_constraint(base, pltpu.HBM), below_x, above_x)
+    )(
+        slots,
+        recv,
+        pltpu.with_memory_space_constraint(base, pltpu.HBM),
+        below_x,
+        above_x,
+        low,
+    )
     out = pl.pallas_call(
         lines_kernel,
         out_shape=struct((3, EL, NODES), F32),
-        in_specs=whole(3) + [anywhere],
+        in_specs=whole(2) + [anywhere],
         out_specs=anywhere,
         scratch_shapes=[
             pltpu.VMEM((NODES, LANES), F32),
             pltpu.VMEM(ends, F32),
-            pltpu.SemaphoreType.DMA((3, 2, tiles)),
+            pltpu.SemaphoreType.DMA((3, tiles)),
         ],
-        input_output_aliases={3: 0},
+        input_output_aliases={2: 0},
         compiler_params=params(10),
         cost_estimate=cost(1),
         name="lines",
-    )(ends_out, below_y, above_y, inner)
+    )(ends_out, above_y, inner)
     return jnp.transpose(out, (1, 0, 2)), particles_next
 
 

time: 88 us -> 86.2 us (0.980)
  the two profiles are of different devices: /device:TPU:33 before, /device:TPU:0 now
where the time goes in v3:
time: 86.2 us; the launch traced here: 85.8 us
  Pallas kernels  34.8 us (40%)
  starting transfers between devices  30.7 us (36%)
  waiting for transfers between devices  18.5 us (21%)
  local copies, waits for them, and re-layouts  0.96 us (1%)
  between operations  0.93 us (1%)
    ppermute x6, starting transfers between devices, passed_along(): return lax.ppermute(x, AXES, pairs)  13.8 us
    pallas_call x2, Pallas kernels, interp(): pl.pallas_call(functools.partial(interp_kernel, moves), out_shape=out_sha...  13.2 us
    all_to_all x1, starting transfers between devices, body(): lax.all_to_all(send_head.reshape(-1), AXES, split_axis=0, concat_axis=0,...  11.2 us
    ppermute x6, waiting for transfers between devices, passed_along(): return lax.ppermute(x, AXES, pairs)  8 us
    pallas_call x1, Pallas kernels, body(): pl.pallas_call(force_kernel, out_shape=(struct((3, tiles, NODES, LANES),...  6.75 us
    all_to_all x1, waiting for transfers between devices, body(): lax.all_to_all(send_head.reshape(-1), AXES, split_axis=0, concat_axis=0,...  6.7 us
    all_to_all x1, starting transfers between devices, body(): recv = lax.all_to_all(send, AXES, split_axis=0, concat_axis=0, tiled=True)  5.75 us
    pallas_call x1, Pallas kernels, body(): pl.pallas_call(place_kernel, out_shape=(struct((3, EL, NODES), F32), stru...  5.53 us
  transfers between devices with their start and end apart: 8, of which 4 were waited for; matrix products, arithmetic and copies ran while one was open for 0% of the time, Pallas kernels for 30%

profile of v3, /device:TPU:0, one launch (start us, length us, event | category | flops | bytes accessed | tf_op | source)
XLA Modules:
  0.0 85.8 jit_solution(13823305682126909577)
XLA Ops:
  0.6 7.6 %moving.1 = (f32[768,128]{1,0:T(8,128)}, s32[1,512]{1,0:T(1,128)}) custom-call(s32[1]{0:T(128)} %bitcast.refs_0_.rank_ref, s32[1,512]{1,0:T(1,128)} %bitcast.12, s32[1,512]{1,0:T(1,128)} %bitcast.15, f32[3,512,512]{2,1,0:T(8,128)} %bitcast.7, f32[512,128]{1,0:T(8,128)} %refs_4_.3), custom_call_target="tpu_custom_call" | custom-call | bytes 18000000 | tf_op jit(solution)/shard_map/moving/pallas_call | solution.py:569
  8.3 11.2 %all-to-all-start = ((f32[128,768,1]{1,2,0:T(1,128)}), f32[128,768,1]{1,2,0:T(1,128)S(1)}, u32[]{:S(2)}, u32[]{:S(2)}) async-start(f32[128,768,1]{1,2,0:T(1,128)} %bitcast.18), calls=%async_computation | async-start | bytes 786432 | tf_op jit(solution)/shard_map/all_to_all | solution.py:598
  19.4 5.4 %pack.1 = f32[128,48,128]{2,1,0:T(8,128)} custom-call(s32[1,512]{1,0:T(1,128)} %get-tuple-element.25.position_ref, f32[3,512,512]{2,1,0:T(8,128)} %bitcast.8), custom_call_target="tpu_custom_call" | custom-call | bytes 15000000 | tf_op jit(solution)/shard_map/pack/pallas_call | solution.py:600
  24.8 0.0 copy-start
  24.8 0.0 copy-start.2
  24.8 0.0 copy-start.3
  24.8 6.7 %all-to-all-done = f32[128,768,1]{1,2,0:T(1,128)S(1)} async-done(((f32[128,768,1]{1,2,0:T(1,128)}), f32[128,768,1]{1,2,0:T(1,128)S(1)}, u32[]{:S(2)}, u32[]{:S(2)}) %all-to-all-start) | async-done | bytes 393248 | tf_op jit(solution)/shard_map/all_to_all | solution.py:598
  31.5 5.7 %all-to-all-start.1 = ((f32[128,48,128]{2,1,0:T(8,128)}), f32[128,48,128]{2,1,0:T(8,128)}, u32[]{:S(2)}, u32[]{:S(2)}) async-start(f32[128,48,128]{2,1,0:T(8,128)} %pack.1), calls=%async_computation.1 | async-start | bytes 6291456 | tf_op jit(solution)/shard_map/all_to_all | solution.py:609
  37.3 0.0 copy-done
  37.3 0.0 copy-done.2
  37.3 0.0 copy-done.3
  37.3 0.0 copy-start.1
  37.3 0.9 %copy-done.1 = f32[512,128]{1,0:T(8,128)S(1)} copy-done((f32[512,128]{1,0:T(8,128)S(1)}, f32[512,128]{1,0:T(8,128)}, u32[]{:S(2)}) %copy-start.1) | copy-done | bytes 262168
  38.3 5.6 %staying.1 = (f32[256,256]{1,0:T(8,128)S(1)}, s32[1,256]{1,0:T(1,128)S(1)}) custom-call(s32[1]{0:T(128)} %bitcast.refs_0_.rank_ref, s32[1,512]{1,0:T(1,128)S(1)} %bitcast.13, s32[1,512]{1,0:T(1,128)S(1)} %bitcast.16, f32[3,512,512]{2,1,0:T(8,128)S(1)} %bitcast.9, f32[512,128]{1,0:T(8,128)S(1)} %copy-done.1), custom_call_target="tpu_custom_call" | custom-call | bytes 18000000 | tf_op jit(solution)/shard_map/staying/pallas_call | solution.py:569
  43.9 6.7 %force.1 = (f32[3,4,512,128]{3,2,1,0:T(8,128)S(1)}, f32[3,64,128]{2,1,0:T(8,128)S(1)}, f32[3,64,128]{2,1,0:T(8,128)S(1)}, f32[3,64,128]{2,1,0:T(8,128)S(1)}, f32...) custom-call(f32[256,256]{1,0:T(8,128)S(1)} %get-tuple-element.21.hea, ...), custom_call_target="tpu_custom_call" | custom-call | bytes 24000000 | tf_op jit(solution)/shard_map/force/pallas_call | solution.py:612
  50.6 2.7 %collective-permute-start = (f32[3,64,128]{2,1,0:T(8,128)S(1)}, f32[3,64,128]{2,1,0:T(8,128)S(1)}, u32[]{:S(2)}, u32[]{:S(2)}) collective-permute-start(f32[3,64,128]{2,1,0:T(8,128)S(1)} %get-tuple-element.28), channel_id=1, source_target_pairs={{0,8},{1,9},{2,10},{3,11},{4,12},{5,13},{6,14},{7,15},{8,16},{9,17... | collective-permute-start | bytes 294920 | tf_op jit(solution)/shard_map/ppermute | solution.py:537
  53.4 1.3 %collective-permute-start.1 = (f32[3,64,128]{2,1,0:T(8,128)S(1)}, f32[3,64,128]{2,1,0:T(8,128)S(1)}, u32[]{:S(2)}, u32[]{:S(2)}) collective-permute-start(f32[3,64,128]{2,1,0:T(8,128)S(1)} %get-tuple-element.29), channel_id=1, source_target_pairs={{8,0},{9,1},{10,2},{11,3},{12,4},{13,5},{14,6},{15,7},{16,8},{17,9... | collective-permute-start | bytes 294920 | tf_op jit(solution)/shard_map/ppermute | solution.py:537
  54.7 1.8 %collective-permute-start.2 = (f32[3,64,128]{2,1,0:T(8,128)S(1)}, f32[3,64,128]{2,1,0:T(8,128)S(1)}, u32[]{:S(2)}, u32[]{:S(2)}) collective-permute-start(f32[3,64,128]{2,1,0:T(8,128)S(1)} %get-tuple-element.31), channel_id=1, source_target_pairs={{0,1},{1,2},{2,3},{3,4},{4,5},{5,6},{6,7},{8,9},{9,10},{10,11},{11... | collective-permute-start | bytes 294920 | tf_op jit(solution)/shard_map/ppermute | solution.py:537
  56.4 5.9 %collective-permute-start.3 = (f32[3,8,128]{2,1,0:T(8,128)S(1)}, f32[3,8,128]{2,1,0:T(8,128)S(1)}, u32[]{:S(2)}, u32[]{:S(2)}) collective-permute-start(f32[3,8,128]{2,1,0:T(8,128)S(1)} %get-tuple-element.32), channel_id=1, source_target_pairs={{0,9},{1,10},{2,11},{3,12},{4,13},{5,14},{6,15},{8,17},{9,18},{10,... | collective-permute-start | bytes 36872 | tf_op jit(solution)/shard_map/ppermute | solution.py:537
  62.3 0.8 collective-permute-start.4
  63.2 2.7 %base.1 = (f32[3,512,512]{2,1,0:T(8,128)}, f32[8,128]{1,0:T(8,128)S(1)}) custom-call(s32[1]{0:T(128)} %bitcast.refs_0_.rank_ref, s32[1,512]{1,0:T(1,128)S(1)} %bitcast.14, f32[3,512,512]{2,1,0:T(8,128)S(1)} %bitcast.10, f32[3,4,512,128]{3,2,1,0:T(8,128)S(1)} %get-tuple-element.26.force_ref), custom_call_target="tpu_custom_call" | custom-call | bytes 15000000 | tf_op jit(solution)/shard_map/base/pallas_call | solution.py:632
  65.9 5.7 %collective-permute-done.3.cb_ref = f32[3,8,128]{2,1,0:T(8,128)S(1)} collective-permute-done((f32[3,8,128]{2,1,0:T(8,128)S(1)}, f32[3,8,128]{2,1,0:T(8,128)S(1)}, u32[]{:S(2)}, u32[]{:S(2)}) %collective-permute-start.3) | collective-permute-done | bytes 12320 | tf_op jit(solution)/shard_map/ppermute | solution.py:537
  71.6 0.0 collective-permute-done.4.ca_ref
  71.6 0.0 collective-permute-done.below_ref.xb_ref
  71.6 2.3 %collective-permute-done.1.above_ref.xa_ref = f32[3,64,128]{2,1,0:T(8,128)S(1)} collective-permute-done((f32[3,64,128]{2,1,0:T(8,128)S(1)}, f32[3,64,128]{2,1,0:T(8,128)S(1)}, u32[]{:S(2)}, u32[]{:S(2)}) %collective-permute-start.1) | collective-permute-done | bytes 98336 | tf_op jit(solution)/shard_map/ppermute | solution.py:537
  73.9 0.0 collective-permute-done.2.yb_ref
  73.9 0.1 edge.1
  73.9 1.3 %collective-permute-start.5 = (f32[3,64,128]{2,1,0:T(8,128)S(1)}, f32[3,64,128]{2,1,0:T(8,128)S(1)}, u32[]{:S(2)}, u32[]{:S(2)}) collective-permute-start(f32[3,64,128]{2,1,0:T(8,128)S(1)} %get-tuple-element.37), channel_id=1, source_target_pairs={{1,0},{2,1},{3,2},{4,3},{5,4},{6,5},{7,6},{9,8},{10,9},{11,10},{12... | collective-permute-start | bytes 294920 | tf_op jit(solution)/shard_map/ppermute | solution.py:537
  75.2 3.8 %all-to-all-done.1.recv_ref = f32[128,48,128]{2,1,0:T(8,128)} async-done(((f32[128,48,128]{2,1,0:T(8,128)}), f32[128,48,128]{2,1,0:T(8,128)}, u32[]{:S(2)}, u32[]{:S(2)}) %all-to-all-start.1) | async-done | bytes 3145760 | tf_op jit(solution)/shard_map/all_to_all | solution.py:609
  79.0 5.5 %place.1 = (f32[3,512,512]{2,1,0:T(8,128)}, f32[3,64,512]{2,1,0:T(8,128)S(1)}) custom-call(s32[1,512]{1,0:T(1,128)S(1)} %get-tuple-element.24.slot_ref, f32[128,48,128]{2,1,0:T(8,128)} %all-to-all-done.1.recv_ref, f32[3,512,512]{2,1,0:T(8,128)} %get-tuple-element.27.base_ref, f32[3,64,128]{2,1,0:T(8,128)S(1)} %collective-permute-done.below_ref.xb_ref, ...), custom_call_target="tpu_custom_call" | custom-call | bytes 9000000 | tf_op jit(solution)/shard_map/place/pallas_call | solution.py:657
  84.6 0.0 collective-permute-done.5.ya_ref
  84.6 1.1 %lines.1 = f32[3,512,512]{2,1,0:T(8,128)} custom-call(f32[3,64,512]{2,1,0:T(8,128)S(1)} %get-tuple-element.36.ends_ref, f32[3,64,128]{2,1,0:T(8,128)S(1)} %collective-permute-done.5.ya_ref, f32[3,512,512]{2,1,0:T(8,128)} %get-tuple-element.38.inner_ref), custom_call_target="tpu_custom_call", output_to_operand_aliasing={{}: (2, {})} | custom-call | bytes 3000000 | tf_op jit(solution)/shard_map/lines/pallas_call | solution.py:681
Async XLA Ops:
  8.3 23.3 %all-to-all-start = ((f32[128,768,1]{1,2,0:T(1,128)}), f32[128,768,1]{1,2,0:T(1,128)S(1)}, u32[]{:S(2)}, u32[]{:S(2)}) async-start(f32[128,768,1]{1,2,0:T(1,128)} %bitcast.18), calls=%async_computation | async-start | bytes 786432 | tf_op jit(solution)/shard_map/all_to_all | solution.py:598
  24.8 12.5 %copy-start = (f32[512,3,512]{2,0,1:T(8,128)S(1)}, f32[512,3,512]{2,0,1:T(8,128)}, u32[]{:S(2)}) copy-start(f32[512,3,512]{2,0,1:T(8,128)} %param.4) | copy-start | bytes 9437188
  24.8 12.5 %copy-start.2 = (s32[512]{0:T(512)S(1)}, s32[512]{0:T(512)}, u32[]{:S(2)}) copy-start(s32[512]{0:T(512)} %param.7) | copy-start | bytes 6148
  24.8 12.5 %copy-start.3 = (s32[512]{0:T(512)S(1)}, s32[512]{0:T(512)}, u32[]{:S(2)}) copy-start(s32[512]{0:T(512)} %param.6) | copy-start | bytes 6148
  31.5 47.5 %all-to-all-start.1 = ((f32[128,48,128]{2,1,0:T(8,128)}), f32[128,48,128]{2,1,0:T(8,128)}, u32[]{:S(2)}, u32[]{:S(2)}) async-start(f32[128,48,128]{2,1,0:T(8,128)} %pack.1), calls=%async_computation.1 | async-start | bytes 6291456 | tf_op jit(solution)/shard_map/all_to_all | solution.py:609
  37.3 1.0 %copy-start.1 = (f32[512,128]{1,0:T(8,128)S(1)}, f32[512,128]{1,0:T(8,128)}, u32[]{:S(2)}) copy-start(f32[512,128]{1,0:T(8,128)} %refs_4_.3) | copy-start | bytes 786436
  50.6 21.0 %collective-permute-start = (f32[3,64,128]{2,1,0:T(8,128)S(1)}, f32[3,64,128]{2,1,0:T(8,128)S(1)}, u32[]{:S(2)}, u32[]{:S(2)}) collective-permute-start(f32[3,64,128]{2,1,0:T(8,128)S(1)} %get-tuple-element.28), channel_id=1, source_target_pairs={{0,8},{1,9},{2,10},{3,11},{4,12},{5,13},{6,14},{7,15},{8,16},{9,17... | collective-permute-start | bytes 294920 | tf_op jit(solution)/shard_map/ppermute | solution.py:537
  53.4 20.5 %collective-permute-start.1 = (f32[3,64,128]{2,1,0:T(8,128)S(1)}, f32[3,64,128]{2,1,0:T(8,128)S(1)}, u32[]{:S(2)}, u32[]{:S(2)}) collective-permute-start(f32[3,64,128]{2,1,0:T(8,128)S(1)} %get-tuple-element.29), channel_id=1, source_target_pairs={{8,0},{9,1},{10,2},{11,3},{12,4},{13,5},{14,6},{15,7},{16,8},{17,9... | collective-permute-start | bytes 294920 | tf_op jit(solution)/shard_map/ppermute | solution.py:537
  54.7 19.2 %collective-permute-start.2 = (f32[3,64,128]{2,1,0:T(8,128)S(1)}, f32[3,64,128]{2,1,0:T(8,128)S(1)}, u32[]{:S(2)}, u32[]{:S(2)}) collective-permute-start(f32[3,64,128]{2,1,0:T(8,128)S(1)} %get-tuple-element.31), channel_id=1, source_target_pairs={{0,1},{1,2},{2,3},{3,4},{4,5},{5,6},{6,7},{8,9},{9,10},{10,11},{11... | collective-permute-start | bytes 294920 | tf_op jit(solution)/shard_map/ppermute | solution.py:537
  56.4 15.2 %collective-permute-start.3 = (f32[3,8,128]{2,1,0:T(8,128)S(1)}, f32[3,8,128]{2,1,0:T(8,128)S(1)}, u32[]{:S(2)}, u32[]{:S(2)}) collective-permute-start(f32[3,8,128]{2,1,0:T(8,128)S(1)} %get-tuple-element.32), channel_id=1, source_target_pairs={{0,9},{1,10},{2,11},{3,12},{4,13},{5,14},{6,15},{8,17},{9,18},{10,... | collective-permute-start | bytes 36872 | tf_op jit(solution)/shard_map/ppermute | solution.py:537
  62.3 9.3 %collective-permute-start.4 = (f32[3,8,128]{2,1,0:T(8,128)S(1)}, f32[3,8,128]{2,1,0:T(8,128)S(1)}, u32[]{:S(2)}, u32[]{:S(2)}) collective-permute-start(f32[3,8,128]{2,1,0:T(8,128)S(1)} %get-tuple-element.33), channel_id=1, source_target_pairs={{8,1},{9,2},{10,3},{11,4},{12,5},{13,6},{14,7},{16,9},{17,10},{18,... | collective-permute-start | bytes 36872 | tf_op jit(solution)/shard_map/ppermute | solution.py:537
  73.9 10.6 %collective-permute-start.5 = (f32[3,64,128]{2,1,0:T(8,128)S(1)}, f32[3,64,128]{2,1,0:T(8,128)S(1)}, u32[]{:S(2)}, u32[]{:S(2)}) collective-permute-start(f32[3,64,128]{2,1,0:T(8,128)S(1)} %get-tuple-element.37), channel_id=1, source_target_pairs={{1,0},{2,1},{3,2},{4,3},{5,4},{6,5},{7,6},{9,8},{10,9},{11,10},{12... | collective-permute-start | bytes 294920 | tf_op jit(solution)/shard_map/ppermute | solution.py:537

commit v4 on v3

--- a/solution.py
+++ b/solution.py
@@ -282,6 +282,7 @@
     right_ref,
     part_ref,
     slot_ref,
+    peers_ref,
     tp_ref,
     push_ref,
     basis_ref,
@@ -303,7 +304,18 @@
     order = turned.astype(BF16)
     row = jnp.dot(high, order, preferred_element_type=F32)
     row = row + jnp.dot(low, order, preferred_element_type=F32)
-    slot_ref[...] = row[0:1].astype(jnp.int32)
+    row = row[0:1].astype(jnp.int32)
+    filled = row > 0
+    earlier = (iota((devices * CAP, devices * CAP), 0) < iota((devices * CAP, devices * CAP), 1)).astype(BF16)
+    rank = jnp.dot(
+        jnp.broadcast_to(filled.astype(F32), (8, devices * CAP)).astype(BF16),
+        earlier,
+        preferred_element_type=F32,
+    )[0:1]
+    key = jnp.where(filled, rank.astype(jnp.int32), -1)
+    packed = (iota((MOVERS, devices * CAP), 0) == key).astype(BF16)
+    slot_ref[...] = picked_row(row, packed).astype(jnp.int32)
+    peers_ref[...] = picked_row(iota((1, devices * CAP), 1) // CAP, packed).astype(jnp.int32)
     slots = jnp.concatenate([slot_row, stay_slot_ref[...]], axis=1)
     onehot = (iota((EL, EL + MOVERS), 0) + 1 == slots).astype(BF16)
     arrived = jnp.concatenate([particles, extra], axis=1)
@@ -449,6 +461,7 @@
 
 
 def place_kernel(
+    peers_ref,
     slot_ref,
     recv_ref,
     base_ref,
@@ -464,32 +477,34 @@
     arrived,
     left,
 ):
-    devices = recv_ref.shape[0]
     tiles = EL // LANES
+
+    def fetch(c, carry):
+        peer = peers_ref[0, CAP * c]
+        pltpu.make_async_copy(recv_ref.at[peer], recv_held.at[c], arrived.at[0, 0]).start()
+        return carry
+
+    lax.fori_loop(0, PEERS, fetch, 0, unroll=8)
+
+    whole_recv = pltpu.make_async_copy(recv_ref.at[pl.ds(0, PEERS)], recv_held, arrived.at[0, 0])
     loads = []
     for f in range(3):
-        part = (pl.ds(0, devices), pl.ds(COMP * f, COMP))
-        loads.append(
-            (
-                pltpu.make_async_copy(recv_ref.at[part], recv_held.at[f], arrived.at[f, 0]),
-                pltpu.make_async_copy(base_ref.at[f], held_ref.at[f], arrived.at[f, 1]),
-            )
-        )
-        for load in loads[f]:
-            load.start()
-    onehot = (iota((EL, EL), 0) + 1 == slot_ref[...]).astype(BF16)
+        loads.append(pltpu.make_async_copy(base_ref.at[f], held_ref.at[f], arrived.at[f, 1]))
+        loads[f].start()
+    onehot = (iota((EL, MOVERS), 0) + 1 == slot_ref[...]).astype(BF16)
     blank = jnp.zeros((64, LANES), F32)
     line_ref[...] = jnp.zeros((NODES, LANES), F32)
     for f in range(3):
         lows_ref[f] = lines_of(low_ref[f], 0, line_ref)
     copies = []
     for f in range(3):
-        loads[f][0].wait()
+        if f == 0:
+            whole_recv.wait()
         pieces = []
         for h in range(2):
-            pieces += list(deinterleave(recv_held[f, :, 8 * h : 8 * h + 8, :]))
+            pieces += list(deinterleave(recv_held[:, COMP * f + 8 * h : COMP * f + 8 * h + 8, :]))
         rows = picked(onehot, jnp.concatenate(pieces, axis=1))
-        loads[f][1].wait()
+        loads[f].wait()
         held_ref[f] += rows
         delta = jnp.concatenate([face_delta(xb_ref[f]), blank], axis=0)
         held_ref[f, 0:LANES, 0:LANES] += delta.T
@@ -609,7 +624,7 @@
     recv = lax.all_to_all(send, AXES, split_axis=0, concat_axis=0, tiled=True)
     face = struct((3, 64, LANES), F32)
     corner = struct((3, NP, LANES), F32)
-    force, xup, xdn, yup, ydn, left, right, particles_next, slots = pl.pallas_call(
+    force, xup, xdn, yup, ydn, left, right, particles_next, slots, peers = pl.pallas_call(
         force_kernel,
         out_shape=(
             struct((3, tiles, NODES, LANES), F32),
@@ -620,10 +635,11 @@
             corner,
             corner,
             struct((EL, PARTS), F32),
-            struct((1, EL), jnp.int32),
+            struct((1, MOVERS), jnp.int32),
+            struct((1, MOVERS), jnp.int32),
         ),
         in_specs=whole(3),
-        out_specs=tuple(whole(9)),
+        out_specs=tuple(whole(10)),
         scratch_shapes=[tile_scratch, tile_scratch, basis_scratch, work_scratch],
         compiler_params=params(40),
         cost_estimate=cost(8),
@@ -657,10 +673,10 @@
     inner, ends_out = pl.pallas_call(
         place_kernel,
         out_shape=(struct((3, EL, NODES), F32), struct(ends, F32)),
-        in_specs=whole(1) + [in_hbm, in_hbm] + whole(3),
+        in_specs=smem + whole(1) + [in_hbm, in_hbm] + whole(3),
         out_specs=(in_hbm, whole(1)[0]),
         scratch_shapes=[
-            pltpu.VMEM((3, devices, COMP, LANES), F32),
+            pltpu.VMEM((PEERS, 3 * COMP, LANES), F32),
             pltpu.VMEM((3, EL, NODES), F32),
             pltpu.VMEM((NODES, LANES), F32),
             pltpu.VMEM(ends, F32),
@@ -671,6 +687,7 @@
         cost_estimate=cost(3),
         name="place",
     )(
+        peers,
         slots,
         recv,
         pltpu.with_memory_space_constraint(base, pltpu.HBM),

time: 86.2 us -> 85.6 us (level)
  transfers between devices with their start and end apart: 8 -> 8, of which waited for: 4 -> 4; matrix products, arithmetic and copies ran while one was open for 0% -> 0% of each run, Pallas kernels for 30% -> 31%
where the time goes in v4:
time: 85.6 us; the launch traced here: 85.1 us
  Pallas kernels  34.7 us (41%)
  starting transfers between devices  30.7 us (36%)
  waiting for transfers between devices  17.9 us (21%)
  local copies, waits for them, and re-layouts  0.96 us (1%)
  between operations  0.93 us (1%)
    ppermute x6, starting transfers between devices, passed_along(): return lax.ppermute(x, AXES, pairs)  13.8 us
    pallas_call x2, Pallas kernels, interp(): pl.pallas_call(functools.partial(interp_kernel, moves), out_shape=out_sha...  13.2 us
    all_to_all x1, starting transfers between devices, body(): lax.all_to_all(send_head.reshape(-1), AXES, split_axis=0, concat_axis=0,...  11.2 us
    ppermute x6, waiting for transfers between devices, passed_along(): return lax.ppermute(x, AXES, pairs)  7.41 us
    pallas_call x1, Pallas kernels, body(): pl.pallas_call(force_kernel, out_shape=(struct((3, tiles, NODES, LANES),...  7.34 us
    all_to_all x1, waiting for transfers between devices, body(): lax.all_to_all(send_head.reshape(-1), AXES, split_axis=0, concat_axis=0,...  6.7 us
    all_to_all x1, starting transfers between devices, body(): recv = lax.all_to_all(send, AXES, split_axis=0, concat_axis=0, tiled=True)  5.75 us
    pallas_call x1, Pallas kernels, body(): pl.pallas_call(pack_kernel, out_shape=struct((devices, 3 * COMP, LANES),...  5.42 us
  transfers between devices with their start and end apart: 8, of which 4 were waited for; matrix products, arithmetic and copies ran while one was open for 0% of the time, Pallas kernels for 31%

profile of v4, /device:TPU:0, one launch (start us, length us, event | category | flops | bytes accessed | tf_op | source)
XLA Modules:
  0.0 85.1 jit_solution(18101623884806460698)
XLA Ops:
  0.6 7.6 %moving.1 = (f32[768,128]{1,0:T(8,128)}, s32[1,512]{1,0:T(1,128)}) custom-call(s32[1]{0:T(128)} %bitcast.refs_0_.rank_ref, s32[1,512]{1,0:T(1,128)} %bitcast.12, s32[1,512]{1,0:T(1,128)} %bitcast.15, f32[3,512,512]{2,1,0:T(8,128)} %bitcast.7, f32[512,128]{1,0:T(8,128)} %refs_4_.3), custom_call_target="tpu_custom_call" | custom-call | bytes 18000000 | tf_op jit(solution)/shard_map/moving/pallas_call | solution.py:584
  8.3 11.2 %all-to-all-start = ((f32[128,768,1]{1,2,0:T(1,128)}), f32[128,768,1]{1,2,0:T(1,128)S(1)}, u32[]{:S(2)}, u32[]{:S(2)}) async-start(f32[128,768,1]{1,2,0:T(1,128)} %bitcast.18), calls=%async_computation | async-start | bytes 786432 | tf_op jit(solution)/shard_map/all_to_all | solution.py:613
  19.4 5.4 %pack.1 = f32[128,48,128]{2,1,0:T(8,128)} custom-call(s32[1,512]{1,0:T(1,128)} %get-tuple-element.27.position_ref, f32[3,512,512]{2,1,0:T(8,128)} %bitcast.8), custom_call_target="tpu_custom_call" | custom-call | bytes 15000000 | tf_op jit(solution)/shard_map/pack/pallas_call | solution.py:615
  24.8 0.0 copy-start
  24.8 0.0 copy-start.2
  24.8 0.0 copy-start.3
  24.8 6.7 %all-to-all-done = f32[128,768,1]{1,2,0:T(1,128)S(1)} async-done(((f32[128,768,1]{1,2,0:T(1,128)}), f32[128,768,1]{1,2,0:T(1,128)S(1)}, u32[]{:S(2)}, u32[]{:S(2)}) %all-to-all-start) | async-done | bytes 393248 | tf_op jit(solution)/shard_map/all_to_all | solution.py:613
  31.5 5.7 %all-to-all-start.1 = ((f32[128,48,128]{2,1,0:T(8,128)}), f32[128,48,128]{2,1,0:T(8,128)}, u32[]{:S(2)}, u32[]{:S(2)}) async-start(f32[128,48,128]{2,1,0:T(8,128)} %pack.1), calls=%async_computation.1 | async-start | bytes 6291456 | tf_op jit(solution)/shard_map/all_to_all | solution.py:624
  37.3 0.0 copy-done
  37.3 0.0 copy-done.2
  37.3 0.0 copy-done.3
  37.3 0.0 copy-start.1
  37.3 0.9 %copy-done.1 = f32[512,128]{1,0:T(8,128)S(1)} copy-done((f32[512,128]{1,0:T(8,128)S(1)}, f32[512,128]{1,0:T(8,128)}, u32[]{:S(2)}) %copy-start.1) | copy-done | bytes 262168
  38.3 5.6 %staying.1 = (f32[256,256]{1,0:T(8,128)S(1)}, s32[1,256]{1,0:T(1,128)S(1)}) custom-call(s32[1]{0:T(128)} %bitcast.refs_0_.rank_ref, s32[1,512]{1,0:T(1,128)S(1)} %bitcast.13, s32[1,512]{1,0:T(1,128)S(1)} %bitcast.16, f32[3,512,512]{2,1,0:T(8,128)S(1)} %bitcast.9, f32[512,128]{1,0:T(8,128)S(1)} %copy-done.1), custom_call_target="tpu_custom_call" | custom-call | bytes 18000000 | tf_op jit(solution)/shard_map/staying/pallas_call | solution.py:584
  43.9 7.3 %force.1 = (f32[3,4,512,128]{3,2,1,0:T(8,128)S(1)}, f32[3,64,128]{2,1,0:T(8,128)S(1)}, f32[3,64,128]{2,1,0:T(8,128)S(1)}, f32[3,64,128]{2,1,0:T(8,128)S(1)}, f32...) custom-call(f32[256,256]{1,0:T(8,128)S(1)} %get-tuple-element.22.hea, ...), custom_call_target="tpu_custom_call" | custom-call | bytes 24000000 | tf_op jit(solution)/shard_map/force/pallas_call | solution.py:627
  51.2 2.7 %collective-permute-start = (f32[3,64,128]{2,1,0:T(8,128)S(1)}, f32[3,64,128]{2,1,0:T(8,128)S(1)}, u32[]{:S(2)}, u32[]{:S(2)}) collective-permute-start(f32[3,64,128]{2,1,0:T(8,128)S(1)} %get-tuple-element.30), channel_id=1, source_target_pairs={{0,8},{1,9},{2,10},{3,11},{4,12},{5,13},{6,14},{7,15},{8,16},{9,17... | collective-permute-start | bytes 294920 | tf_op jit(solution)/shard_map/ppermute | solution.py:552
  53.9 1.3 %collective-permute-start.1 = (f32[3,64,128]{2,1,0:T(8,128)S(1)}, f32[3,64,128]{2,1,0:T(8,128)S(1)}, u32[]{:S(2)}, u32[]{:S(2)}) collective-permute-start(f32[3,64,128]{2,1,0:T(8,128)S(1)} %get-tuple-element.31), channel_id=1, source_target_pairs={{8,0},{9,1},{10,2},{11,3},{12,4},{13,5},{14,6},{15,7},{16,8},{17,9... | collective-permute-start | bytes 294920 | tf_op jit(solution)/shard_map/ppermute | solution.py:552
  55.2 2.0 %collective-permute-start.2 = (f32[3,64,128]{2,1,0:T(8,128)S(1)}, f32[3,64,128]{2,1,0:T(8,128)S(1)}, u32[]{:S(2)}, u32[]{:S(2)}) collective-permute-start(f32[3,64,128]{2,1,0:T(8,128)S(1)} %get-tuple-element.33), channel_id=1, source_target_pairs={{0,1},{1,2},{2,3},{3,4},{4,5},{5,6},{6,7},{8,9},{9,10},{10,11},{11... | collective-permute-start | bytes 294920 | tf_op jit(solution)/shard_map/ppermute | solution.py:552
  57.2 5.9 %collective-permute-start.3 = (f32[3,8,128]{2,1,0:T(8,128)S(1)}, f32[3,8,128]{2,1,0:T(8,128)S(1)}, u32[]{:S(2)}, u32[]{:S(2)}) collective-permute-start(f32[3,8,128]{2,1,0:T(8,128)S(1)} %get-tuple-element.34), channel_id=1, source_target_pairs={{0,9},{1,10},{2,11},{3,12},{4,13},{5,14},{6,15},{8,17},{9,18},{10,... | collective-permute-start | bytes 36872 | tf_op jit(solution)/shard_map/ppermute | solution.py:552
  63.1 0.7 collective-permute-start.4
  63.8 2.7 %base.1 = (f32[3,512,512]{2,1,0:T(8,128)}, f32[8,128]{1,0:T(8,128)S(1)}) custom-call(s32[1]{0:T(128)} %bitcast.refs_0_.rank_ref, s32[1,512]{1,0:T(1,128)S(1)} %bitcast.14, f32[3,512,512]{2,1,0:T(8,128)S(1)} %bitcast.10, f32[3,4,512,128]{3,2,1,0:T(8,128)S(1)} %get-tuple-element.28.force_ref), custom_call_target="tpu_custom_call" | custom-call | bytes 15000000 | tf_op jit(solution)/shard_map/base/pallas_call | solution.py:648
  66.5 5.1 %collective-permute-done.3.cb_ref = f32[3,8,128]{2,1,0:T(8,128)S(1)} collective-permute-done((f32[3,8,128]{2,1,0:T(8,128)S(1)}, f32[3,8,128]{2,1,0:T(8,128)S(1)}, u32[]{:S(2)}, u32[]{:S(2)}) %collective-permute-start.3) | collective-permute-done | bytes 12320 | tf_op jit(solution)/shard_map/ppermute | solution.py:552
  71.6 0.0 collective-permute-done.4.ca_ref
  71.6 0.0 collective-permute-done.below_ref.xb_ref
  71.6 2.3 %collective-permute-done.1.above_ref.xa_ref = f32[3,64,128]{2,1,0:T(8,128)S(1)} collective-permute-done((f32[3,64,128]{2,1,0:T(8,128)S(1)}, f32[3,64,128]{2,1,0:T(8,128)S(1)}, u32[]{:S(2)}, u32[]{:S(2)}) %collective-permute-start.1) | collective-permute-done | bytes 98336 | tf_op jit(solution)/shard_map/ppermute | solution.py:552
  73.9 0.0 collective-permute-done.2.yb_ref
  73.9 0.1 edge.1
  73.9 1.3 %collective-permute-start.5 = (f32[3,64,128]{2,1,0:T(8,128)S(1)}, f32[3,64,128]{2,1,0:T(8,128)S(1)}, u32[]{:S(2)}, u32[]{:S(2)}) collective-permute-start(f32[3,64,128]{2,1,0:T(8,128)S(1)} %get-tuple-element.39), channel_id=1, source_target_pairs={{1,0},{2,1},{3,2},{4,3},{5,4},{6,5},{7,6},{9,8},{10,9},{11,10},{12... | collective-permute-start | bytes 294920 | tf_op jit(solution)/shard_map/ppermute | solution.py:552
  75.2 3.8 %all-to-all-done.1.recv_ref = f32[128,48,128]{2,1,0:T(8,128)} async-done(((f32[128,48,128]{2,1,0:T(8,128)}), f32[128,48,128]{2,1,0:T(8,128)}, u32[]{:S(2)}, u32[]{:S(2)}) %all-to-all-start.1) | async-done | bytes 3145760 | tf_op jit(solution)/shard_map/all_to_all | solution.py:624
  79.0 4.8 %place.1 = (f32[3,512,512]{2,1,0:T(8,128)}, f32[3,64,512]{2,1,0:T(8,128)S(1)}) custom-call(s32[1,256]{1,0:T(1,128)S(1)} %get-tuple-element.25.peers_ref, s32[1,256]{1,0:T(1,128)S(1)} %get-tuple-element.26.slot_ref, f32[128,48,128]{2,1,0:T(8,128)} %all-to-all-done.1.recv_ref, f32[3,512,512]{2,1,0:T(8,128)} %get-tuple-element.29.base_ref, ...), custom_call_target="tpu_custom_call" | custom-call | bytes 9000000 | tf_op jit(solution)/shard_map/place/pallas_call | solution.py:673
  83.9 0.0 collective-permute-done.5.ya_ref
  83.9 1.1 %lines.1 = f32[3,512,512]{2,1,0:T(8,128)} custom-call(f32[3,64,512]{2,1,0:T(8,128)S(1)} %get-tuple-element.38.ends_ref, f32[3,64,128]{2,1,0:T(8,128)S(1)} %collective-permute-done.5.ya_ref, f32[3,512,512]{2,1,0:T(8,128)} %get-tuple-element.40.inner_ref), custom_call_target="tpu_custom_call", output_to_operand_aliasing={{}: (2, {})} | custom-call | bytes 3000000 | tf_op jit(solution)/shard_map/lines/pallas_call | solution.py:698
Async XLA Ops:
  8.3 23.3 %all-to-all-start = ((f32[128,768,1]{1,2,0:T(1,128)}), f32[128,768,1]{1,2,0:T(1,128)S(1)}, u32[]{:S(2)}, u32[]{:S(2)}) async-start(f32[128,768,1]{1,2,0:T(1,128)} %bitcast.18), calls=%async_computation | async-start | bytes 786432 | tf_op jit(solution)/shard_map/all_to_all | solution.py:613
  24.8 12.5 %copy-start = (f32[512,3,512]{2,0,1:T(8,128)S(1)}, f32[512,3,512]{2,0,1:T(8,128)}, u32[]{:S(2)}) copy-start(f32[512,3,512]{2,0,1:T(8,128)} %param.4) | copy-start | bytes 9437188
  24.8 12.5 %copy-start.2 = (s32[512]{0:T(512)S(1)}, s32[512]{0:T(512)}, u32[]{:S(2)}) copy-start(s32[512]{0:T(512)} %param.7) | copy-start | bytes 6148
  24.8 12.5 %copy-start.3 = (s32[512]{0:T(512)S(1)}, s32[512]{0:T(512)}, u32[]{:S(2)}) copy-start(s32[512]{0:T(512)} %param.6) | copy-start | bytes 6148
  31.5 47.5 %all-to-all-start.1 = ((f32[128,48,128]{2,1,0:T(8,128)}), f32[128,48,128]{2,1,0:T(8,128)}, u32[]{:S(2)}, u32[]{:S(2)}) async-start(f32[128,48,128]{2,1,0:T(8,128)} %pack.1), calls=%async_computation.1 | async-start | bytes 6291456 | tf_op jit(solution)/shard_map/all_to_all | solution.py:624
  37.3 1.0 %copy-start.1 = (f32[512,128]{1,0:T(8,128)S(1)}, f32[512,128]{1,0:T(8,128)}, u32[]{:S(2)}) copy-start(f32[512,128]{1,0:T(8,128)} %refs_4_.3) | copy-start | bytes 786436
  51.2 20.4 %collective-permute-start = (f32[3,64,128]{2,1,0:T(8,128)S(1)}, f32[3,64,128]{2,1,0:T(8,128)S(1)}, u32[]{:S(2)}, u32[]{:S(2)}) collective-permute-start(f32[3,64,128]{2,1,0:T(8,128)S(1)} %get-tuple-element.30), channel_id=1, source_target_pairs={{0,8},{1,9},{2,10},{3,11},{4,12},{5,13},{6,14},{7,15},{8,16},{9,17... | collective-permute-start | bytes 294920 | tf_op jit(solution)/shard_map/ppermute | solution.py:552
  53.9 19.9 %collective-permute-start.1 = (f32[3,64,128]{2,1,0:T(8,128)S(1)}, f32[3,64,128]{2,1,0:T(8,128)S(1)}, u32[]{:S(2)}, u32[]{:S(2)}) collective-permute-start(f32[3,64,128]{2,1,0:T(8,128)S(1)} %get-tuple-element.31), channel_id=1, source_target_pairs={{8,0},{9,1},{10,2},{11,3},{12,4},{13,5},{14,6},{15,7},{16,8},{17,9... | collective-permute-start | bytes 294920 | tf_op jit(solution)/shard_map/ppermute | solution.py:552
  55.2 18.6 %collective-permute-start.2 = (f32[3,64,128]{2,1,0:T(8,128)S(1)}, f32[3,64,128]{2,1,0:T(8,128)S(1)}, u32[]{:S(2)}, u32[]{:S(2)}) collective-permute-start(f32[3,64,128]{2,1,0:T(8,128)S(1)} %get-tuple-element.33), channel_id=1, source_target_pairs={{0,1},{1,2},{2,3},{3,4},{4,5},{5,6},{6,7},{8,9},{9,10},{10,11},{11... | collective-permute-start | bytes 294920 | tf_op jit(solution)/shard_map/ppermute | solution.py:552
  57.2 14.4 %collective-permute-start.3 = (f32[3,8,128]{2,1,0:T(8,128)S(1)}, f32[3,8,128]{2,1,0:T(8,128)S(1)}, u32[]{:S(2)}, u32[]{:S(2)}) collective-permute-start(f32[3,8,128]{2,1,0:T(8,128)S(1)} %get-tuple-element.34), channel_id=1, source_target_pairs={{0,9},{1,10},{2,11},{3,12},{4,13},{5,14},{6,15},{8,17},{9,18},{10,... | collective-permute-start | bytes 36872 | tf_op jit(solution)/shard_map/ppermute | solution.py:552
  63.1 8.5 %collective-permute-start.4 = (f32[3,8,128]{2,1,0:T(8,128)S(1)}, f32[3,8,128]{2,1,0:T(8,128)S(1)}, u32[]{:S(2)}, u32[]{:S(2)}) collective-permute-start(f32[3,8,128]{2,1,0:T(8,128)S(1)} %get-tuple-element.35), channel_id=1, source_target_pairs={{8,1},{9,2},{10,3},{11,4},{12,5},{13,6},{14,7},{16,9},{17,10},{18,... | collective-permute-start | bytes 36872 | tf_op jit(solution)/shard_map/ppermute | solution.py:552
  73.9 9.9 %collective-permute-start.5 = (f32[3,64,128]{2,1,0:T(8,128)S(1)}, f32[3,64,128]{2,1,0:T(8,128)S(1)}, u32[]{:S(2)}, u32[]{:S(2)}) collective-permute-start(f32[3,64,128]{2,1,0:T(8,128)S(1)} %get-tuple-element.39), channel_id=1, source_target_pairs={{1,0},{2,1},{3,2},{4,3},{5,4},{6,5},{7,6},{9,8},{10,9},{11,10},{12... | collective-permute-start | bytes 294920 | tf_op jit(solution)/shard_map/ppermute | solution.py:552

commit v5 on v4

--- a/solution.py
+++ b/solution.py
@@ -49,8 +49,10 @@
 
 def picked(onehot, x):
     high, low = split(x)
-    return jnp.dot(onehot, high, preferred_element_type=F32) + jnp.dot(
-        onehot, low, preferred_element_type=F32
+    return jnp.dot(
+        jnp.concatenate([onehot, onehot], axis=1),
+        jnp.concatenate([high, low], axis=0),
+        preferred_element_type=F32,
     )
 
 
@@ -124,9 +126,17 @@
     )[0:1]
     key = jnp.where(chosen, order.astype(jnp.int32), -1)
     onehot = (iota((MOVERS, EL), 0) == key).astype(BF16)
-    slot_row = picked_row(place % EL + 1, onehot)
     copies[1].wait()
     count_row_ref[...] = picked_row(count_held[...], onehot).astype(jnp.int32)
+    slot_row = picked_row(place % EL + 1, onehot)
+    if moves:
+        send_ref, position_ref = out_refs
+        devices = send_ref.shape[0] // HEAD
+        position = pack_positions(place, rank_ref[0])
+        position_ref[...] = position
+        goes_to = picked_row(position, onehot).astype(jnp.int32)
+        goes_to = goes_to % CAP * devices + goes_to // CAP
+        scatter = (iota((devices * CAP, MOVERS), 0) == goes_to).astype(BF16)
     copies[2].wait()
     records = picked(onehot, part_held[...])
     for t in range(tiles):
@@ -139,7 +149,17 @@
                 basis_ref[t, d, n * SLOTS : (n + 1) * SLOTS, :] = rows[n]
         return carry
 
-    lax.fori_loop(0, tiles, make_basis, 0)
+    def gather(f):
+        copies[3 + f].wait()
+        rows = picked(onehot, held_ref[f])
+        for t in range(tiles):
+            for j in range(NODES // LANES):
+                cols = slice(j * LANES, (j + 1) * LANES)
+                t_ref[f, t, cols, :] = rows[t * LANES : (t + 1) * LANES, cols].T
+
+    for t in range(tiles):
+        make_basis(t, 0)
+    gather(0)
 
     def step(t, f):
         def basis(which, n, p):
@@ -178,12 +198,8 @@
         return f
 
     for f in range(3):
-        copies[3 + f].wait()
-        rows = picked(onehot, held_ref[f])
-        for t in range(tiles):
-            for j in range(NODES // LANES):
-                cols = slice(j * LANES, (j + 1) * LANES)
-                t_ref[f, t, cols, :] = rows[t * LANES : (t + 1) * LANES, cols].T
+        if f:
+            gather(f)
         lax.fori_loop(0, tiles, step, f)
 
     heads = []
@@ -196,11 +212,6 @@
     if moves:
         send_ref, position_ref = out_refs
         devices = send_ref.shape[0] // HEAD
-        position = pack_positions(place, rank_ref[0])
-        position_ref[...] = position
-        goes_to = picked_row(position, onehot).astype(jnp.int32)
-        goes_to = goes_to % CAP * devices + goes_to // CAP
-        scatter = (iota((devices * CAP, MOVERS), 0) == goes_to).astype(BF16)
         rows = picked(scatter, head)
         lane = iota((devices, LANES), 1)
         for q in range(CAP):
@@ -479,13 +490,10 @@
 ):
     tiles = EL // LANES
 
-    def fetch(c, carry):
-        peer = peers_ref[0, CAP * c]
-        pltpu.make_async_copy(recv_ref.at[peer], recv_held.at[c], arrived.at[0, 0]).start()
-        return carry
-
-    lax.fori_loop(0, PEERS, fetch, 0, unroll=8)
-
+    peers = peers_ref[...]
+    for c in range(PEERS):
+        block = recv_ref.at[peers[0, CAP * c]]
+        pltpu.make_async_copy(block, recv_held.at[c], arrived.at[0, 0]).start()
     whole_recv = pltpu.make_async_copy(recv_ref.at[pl.ds(0, PEERS)], recv_held, arrived.at[0, 0])
     loads = []
     for f in range(3):
@@ -673,7 +681,7 @@
     inner, ends_out = pl.pallas_call(
         place_kernel,
         out_shape=(struct((3, EL, NODES), F32), struct(ends, F32)),
-        in_specs=smem + whole(1) + [in_hbm, in_hbm] + whole(3),
+        in_specs=whole(2) + [in_hbm, in_hbm] + whole(3),
         out_specs=(in_hbm, whole(1)[0]),
         scratch_shapes=[
             pltpu.VMEM((PEERS, 3 * COMP, LANES), F32),

time: 85.6 us -> 84.5 us (0.987)
  Pallas kernels: 34.7 us -> 33.1 us
    pallas_call x2, Pallas kernels: 13.2 us -> 12.2 us  [interp(): pl.pallas_call(functools.partial(interp_kernel, moves), out_shape=out_sha...]
  transfers between devices with their start and end apart: 8 -> 8, of which waited for: 4 -> 4; matrix products, arithmetic and copies ran while one was open for 0% -> 0% of each run, Pallas kernels for 31% -> 30%
where the time goes in v5:
time: 84.5 us; the launch traced here: 84.1 us
  Pallas kernels  33.1 us (39%)
  starting transfers between devices  30.5 us (36%)
  waiting for transfers between devices  18.6 us (22%)
  local copies, waits for them, and re-layouts  0.96 us (1%)
  between operations  0.93 us (1%)
    ppermute x6, starting transfers between devices, passed_along(): return lax.ppermute(x, AXES, pairs)  13.6 us
    pallas_call x2, Pallas kernels, interp(): pl.pallas_call(functools.partial(interp_kernel, moves), out_shape=out_sha...  12.2 us
    all_to_all x1, starting transfers between devices, body(): lax.all_to_all(send_head.reshape(-1), AXES, split_axis=0, concat_axis=0,...  11.2 us
    ppermute x6, waiting for transfers between devices, passed_along(): return lax.ppermute(x, AXES, pairs)  8.02 us
    pallas_call x1, Pallas kernels, body(): pl.pallas_call(force_kernel, out_shape=(struct((3, tiles, NODES, LANES),...  7.36 us
    all_to_all x1, waiting for transfers between devices, body(): lax.all_to_all(send_head.reshape(-1), AXES, split_axis=0, concat_axis=0,...  6.74 us
    all_to_all x1, starting transfers between devices, body(): recv = lax.all_to_all(send, AXES, split_axis=0, concat_axis=0, tiled=True)  5.75 us
    pallas_call x1, Pallas kernels, body(): pl.pallas_call(pack_kernel, out_shape=struct((devices, 3 * COMP, LANES),...  5.38 us
  transfers between devices with their start and end apart: 8, of which 4 were waited for; matrix products, arithmetic and copies ran while one was open for 0% of the time, Pallas kernels for 30%

profile of v5, /device:TPU:0, one launch (start us, length us, event | category | flops | bytes accessed | tf_op | source)
XLA Modules:
  0.0 84.1 jit_solution(11415757844753979396)
XLA Ops:
  0.6 7.1 %moving.1 = (f32[768,128]{1,0:T(8,128)}, s32[1,512]{1,0:T(1,128)}) custom-call(s32[1]{0:T(128)} %bitcast.refs_0_.rank_ref, s32[1,512]{1,0:T(1,128)} %bitcast.12, s32[1,512]{1,0:T(1,128)} %bitcast.15, f32[3,512,512]{2,1,0:T(8,128)} %bitcast.7, f32[512,128]{1,0:T(8,128)} %refs_4_.3), custom_call_target="tpu_custom_call" | custom-call | bytes 18000000 | tf_op jit(solution)/shard_map/moving/pallas_call | solution.py:592
  7.7 11.2 %all-to-all-start = ((f32[128,768,1]{1,2,0:T(1,128)}), f32[128,768,1]{1,2,0:T(1,128)S(1)}, u32[]{:S(2)}, u32[]{:S(2)}) async-start(f32[128,768,1]{1,2,0:T(1,128)} %bitcast.18), calls=%async_computation | async-start | bytes 786432 | tf_op jit(solution)/shard_map/all_to_all | solution.py:621
  18.9 5.4 %pack.1 = f32[128,48,128]{2,1,0:T(8,128)} custom-call(s32[1,512]{1,0:T(1,128)} %get-tuple-element.27.position_ref, f32[3,512,512]{2,1,0:T(8,128)} %bitcast.8), custom_call_target="tpu_custom_call" | custom-call | bytes 15000000 | tf_op jit(solution)/shard_map/pack/pallas_call | solution.py:623
  24.3 0.0 copy-start
  24.3 0.0 copy-start.2
  24.3 0.0 copy-start.3
  24.3 6.7 %all-to-all-done = f32[128,768,1]{1,2,0:T(1,128)S(1)} async-done(((f32[128,768,1]{1,2,0:T(1,128)}), f32[128,768,1]{1,2,0:T(1,128)S(1)}, u32[]{:S(2)}, u32[]{:S(2)}) %all-to-all-start) | async-done | bytes 393248 | tf_op jit(solution)/shard_map/all_to_all | solution.py:621
  31.0 5.7 %all-to-all-start.1 = ((f32[128,48,128]{2,1,0:T(8,128)}), f32[128,48,128]{2,1,0:T(8,128)}, u32[]{:S(2)}, u32[]{:S(2)}) async-start(f32[128,48,128]{2,1,0:T(8,128)} %pack.1), calls=%async_computation.1 | async-start | bytes 6291456 | tf_op jit(solution)/shard_map/all_to_all | solution.py:632
  36.8 0.0 copy-done
  36.8 0.0 copy-done.2
  36.8 0.0 copy-done.3
  36.8 0.0 copy-start.1
  36.8 0.9 %copy-done.1 = f32[512,128]{1,0:T(8,128)S(1)} copy-done((f32[512,128]{1,0:T(8,128)S(1)}, f32[512,128]{1,0:T(8,128)}, u32[]{:S(2)}) %copy-start.1) | copy-done | bytes 262168
  37.8 5.1 %staying.1 = (f32[256,256]{1,0:T(8,128)S(1)}, s32[1,256]{1,0:T(1,128)S(1)}) custom-call(s32[1]{0:T(128)} %bitcast.refs_0_.rank_ref, s32[1,512]{1,0:T(1,128)S(1)} %bitcast.13, s32[1,512]{1,0:T(1,128)S(1)} %bitcast.16, f32[3,512,512]{2,1,0:T(8,128)S(1)} %bitcast.9, f32[512,128]{1,0:T(8,128)S(1)} %copy-done.1), custom_call_target="tpu_custom_call" | custom-call | bytes 18000000 | tf_op jit(solution)/shard_map/staying/pallas_call | solution.py:592
  42.9 7.4 %force.1 = (f32[3,4,512,128]{3,2,1,0:T(8,128)S(1)}, f32[3,64,128]{2,1,0:T(8,128)S(1)}, f32[3,64,128]{2,1,0:T(8,128)S(1)}, f32[3,64,128]{2,1,0:T(8,128)S(1)}, f32...) custom-call(f32[256,256]{1,0:T(8,128)S(1)} %get-tuple-element.22.hea, ...), custom_call_target="tpu_custom_call" | custom-call | bytes 24000000 | tf_op jit(solution)/shard_map/force/pallas_call | solution.py:635
  50.3 2.7 %collective-permute-start = (f32[3,64,128]{2,1,0:T(8,128)S(1)}, f32[3,64,128]{2,1,0:T(8,128)S(1)}, u32[]{:S(2)}, u32[]{:S(2)}) collective-permute-start(f32[3,64,128]{2,1,0:T(8,128)S(1)} %get-tuple-element.30), channel_id=1, source_target_pairs={{0,8},{1,9},{2,10},{3,11},{4,12},{5,13},{6,14},{7,15},{8,16},{9,17... | collective-permute-start | bytes 294920 | tf_op jit(solution)/shard_map/ppermute | solution.py:560
  53.0 1.3 %collective-permute-start.1 = (f32[3,64,128]{2,1,0:T(8,128)S(1)}, f32[3,64,128]{2,1,0:T(8,128)S(1)}, u32[]{:S(2)}, u32[]{:S(2)}) collective-permute-start(f32[3,64,128]{2,1,0:T(8,128)S(1)} %get-tuple-element.31), channel_id=1, source_target_pairs={{8,0},{9,1},{10,2},{11,3},{12,4},{13,5},{14,6},{15,7},{16,8},{17,9... | collective-permute-start | bytes 294920 | tf_op jit(solution)/shard_map/ppermute | solution.py:560
  54.3 1.8 %collective-permute-start.2 = (f32[3,64,128]{2,1,0:T(8,128)S(1)}, f32[3,64,128]{2,1,0:T(8,128)S(1)}, u32[]{:S(2)}, u32[]{:S(2)}) collective-permute-start(f32[3,64,128]{2,1,0:T(8,128)S(1)} %get-tuple-element.33), channel_id=1, source_target_pairs={{0,1},{1,2},{2,3},{3,4},{4,5},{5,6},{6,7},{8,9},{9,10},{10,11},{11... | collective-permute-start | bytes 294920 | tf_op jit(solution)/shard_map/ppermute | solution.py:560
  56.1 5.9 %collective-permute-start.3 = (f32[3,8,128]{2,1,0:T(8,128)S(1)}, f32[3,8,128]{2,1,0:T(8,128)S(1)}, u32[]{:S(2)}, u32[]{:S(2)}) collective-permute-start(f32[3,8,128]{2,1,0:T(8,128)S(1)} %get-tuple-element.34), channel_id=1, source_target_pairs={{0,9},{1,10},{2,11},{3,12},{4,13},{5,14},{6,15},{8,17},{9,18},{10,... | collective-permute-start | bytes 36872 | tf_op jit(solution)/shard_map/ppermute | solution.py:560
  62.0 0.7 collective-permute-start.4
  62.6 2.7 %base.1 = (f32[3,512,512]{2,1,0:T(8,128)}, f32[8,128]{1,0:T(8,128)S(1)}) custom-call(s32[1]{0:T(128)} %bitcast.refs_0_.rank_ref, s32[1,512]{1,0:T(1,128)S(1)} %bitcast.14, f32[3,512,512]{2,1,0:T(8,128)S(1)} %bitcast.10, f32[3,4,512,128]{3,2,1,0:T(8,128)S(1)} %get-tuple-element.28.force_ref), custom_call_target="tpu_custom_call" | custom-call | bytes 15000000 | tf_op jit(solution)/shard_map/base/pallas_call | solution.py:656
  65.3 5.8 %collective-permute-done.3.cb_ref = f32[3,8,128]{2,1,0:T(8,128)S(1)} collective-permute-done((f32[3,8,128]{2,1,0:T(8,128)S(1)}, f32[3,8,128]{2,1,0:T(8,128)S(1)}, u32[]{:S(2)}, u32[]{:S(2)}) %collective-permute-start.3) | collective-permute-done | bytes 12320 | tf_op jit(solution)/shard_map/ppermute | solution.py:560
  71.1 0.0 collective-permute-done.4.ca_ref
  71.1 0.0 collective-permute-done.below_ref.xb_ref
  71.1 2.3 %collective-permute-done.1.above_ref.xa_ref = f32[3,64,128]{2,1,0:T(8,128)S(1)} collective-permute-done((f32[3,64,128]{2,1,0:T(8,128)S(1)}, f32[3,64,128]{2,1,0:T(8,128)S(1)}, u32[]{:S(2)}, u32[]{:S(2)}) %collective-permute-start.1) | collective-permute-done | bytes 98336 | tf_op jit(solution)/shard_map/ppermute | solution.py:560
  73.3 0.0 collective-permute-done.2.yb_ref
  73.4 0.1 edge.1
  73.4 1.3 %collective-permute-start.5 = (f32[3,64,128]{2,1,0:T(8,128)S(1)}, f32[3,64,128]{2,1,0:T(8,128)S(1)}, u32[]{:S(2)}, u32[]{:S(2)}) collective-permute-start(f32[3,64,128]{2,1,0:T(8,128)S(1)} %get-tuple-element.39), channel_id=1, source_target_pairs={{1,0},{2,1},{3,2},{4,3},{5,4},{6,5},{7,6},{9,8},{10,9},{11,10},{12... | collective-permute-start | bytes 294920 | tf_op jit(solution)/shard_map/ppermute | solution.py:560
  74.7 3.8 %all-to-all-done.1.recv_ref = f32[128,48,128]{2,1,0:T(8,128)} async-done(((f32[128,48,128]{2,1,0:T(8,128)}), f32[128,48,128]{2,1,0:T(8,128)}, u32[]{:S(2)}, u32[]{:S(2)}) %all-to-all-start.1) | async-done | bytes 3145760 | tf_op jit(solution)/shard_map/all_to_all | solution.py:632
  78.5 4.3 %place.1 = (f32[3,512,512]{2,1,0:T(8,128)}, f32[3,64,512]{2,1,0:T(8,128)S(1)}) custom-call(s32[1,256]{1,0:T(1,128)S(1)} %get-tuple-element.25.peers_ref, s32[1,256]{1,0:T(1,128)S(1)} %get-tuple-element.26.slot_ref, f32[128,48,128]{2,1,0:T(8,128)} %all-to-all-done.1.recv_ref, f32[3,512,512]{2,1,0:T(8,128)} %get-tuple-element.29.base_ref, ...), custom_call_target="tpu_custom_call" | custom-call | bytes 9000000 | tf_op jit(solution)/shard_map/place/pallas_call | solution.py:681
  82.8 0.0 collective-permute-done.5.ya_ref
  82.9 1.1 %lines.1 = f32[3,512,512]{2,1,0:T(8,128)} custom-call(f32[3,64,512]{2,1,0:T(8,128)S(1)} %get-tuple-element.38.ends_ref, f32[3,64,128]{2,1,0:T(8,128)S(1)} %collective-permute-done.5.ya_ref, f32[3,512,512]{2,1,0:T(8,128)} %get-tuple-element.40.inner_ref), custom_call_target="tpu_custom_call", output_to_operand_aliasing={{}: (2, {})} | custom-call | bytes 3000000 | tf_op jit(solution)/shard_map/lines/pallas_call | solution.py:706
Async XLA Ops:
  7.7 23.3 %all-to-all-start = ((f32[128,768,1]{1,2,0:T(1,128)}), f32[128,768,1]{1,2,0:T(1,128)S(1)}, u32[]{:S(2)}, u32[]{:S(2)}) async-start(f32[128,768,1]{1,2,0:T(1,128)} %bitcast.18), calls=%async_computation | async-start | bytes 786432 | tf_op jit(solution)/shard_map/all_to_all | solution.py:621
  24.3 12.5 %copy-start = (f32[512,3,512]{2,0,1:T(8,128)S(1)}, f32[512,3,512]{2,0,1:T(8,128)}, u32[]{:S(2)}) copy-start(f32[512,3,512]{2,0,1:T(8,128)} %param.4) | copy-start | bytes 9437188
  24.3 12.5 %copy-start.2 = (s32[512]{0:T(512)S(1)}, s32[512]{0:T(512)}, u32[]{:S(2)}) copy-start(s32[512]{0:T(512)} %param.7) | copy-start | bytes 6148
  24.3 12.5 %copy-start.3 = (s32[512]{0:T(512)S(1)}, s32[512]{0:T(512)}, u32[]{:S(2)}) copy-start(s32[512]{0:T(512)} %param.6) | copy-start | bytes 6148
  31.0 47.5 %all-to-all-start.1 = ((f32[128,48,128]{2,1,0:T(8,128)}), f32[128,48,128]{2,1,0:T(8,128)}, u32[]{:S(2)}, u32[]{:S(2)}) async-start(f32[128,48,128]{2,1,0:T(8,128)} %pack.1), calls=%async_computation.1 | async-start | bytes 6291456 | tf_op jit(solution)/shard_map/all_to_all | solution.py:632
  36.8 1.0 %copy-start.1 = (f32[512,128]{1,0:T(8,128)S(1)}, f32[512,128]{1,0:T(8,128)}, u32[]{:S(2)}) copy-start(f32[512,128]{1,0:T(8,128)} %refs_4_.3) | copy-start | bytes 786436
  50.3 20.8 %collective-permute-start = (f32[3,64,128]{2,1,0:T(8,128)S(1)}, f32[3,64,128]{2,1,0:T(8,128)S(1)}, u32[]{:S(2)}, u32[]{:S(2)}) collective-permute-start(f32[3,64,128]{2,1,0:T(8,128)S(1)} %get-tuple-element.30), channel_id=1, source_target_pairs={{0,8},{1,9},{2,10},{3,11},{4,12},{5,13},{6,14},{7,15},{8,16},{9,17... | collective-permute-start | bytes 294920 | tf_op jit(solution)/shard_map/ppermute | solution.py:560
  53.0 20.4 %collective-permute-start.1 = (f32[3,64,128]{2,1,0:T(8,128)S(1)}, f32[3,64,128]{2,1,0:T(8,128)S(1)}, u32[]{:S(2)}, u32[]{:S(2)}) collective-permute-start(f32[3,64,128]{2,1,0:T(8,128)S(1)} %get-tuple-element.31), channel_id=1, source_target_pairs={{8,0},{9,1},{10,2},{11,3},{12,4},{13,5},{14,6},{15,7},{16,8},{17,9... | collective-permute-start | bytes 294920 | tf_op jit(solution)/shard_map/ppermute | solution.py:560
  54.3 19.1 %collective-permute-start.2 = (f32[3,64,128]{2,1,0:T(8,128)S(1)}, f32[3,64,128]{2,1,0:T(8,128)S(1)}, u32[]{:S(2)}, u32[]{:S(2)}) collective-permute-start(f32[3,64,128]{2,1,0:T(8,128)S(1)} %get-tuple-element.33), channel_id=1, source_target_pairs={{0,1},{1,2},{2,3},{3,4},{4,5},{5,6},{6,7},{8,9},{9,10},{10,11},{11... | collective-permute-start | bytes 294920 | tf_op jit(solution)/shard_map/ppermute | solution.py:560
  56.1 15.0 %collective-permute-start.3 = (f32[3,8,128]{2,1,0:T(8,128)S(1)}, f32[3,8,128]{2,1,0:T(8,128)S(1)}, u32[]{:S(2)}, u32[]{:S(2)}) collective-permute-start(f32[3,8,128]{2,1,0:T(8,128)S(1)} %get-tuple-element.34), channel_id=1, source_target_pairs={{0,9},{1,10},{2,11},{3,12},{4,13},{5,14},{6,15},{8,17},{9,18},{10,... | collective-permute-start | bytes 36872 | tf_op jit(solution)/shard_map/ppermute | solution.py:560
  62.0 9.1 %collective-permute-start.4 = (f32[3,8,128]{2,1,0:T(8,128)S(1)}, f32[3,8,128]{2,1,0:T(8,128)S(1)}, u32[]{:S(2)}, u32[]{:S(2)}) collective-permute-start(f32[3,8,128]{2,1,0:T(8,128)S(1)} %get-tuple-element.35), channel_id=1, source_target_pairs={{8,1},{9,2},{10,3},{11,4},{12,5},{13,6},{14,7},{16,9},{17,10},{18,... | collective-permute-start | bytes 36872 | tf_op jit(solution)/shard_map/ppermute | solution.py:560
  73.4 9.4 %collective-permute-start.5 = (f32[3,64,128]{2,1,0:T(8,128)S(1)}, f32[3,64,128]{2,1,0:T(8,128)S(1)}, u32[]{:S(2)}, u32[]{:S(2)}) collective-permute-start(f32[3,64,128]{2,1,0:T(8,128)S(1)} %get-tuple-element.39), channel_id=1, source_target_pairs={{1,0},{2,1},{3,2},{4,3},{5,4},{6,5},{7,6},{9,8},{10,9},{11,10},{12... | collective-permute-start | bytes 294920 | tf_op jit(solution)/shard_map/ppermute | solution.py:560

commit v6 on v5

--- a/solution.py
+++ b/solution.py
@@ -12,6 +12,9 @@
 SLOTS = 16
 CAP = 4
 PEERS = 64
+N_EX = 16
+N_EY = 8
+ORDER = ("ey", "ex")
 BX = 4
 BY = 8
 BZ = 16
@@ -72,7 +75,8 @@
         same = (key_col == piece) & earlier
         order.append(jnp.sum(same.astype(F32), axis=0, keepdims=True))
     order = jnp.concatenate(order, axis=1).astype(jnp.int32)
-    return jnp.where(moving, target * CAP + order, -1)
+    block = target % N_EY * N_EX + target // N_EY
+    return jnp.where(moving, block * CAP + order, -1)
 
 
 def interleave(first, second):
@@ -618,7 +622,7 @@
     head, stay_slots = interp(
         False, (struct((MOVERS, 2 * LANES), F32), struct((1, MOVERS), jnp.int32)), 40, "staying"
     )
-    recv_head = lax.all_to_all(send_head.reshape(-1), AXES, split_axis=0, concat_axis=0, tiled=True)
+    recv_head = lax.all_to_all(send_head.reshape(-1), ORDER, split_axis=0, concat_axis=0, tiled=True)
     recv_head = recv_head.reshape(devices * HEAD, LANES)
     send = pl.pallas_call(
         pack_kernel,
@@ -629,7 +633,7 @@
         cost_estimate=cost(5),
         name="pack",
     )(position, fields)
-    recv = lax.all_to_all(send, AXES, split_axis=0, concat_axis=0, tiled=True)
+    recv = lax.all_to_all(send, ORDER, split_axis=0, concat_axis=0, tiled=True)
     face = struct((3, 64, LANES), F32)
     corner = struct((3, NP, LANES), F32)
     force, xup, xdn, yup, ydn, left, right, particles_next, slots, peers = pl.pallas_call(

time: 84.5 us -> 83.8 us (level); the launches traced: 84.1 us -> 82.4 us
  waiting for transfers between devices: 18.6 us -> 16.9 us
    all_to_all x2, waiting for transfers between devices: 10.5 us -> 8.04 us  [the longest x1 6.86 us: body(): lax.all_to_all(send_head.reshape(-1), ORDER, split_axis=0, concat_axis=0,...]
where the time goes in v6:
time: 83.8 us; the launch traced here: 82.4 us
  Pallas kernels  33.1 us (39%)
  starting transfers between devices  30.5 us (36%)
  waiting for transfers between devices  16.9 us (20%)
  local copies, waits for them, and re-layouts  0.96 us (1%)
  between operations  0.93 us (1%)
    ppermute x6, starting transfers between devices, passed_along(): return lax.ppermute(x, AXES, pairs)  13.6 us
    pallas_call x2, Pallas kernels, interp(): pl.pallas_call(functools.partial(interp_kernel, moves), out_shape=out_sha...  12.2 us
    all_to_all x1, starting transfers between devices, body(): lax.all_to_all(send_head.reshape(-1), ORDER, split_axis=0, concat_axis=0,...  11.2 us
    ppermute x6, waiting for transfers between devices, passed_along(): return lax.ppermute(x, AXES, pairs)  8.84 us
    pallas_call x1, Pallas kernels, body(): pl.pallas_call(force_kernel, out_shape=(struct((3, tiles, NODES, LANES),...  7.36 us
    all_to_all x1, waiting for transfers between devices, body(): lax.all_to_all(send_head.reshape(-1), ORDER, split_axis=0, concat_axis=0,...  6.86 us
    all_to_all x1, starting transfers between devices, body(): recv = lax.all_to_all(send, ORDER, split_axis=0, concat_axis=0, tiled=True)  5.75 us
    pallas_call x1, Pallas kernels, body(): pl.pallas_call(pack_kernel, out_shape=struct((devices, 3 * COMP, LANES),...  5.38 us
  transfers between devices with their start and end apart: 8, of which 4 were waited for; matrix products, arithmetic and copies ran while one was open for 0% of the time, Pallas kernels for 30%

profile of v6, /device:TPU:0, one launch (start us, length us, event | category | flops | bytes accessed | tf_op | source)
XLA Modules:
  0.0 82.4 jit_solution(12550923225188123045)
XLA Ops:
  0.6 7.1 %moving.1 = (f32[768,128]{1,0:T(8,128)}, s32[1,512]{1,0:T(1,128)}) custom-call(s32[1]{0:T(128)} %bitcast.refs_0_.rank_ref, s32[1,512]{1,0:T(1,128)} %bitcast.12, s32[1,512]{1,0:T(1,128)} %bitcast.15, f32[3,512,512]{2,1,0:T(8,128)} %bitcast.7, f32[512,128]{1,0:T(8,128)} %refs_4_.3), custom_call_target="tpu_custom_call" | custom-call | bytes 18000000 | tf_op jit(solution)/shard_map/moving/pallas_call | solution.py:596
  7.7 11.2 %all-to-all-start = ((f32[128,768,1]{1,2,0:T(1,128)}), f32[128,768,1]{1,2,0:T(1,128)S(1)}, u32[]{:S(2)}, u32[]{:S(2)}) async-start(f32[128,768,1]{1,2,0:T(1,128)} %bitcast.18), calls=%async_computation | async-start | bytes 786432 | tf_op jit(solution)/shard_map/all_to_all | solution.py:625
  18.9 5.4 %pack.1 = f32[128,48,128]{2,1,0:T(8,128)} custom-call(s32[1,512]{1,0:T(1,128)} %get-tuple-element.27.position_ref, f32[3,512,512]{2,1,0:T(8,128)} %bitcast.8), custom_call_target="tpu_custom_call" | custom-call | bytes 15000000 | tf_op jit(solution)/shard_map/pack/pallas_call | solution.py:627
  24.3 0.0 copy-start
  24.3 0.0 copy-start.2
  24.3 0.0 copy-start.3
  24.3 6.9 %all-to-all-done = f32[128,768,1]{1,2,0:T(1,128)S(1)} async-done(((f32[128,768,1]{1,2,0:T(1,128)}), f32[128,768,1]{1,2,0:T(1,128)S(1)}, u32[]{:S(2)}, u32[]{:S(2)}) %all-to-all-start) | async-done | bytes 393248 | tf_op jit(solution)/shard_map/all_to_all | solution.py:625
  31.1 5.7 %all-to-all-start.1 = ((f32[128,48,128]{2,1,0:T(8,128)}), f32[128,48,128]{2,1,0:T(8,128)}, u32[]{:S(2)}, u32[]{:S(2)}) async-start(f32[128,48,128]{2,1,0:T(8,128)} %pack.1), calls=%async_computation.1 | async-start | bytes 6291456 | tf_op jit(solution)/shard_map/all_to_all | solution.py:636
  36.9 0.0 copy-done
  36.9 0.0 copy-done.2
  36.9 0.0 copy-done.3
  36.9 0.0 copy-start.1
  36.9 0.9 %copy-done.1 = f32[512,128]{1,0:T(8,128)S(1)} copy-done((f32[512,128]{1,0:T(8,128)S(1)}, f32[512,128]{1,0:T(8,128)}, u32[]{:S(2)}) %copy-start.1) | copy-done | bytes 262168
  37.9 5.1 %staying.1 = (f32[256,256]{1,0:T(8,128)S(1)}, s32[1,256]{1,0:T(1,128)S(1)}) custom-call(s32[1]{0:T(128)} %bitcast.refs_0_.rank_ref, s32[1,512]{1,0:T(1,128)S(1)} %bitcast.13, s32[1,512]{1,0:T(1,128)S(1)} %bitcast.16, f32[3,512,512]{2,1,0:T(8,128)S(1)} %bitcast.9, f32[512,128]{1,0:T(8,128)S(1)} %copy-done.1), custom_call_target="tpu_custom_call" | custom-call | bytes 18000000 | tf_op jit(solution)/shard_map/staying/pallas_call | solution.py:596
  43.0 7.4 %force.1 = (f32[3,4,512,128]{3,2,1,0:T(8,128)S(1)}, f32[3,64,128]{2,1,0:T(8,128)S(1)}, f32[3,64,128]{2,1,0:T(8,128)S(1)}, f32[3,64,128]{2,1,0:T(8,128)S(1)}, f32...) custom-call(f32[256,256]{1,0:T(8,128)S(1)} %get-tuple-element.22.hea, ...), custom_call_target="tpu_custom_call" | custom-call | bytes 24000000 | tf_op jit(solution)/shard_map/force/pallas_call | solution.py:639
  50.4 2.7 %collective-permute-start = (f32[3,64,128]{2,1,0:T(8,128)S(1)}, f32[3,64,128]{2,1,0:T(8,128)S(1)}, u32[]{:S(2)}, u32[]{:S(2)}) collective-permute-start(f32[3,64,128]{2,1,0:T(8,128)S(1)} %get-tuple-element.30), channel_id=1, source_target_pairs={{0,8},{1,9},{2,10},{3,11},{4,12},{5,13},{6,14},{7,15},{8,16},{9,17... | collective-permute-start | bytes 294920 | tf_op jit(solution)/shard_map/ppermute | solution.py:564
  53.1 1.3 %collective-permute-start.1 = (f32[3,64,128]{2,1,0:T(8,128)S(1)}, f32[3,64,128]{2,1,0:T(8,128)S(1)}, u32[]{:S(2)}, u32[]{:S(2)}) collective-permute-start(f32[3,64,128]{2,1,0:T(8,128)S(1)} %get-tuple-element.31), channel_id=1, source_target_pairs={{8,0},{9,1},{10,2},{11,3},{12,4},{13,5},{14,6},{15,7},{16,8},{17,9... | collective-permute-start | bytes 294920 | tf_op jit(solution)/shard_map/ppermute | solution.py:564
  54.4 1.8 %collective-permute-start.2 = (f32[3,64,128]{2,1,0:T(8,128)S(1)}, f32[3,64,128]{2,1,0:T(8,128)S(1)}, u32[]{:S(2)}, u32[]{:S(2)}) collective-permute-start(f32[3,64,128]{2,1,0:T(8,128)S(1)} %get-tuple-element.33), channel_id=1, source_target_pairs={{0,1},{1,2},{2,3},{3,4},{4,5},{5,6},{6,7},{8,9},{9,10},{10,11},{11... | collective-permute-start | bytes 294920 | tf_op jit(solution)/shard_map/ppermute | solution.py:564
  56.2 5.9 %collective-permute-start.3 = (f32[3,8,128]{2,1,0:T(8,128)S(1)}, f32[3,8,128]{2,1,0:T(8,128)S(1)}, u32[]{:S(2)}, u32[]{:S(2)}) collective-permute-start(f32[3,8,128]{2,1,0:T(8,128)S(1)} %get-tuple-element.34), channel_id=1, source_target_pairs={{0,9},{1,10},{2,11},{3,12},{4,13},{5,14},{6,15},{8,17},{9,18},{10,... | collective-permute-start | bytes 36872 | tf_op jit(solution)/shard_map/ppermute | solution.py:564
  62.1 0.7 collective-permute-start.4
  62.8 2.7 %base.1 = (f32[3,512,512]{2,1,0:T(8,128)}, f32[8,128]{1,0:T(8,128)S(1)}) custom-call(s32[1]{0:T(128)} %bitcast.refs_0_.rank_ref, s32[1,512]{1,0:T(1,128)S(1)} %bitcast.14, f32[3,512,512]{2,1,0:T(8,128)S(1)} %bitcast.10, f32[3,4,512,128]{3,2,1,0:T(8,128)S(1)} %get-tuple-element.28.force_ref), custom_call_target="tpu_custom_call" | custom-call | bytes 15000000 | tf_op jit(solution)/shard_map/base/pallas_call | solution.py:660
  65.4 6.5 %collective-permute-done.3.cb_ref = f32[3,8,128]{2,1,0:T(8,128)S(1)} collective-permute-done((f32[3,8,128]{2,1,0:T(8,128)S(1)}, f32[3,8,128]{2,1,0:T(8,128)S(1)}, u32[]{:S(2)}, u32[]{:S(2)}) %collective-permute-start.3) | collective-permute-done | bytes 12320 | tf_op jit(solution)/shard_map/ppermute | solution.py:564
  71.9 0.0 collective-permute-done.4.ca_ref
  71.9 0.0 collective-permute-done.below_ref.xb_ref
  71.9 2.4 %collective-permute-done.1.above_ref.xa_ref = f32[3,64,128]{2,1,0:T(8,128)S(1)} collective-permute-done((f32[3,64,128]{2,1,0:T(8,128)S(1)}, f32[3,64,128]{2,1,0:T(8,128)S(1)}, u32[]{:S(2)}, u32[]{:S(2)}) %collective-permute-start.1) | collective-permute-done | bytes 98336 | tf_op jit(solution)/shard_map/ppermute | solution.py:564
  74.3 0.0 collective-permute-done.2.yb_ref
  74.3 0.1 edge.1
  74.4 1.3 %collective-permute-start.5 = (f32[3,64,128]{2,1,0:T(8,128)S(1)}, f32[3,64,128]{2,1,0:T(8,128)S(1)}, u32[]{:S(2)}, u32[]{:S(2)}) collective-permute-start(f32[3,64,128]{2,1,0:T(8,128)S(1)} %get-tuple-element.39), channel_id=1, source_target_pairs={{1,0},{2,1},{3,2},{4,3},{5,4},{6,5},{7,6},{9,8},{10,9},{11,10},{12... | collective-permute-start | bytes 294920 | tf_op jit(solution)/shard_map/ppermute | solution.py:564
  75.7 1.2 %all-to-all-done.1.recv_ref = f32[128,48,128]{2,1,0:T(8,128)} async-done(((f32[128,48,128]{2,1,0:T(8,128)}), f32[128,48,128]{2,1,0:T(8,128)}, u32[]{:S(2)}, u32[]{:S(2)}) %all-to-all-start.1) | async-done | bytes 3145760 | tf_op jit(solution)/shard_map/all_to_all | solution.py:636
  76.8 4.3 %place.1 = (f32[3,512,512]{2,1,0:T(8,128)}, f32[3,64,512]{2,1,0:T(8,128)S(1)}) custom-call(s32[1,256]{1,0:T(1,128)S(1)} %get-tuple-element.25.peers_ref, s32[1,256]{1,0:T(1,128)S(1)} %get-tuple-element.26.slot_ref, f32[128,48,128]{2,1,0:T(8,128)} %all-to-all-done.1.recv_ref, f32[3,512,512]{2,1,0:T(8,128)} %get-tuple-element.29.base_ref, ...), custom_call_target="tpu_custom_call" | custom-call | bytes 9000000 | tf_op jit(solution)/shard_map/place/pallas_call | solution.py:685
  81.2 0.0 collective-permute-done.5.ya_ref
  81.2 1.1 %lines.1 = f32[3,512,512]{2,1,0:T(8,128)} custom-call(f32[3,64,512]{2,1,0:T(8,128)S(1)} %get-tuple-element.38.ends_ref, f32[3,64,128]{2,1,0:T(8,128)S(1)} %collective-permute-done.5.ya_ref, f32[3,512,512]{2,1,0:T(8,128)} %get-tuple-element.40.inner_ref), custom_call_target="tpu_custom_call", output_to_operand_aliasing={{}: (2, {})} | custom-call | bytes 3000000 | tf_op jit(solution)/shard_map/lines/pallas_call | solution.py:710
Async XLA Ops:
  7.7 23.4 %all-to-all-start = ((f32[128,768,1]{1,2,0:T(1,128)}), f32[128,768,1]{1,2,0:T(1,128)S(1)}, u32[]{:S(2)}, u32[]{:S(2)}) async-start(f32[128,768,1]{1,2,0:T(1,128)} %bitcast.18), calls=%async_computation | async-start | bytes 786432 | tf_op jit(solution)/shard_map/all_to_all | solution.py:625
  24.3 12.6 %copy-start = (f32[512,3,512]{2,0,1:T(8,128)S(1)}, f32[512,3,512]{2,0,1:T(8,128)}, u32[]{:S(2)}) copy-start(f32[512,3,512]{2,0,1:T(8,128)} %param.4) | copy-start | bytes 9437188
  24.3 12.6 %copy-start.2 = (s32[512]{0:T(512)S(1)}, s32[512]{0:T(512)}, u32[]{:S(2)}) copy-start(s32[512]{0:T(512)} %param.7) | copy-start | bytes 6148
  24.3 12.6 %copy-start.3 = (s32[512]{0:T(512)S(1)}, s32[512]{0:T(512)}, u32[]{:S(2)}) copy-start(s32[512]{0:T(512)} %param.6) | copy-start | bytes 6148
  31.1 45.7 %all-to-all-start.1 = ((f32[128,48,128]{2,1,0:T(8,128)}), f32[128,48,128]{2,1,0:T(8,128)}, u32[]{:S(2)}, u32[]{:S(2)}) async-start(f32[128,48,128]{2,1,0:T(8,128)} %pack.1), calls=%async_computation.1 | async-start | bytes 6291456 | tf_op jit(solution)/shard_map/all_to_all | solution.py:636
  36.9 1.0 %copy-start.1 = (f32[512,128]{1,0:T(8,128)S(1)}, f32[512,128]{1,0:T(8,128)}, u32[]{:S(2)}) copy-start(f32[512,128]{1,0:T(8,128)} %refs_4_.3) | copy-start | bytes 786436
  50.4 21.5 %collective-permute-start = (f32[3,64,128]{2,1,0:T(8,128)S(1)}, f32[3,64,128]{2,1,0:T(8,128)S(1)}, u32[]{:S(2)}, u32[]{:S(2)}) collective-permute-start(f32[3,64,128]{2,1,0:T(8,128)S(1)} %get-tuple-element.30), channel_id=1, source_target_pairs={{0,8},{1,9},{2,10},{3,11},{4,12},{5,13},{6,14},{7,15},{8,16},{9,17... | collective-permute-start | bytes 294920 | tf_op jit(solution)/shard_map/ppermute | solution.py:564
  53.1 21.2 %collective-permute-start.1 = (f32[3,64,128]{2,1,0:T(8,128)S(1)}, f32[3,64,128]{2,1,0:T(8,128)S(1)}, u32[]{:S(2)}, u32[]{:S(2)}) collective-permute-start(f32[3,64,128]{2,1,0:T(8,128)S(1)} %get-tuple-element.31), channel_id=1, source_target_pairs={{8,0},{9,1},{10,2},{11,3},{12,4},{13,5},{14,6},{15,7},{16,8},{17,9... | collective-permute-start | bytes 294920 | tf_op jit(solution)/shard_map/ppermute | solution.py:564
  54.4 19.9 %collective-permute-start.2 = (f32[3,64,128]{2,1,0:T(8,128)S(1)}, f32[3,64,128]{2,1,0:T(8,128)S(1)}, u32[]{:S(2)}, u32[]{:S(2)}) collective-permute-start(f32[3,64,128]{2,1,0:T(8,128)S(1)} %get-tuple-element.33), channel_id=1, source_target_pairs={{0,1},{1,2},{2,3},{3,4},{4,5},{5,6},{6,7},{8,9},{9,10},{10,11},{11... | collective-permute-start | bytes 294920 | tf_op jit(solution)/shard_map/ppermute | solution.py:564
  56.2 15.7 %collective-permute-start.3 = (f32[3,8,128]{2,1,0:T(8,128)S(1)}, f32[3,8,128]{2,1,0:T(8,128)S(1)}, u32[]{:S(2)}, u32[]{:S(2)}) collective-permute-start(f32[3,8,128]{2,1,0:T(8,128)S(1)} %get-tuple-element.34), channel_id=1, source_target_pairs={{0,9},{1,10},{2,11},{3,12},{4,13},{5,14},{6,15},{8,17},{9,18},{10,... | collective-permute-start | bytes 36872 | tf_op jit(solution)/shard_map/ppermute | solution.py:564
  62.1 9.8 %collective-permute-start.4 = (f32[3,8,128]{2,1,0:T(8,128)S(1)}, f32[3,8,128]{2,1,0:T(8,128)S(1)}, u32[]{:S(2)}, u32[]{:S(2)}) collective-permute-start(f32[3,8,128]{2,1,0:T(8,128)S(1)} %get-tuple-element.35), channel_id=1, source_target_pairs={{8,1},{9,2},{10,3},{11,4},{12,5},{13,6},{14,7},{16,9},{17,10},{18,... | collective-permute-start | bytes 36872 | tf_op jit(solution)/shard_map/ppermute | solution.py:564
  74.4 6.8 %collective-permute-start.5 = (f32[3,64,128]{2,1,0:T(8,128)S(1)}, f32[3,64,128]{2,1,0:T(8,128)S(1)}, u32[]{:S(2)}, u32[]{:S(2)}) collective-permute-start(f32[3,64,128]{2,1,0:T(8,128)S(1)} %get-tuple-element.39), channel_id=1, source_target_pairs={{1,0},{2,1},{3,2},{4,3},{5,4},{6,5},{7,6},{9,8},{10,9},{11,10},{12... | collective-permute-start | bytes 294920 | tf_op jit(solution)/shard_map/ppermute | solution.py:564

commit v7 on v6

--- a/solution.py
+++ b/solution.py
@@ -14,7 +14,9 @@
 PEERS = 64
 N_EX = 16
 N_EY = 8
-ORDER = ("ey", "ex")
+STEP = 37
+BACK = 45
+ORDER = [[k * BACK % (N_EX * N_EY) for k in range(N_EX * N_EY)]]
 BX = 4
 BY = 8
 BZ = 16
@@ -75,7 +77,7 @@
         same = (key_col == piece) & earlier
         order.append(jnp.sum(same.astype(F32), axis=0, keepdims=True))
     order = jnp.concatenate(order, axis=1).astype(jnp.int32)
-    block = target % N_EY * N_EX + target // N_EY
+    block = target * STEP % (N_EX * N_EY)
     return jnp.where(moving, block * CAP + order, -1)
 
 
@@ -622,7 +624,7 @@
     head, stay_slots = interp(
         False, (struct((MOVERS, 2 * LANES), F32), struct((1, MOVERS), jnp.int32)), 40, "staying"
     )
-    recv_head = lax.all_to_all(send_head.reshape(-1), ORDER, split_axis=0, concat_axis=0, tiled=True)
+    recv_head = lax.all_to_all(send_head.reshape(-1), AXES, split_axis=0, concat_axis=0, tiled=True, axis_index_groups=ORDER)
     recv_head = recv_head.reshape(devices * HEAD, LANES)
     send = pl.pallas_call(
         pack_kernel,
@@ -633,7 +635,7 @@
         cost_estimate=cost(5),
         name="pack",
     )(position, fields)
-    recv = lax.all_to_all(send, ORDER, split_axis=0, concat_axis=0, tiled=True)
+    recv = lax.all_to_all(send, AXES, split_axis=0, concat_axis=0, tiled=True, axis_index_groups=ORDER)
     face = struct((3, 64, LANES), F32)
     corner = struct((3, NP, LANES), F32)
     force, xup, xdn, yup, ydn, left, right, particles_next, slots, peers = pl.pallas_call(

time: 83.8 us -> 83.7 us (level); the launches traced: 82.4 us -> 83.3 us
  waiting for transfers between devices: 16.9 us -> 17.8 us
    all_to_all x2, waiting for transfers between devices: 8.04 us -> 10.5 us  [the longest x1 6.89 us: body(): lax.all_to_all(send_head.reshape(-1), AXES, split_axis=0, concat_axis=0,...]
    ppermute x6, waiting for transfers between devices: 8.84 us -> 7.23 us  [passed_along(): return lax.ppermute(x, AXES, pairs)]
where the time goes in v7:
time: 83.7 us; the launch traced here: 83.3 us
  Pallas kernels  33.1 us (40%)
  starting transfers between devices  30.5 us (36%)
  waiting for transfers between devices  17.8 us (21%)
  local copies, waits for them, and re-layouts  0.96 us (1%)
  between operations  0.93 us (1%)
    ppermute x6, starting transfers between devices, passed_along(): return lax.ppermute(x, AXES, pairs)  13.6 us
    pallas_call x2, Pallas kernels, interp(): pl.pallas_call(functools.partial(interp_kernel, moves), out_shape=out_sha...  12.2 us
    all_to_all x1, starting transfers between devices, body(): lax.all_to_all(send_head.reshape(-1), AXES, split_axis=0, concat_axis=0,...  11.2 us
    pallas_call x1, Pallas kernels, body(): pl.pallas_call(force_kernel, out_shape=(struct((3, tiles, NODES, LANES),...  7.36 us
    ppermute x6, waiting for transfers between devices, passed_along(): return lax.ppermute(x, AXES, pairs)  7.23 us
    all_to_all x1, waiting for transfers between devices, body(): lax.all_to_all(send_head.reshape(-1), AXES, split_axis=0, concat_axis=0,...  6.89 us
    all_to_all x1, starting transfers between devices, body(): lax.all_to_all(send, AXES, split_axis=0, concat_axis=0, tiled=True, axis_...  5.75 us
    pallas_call x1, Pallas kernels, body(): pl.pallas_call(pack_kernel, out_shape=struct((devices, 3 * COMP, LANES),...  5.38 us
  transfers between devices with their start and end apart: 8, of which 4 were waited for; matrix products, arithmetic and copies ran while one was open for 0% of the time, Pallas kernels for 30%

profile of v7, /device:TPU:0, one launch (start us, length us, event | category | flops | bytes accessed | tf_op | source)
XLA Modules:
  0.0 83.3 jit_solution(18179707966420328816)
XLA Ops:
  0.6 7.1 %moving.1 = (f32[768,128]{1,0:T(8,128)}, s32[1,512]{1,0:T(1,128)}) custom-call(s32[1]{0:T(128)} %bitcast.refs_0_.rank_ref, s32[1,512]{1,0:T(1,128)} %bitcast.12, s32[1,512]{1,0:T(1,128)} %bitcast.15, f32[3,512,512]{2,1,0:T(8,128)} %bitcast.7, f32[512,128]{1,0:T(8,128)} %refs_4_.3), custom_call_target="tpu_custom_call" | custom-call | bytes 18000000 | tf_op jit(solution)/shard_map/moving/pallas_call | solution.py:598
  7.7 11.2 %all-to-all-start = ((f32[128,768,1]{1,2,0:T(1,128)}), f32[128,768,1]{1,2,0:T(1,128)S(1)}, u32[]{:S(2)}, u32[]{:S(2)}) async-start(f32[128,768,1]{1,2,0:T(1,128)} %bitcast.18), calls=%async_computation | async-start | bytes 786432 | tf_op jit(solution)/shard_map/all_to_all | solution.py:627
  18.9 5.4 %pack.1 = f32[128,48,128]{2,1,0:T(8,128)} custom-call(s32[1,512]{1,0:T(1,128)} %get-tuple-element.27.position_ref, f32[3,512,512]{2,1,0:T(8,128)} %bitcast.8), custom_call_target="tpu_custom_call" | custom-call | bytes 15000000 | tf_op jit(solution)/shard_map/pack/pallas_call | solution.py:629
  24.3 0.0 copy-start
  24.3 0.0 copy-start.2
  24.3 0.0 copy-start.3
  24.3 6.9 %all-to-all-done = f32[128,768,1]{1,2,0:T(1,128)S(1)} async-done(((f32[128,768,1]{1,2,0:T(1,128)}), f32[128,768,1]{1,2,0:T(1,128)S(1)}, u32[]{:S(2)}, u32[]{:S(2)}) %all-to-all-start) | async-done | bytes 393248 | tf_op jit(solution)/shard_map/all_to_all | solution.py:627
  31.2 5.7 %all-to-all-start.1 = ((f32[128,48,128]{2,1,0:T(8,128)}), f32[128,48,128]{2,1,0:T(8,128)}, u32[]{:S(2)}, u32[]{:S(2)}) async-start(f32[128,48,128]{2,1,0:T(8,128)} %pack.1), calls=%async_computation.1 | async-start | bytes 6291456 | tf_op jit(solution)/shard_map/all_to_all | solution.py:638
  36.9 0.0 copy-done
  36.9 0.0 copy-done.2
  37.0 0.0 copy-done.3
  37.0 0.0 copy-start.1
  37.0 0.9 %copy-done.1 = f32[512,128]{1,0:T(8,128)S(1)} copy-done((f32[512,128]{1,0:T(8,128)S(1)}, f32[512,128]{1,0:T(8,128)}, u32[]{:S(2)}) %copy-start.1) | copy-done | bytes 262168
  37.9 5.1 %staying.1 = (f32[256,256]{1,0:T(8,128)S(1)}, s32[1,256]{1,0:T(1,128)S(1)}) custom-call(s32[1]{0:T(128)} %bitcast.refs_0_.rank_ref, s32[1,512]{1,0:T(1,128)S(1)} %bitcast.13, s32[1,512]{1,0:T(1,128)S(1)} %bitcast.16, f32[3,512,512]{2,1,0:T(8,128)S(1)} %bitcast.9, f32[512,128]{1,0:T(8,128)S(1)} %copy-done.1), custom_call_target="tpu_custom_call" | custom-call | bytes 18000000 | tf_op jit(solution)/shard_map/staying/pallas_call | solution.py:598
  43.1 7.4 %force.1 = (f32[3,4,512,128]{3,2,1,0:T(8,128)S(1)}, f32[3,64,128]{2,1,0:T(8,128)S(1)}, f32[3,64,128]{2,1,0:T(8,128)S(1)}, f32[3,64,128]{2,1,0:T(8,128)S(1)}, f32...) custom-call(f32[256,256]{1,0:T(8,128)S(1)} %get-tuple-element.22.hea, ...), custom_call_target="tpu_custom_call" | custom-call | bytes 24000000 | tf_op jit(solution)/shard_map/force/pallas_call | solution.py:641
  50.4 2.7 %collective-permute-start = (f32[3,64,128]{2,1,0:T(8,128)S(1)}, f32[3,64,128]{2,1,0:T(8,128)S(1)}, u32[]{:S(2)}, u32[]{:S(2)}) collective-permute-start(f32[3,64,128]{2,1,0:T(8,128)S(1)} %get-tuple-element.30), channel_id=1, source_target_pairs={{0,8},{1,9},{2,10},{3,11},{4,12},{5,13},{6,14},{7,15},{8,16},{9,17... | collective-permute-start | bytes 294920 | tf_op jit(solution)/shard_map/ppermute | solution.py:566
  53.1 1.3 %collective-permute-start.1 = (f32[3,64,128]{2,1,0:T(8,128)S(1)}, f32[3,64,128]{2,1,0:T(8,128)S(1)}, u32[]{:S(2)}, u32[]{:S(2)}) collective-permute-start(f32[3,64,128]{2,1,0:T(8,128)S(1)} %get-tuple-element.31), channel_id=1, source_target_pairs={{8,0},{9,1},{10,2},{11,3},{12,4},{13,5},{14,6},{15,7},{16,8},{17,9... | collective-permute-start | bytes 294920 | tf_op jit(solution)/shard_map/ppermute | solution.py:566
  54.4 1.8 %collective-permute-start.2 = (f32[3,64,128]{2,1,0:T(8,128)S(1)}, f32[3,64,128]{2,1,0:T(8,128)S(1)}, u32[]{:S(2)}, u32[]{:S(2)}) collective-permute-start(f32[3,64,128]{2,1,0:T(8,128)S(1)} %get-tuple-element.33), channel_id=1, source_target_pairs={{0,1},{1,2},{2,3},{3,4},{4,5},{5,6},{6,7},{8,9},{9,10},{10,11},{11... | collective-permute-start | bytes 294920 | tf_op jit(solution)/shard_map/ppermute | solution.py:566
  56.2 5.9 %collective-permute-start.3 = (f32[3,8,128]{2,1,0:T(8,128)S(1)}, f32[3,8,128]{2,1,0:T(8,128)S(1)}, u32[]{:S(2)}, u32[]{:S(2)}) collective-permute-start(f32[3,8,128]{2,1,0:T(8,128)S(1)} %get-tuple-element.34), channel_id=1, source_target_pairs={{0,9},{1,10},{2,11},{3,12},{4,13},{5,14},{6,15},{8,17},{9,18},{10,... | collective-permute-start | bytes 36872 | tf_op jit(solution)/shard_map/ppermute | solution.py:566
  62.1 0.7 collective-permute-start.4
  62.8 2.7 %base.1 = (f32[3,512,512]{2,1,0:T(8,128)}, f32[8,128]{1,0:T(8,128)S(1)}) custom-call(s32[1]{0:T(128)} %bitcast.refs_0_.rank_ref, s32[1,512]{1,0:T(1,128)S(1)} %bitcast.14, f32[3,512,512]{2,1,0:T(8,128)S(1)} %bitcast.10, f32[3,4,512,128]{3,2,1,0:T(8,128)S(1)} %get-tuple-element.28.force_ref), custom_call_target="tpu_custom_call" | custom-call | bytes 15000000 | tf_op jit(solution)/shard_map/base/pallas_call | solution.py:662
  65.5 6.0 %collective-permute-done.3.cb_ref = f32[3,8,128]{2,1,0:T(8,128)S(1)} collective-permute-done((f32[3,8,128]{2,1,0:T(8,128)S(1)}, f32[3,8,128]{2,1,0:T(8,128)S(1)}, u32[]{:S(2)}, u32[]{:S(2)}) %collective-permute-start.3) | collective-permute-done | bytes 12320 | tf_op jit(solution)/shard_map/ppermute | solution.py:566
  71.5 0.0 collective-permute-done.4.ca_ref
  71.5 0.0 collective-permute-done.below_ref.xb_ref
  71.5 1.2 %collective-permute-done.1.above_ref.xa_ref = f32[3,64,128]{2,1,0:T(8,128)S(1)} collective-permute-done((f32[3,64,128]{2,1,0:T(8,128)S(1)}, f32[3,64,128]{2,1,0:T(8,128)S(1)}, u32[]{:S(2)}, u32[]{:S(2)}) %collective-permute-start.1) | collective-permute-done | bytes 98336 | tf_op jit(solution)/shard_map/ppermute | solution.py:566
  72.7 0.0 collective-permute-done.2.yb_ref
  72.7 0.1 edge.1
  72.8 1.3 %collective-permute-start.5 = (f32[3,64,128]{2,1,0:T(8,128)S(1)}, f32[3,64,128]{2,1,0:T(8,128)S(1)}, u32[]{:S(2)}, u32[]{:S(2)}) collective-permute-start(f32[3,64,128]{2,1,0:T(8,128)S(1)} %get-tuple-element.39), channel_id=1, source_target_pairs={{1,0},{2,1},{3,2},{4,3},{5,4},{6,5},{7,6},{9,8},{10,9},{11,10},{12... | collective-permute-start | bytes 294920 | tf_op jit(solution)/shard_map/ppermute | solution.py:566
  74.1 3.7 %all-to-all-done.1.recv_ref = f32[128,48,128]{2,1,0:T(8,128)} async-done(((f32[128,48,128]{2,1,0:T(8,128)}), f32[128,48,128]{2,1,0:T(8,128)}, u32[]{:S(2)}, u32[]{:S(2)}) %all-to-all-start.1) | async-done | bytes 3145760 | tf_op jit(solution)/shard_map/all_to_all | solution.py:638
  77.7 4.3 %place.1 = (f32[3,512,512]{2,1,0:T(8,128)}, f32[3,64,512]{2,1,0:T(8,128)S(1)}) custom-call(s32[1,256]{1,0:T(1,128)S(1)} %get-tuple-element.25.peers_ref, s32[1,256]{1,0:T(1,128)S(1)} %get-tuple-element.26.slot_ref, f32[128,48,128]{2,1,0:T(8,128)} %all-to-all-done.1.recv_ref, f32[3,512,512]{2,1,0:T(8,128)} %get-tuple-element.29.base_ref, ...), custom_call_target="tpu_custom_call" | custom-call | bytes 9000000 | tf_op jit(solution)/shard_map/place/pallas_call | solution.py:687
  82.0 0.0 collective-permute-done.5.ya_ref
  82.1 1.1 %lines.1 = f32[3,512,512]{2,1,0:T(8,128)} custom-call(f32[3,64,512]{2,1,0:T(8,128)S(1)} %get-tuple-element.38.ends_ref, f32[3,64,128]{2,1,0:T(8,128)S(1)} %collective-permute-done.5.ya_ref, f32[3,512,512]{2,1,0:T(8,128)} %get-tuple-element.40.inner_ref), custom_call_target="tpu_custom_call", output_to_operand_aliasing={{}: (2, {})} | custom-call | bytes 3000000 | tf_op jit(solution)/shard_map/lines/pallas_call | solution.py:712
Async XLA Ops:
  7.7 23.4 %all-to-all-start = ((f32[128,768,1]{1,2,0:T(1,128)}), f32[128,768,1]{1,2,0:T(1,128)S(1)}, u32[]{:S(2)}, u32[]{:S(2)}) async-start(f32[128,768,1]{1,2,0:T(1,128)} %bitcast.18), calls=%async_computation | async-start | bytes 786432 | tf_op jit(solution)/shard_map/all_to_all | solution.py:627
  24.3 12.7 %copy-start = (f32[512,3,512]{2,0,1:T(8,128)S(1)}, f32[512,3,512]{2,0,1:T(8,128)}, u32[]{:S(2)}) copy-start(f32[512,3,512]{2,0,1:T(8,128)} %param.4) | copy-start | bytes 9437188
  24.3 12.7 %copy-start.2 = (s32[512]{0:T(512)S(1)}, s32[512]{0:T(512)}, u32[]{:S(2)}) copy-start(s32[512]{0:T(512)} %param.7) | copy-start | bytes 6148
  24.3 12.7 %copy-start.3 = (s32[512]{0:T(512)S(1)}, s32[512]{0:T(512)}, u32[]{:S(2)}) copy-start(s32[512]{0:T(512)} %param.6) | copy-start | bytes 6148
  31.2 46.5 %all-to-all-start.1 = ((f32[128,48,128]{2,1,0:T(8,128)}), f32[128,48,128]{2,1,0:T(8,128)}, u32[]{:S(2)}, u32[]{:S(2)}) async-start(f32[128,48,128]{2,1,0:T(8,128)} %pack.1), calls=%async_computation.1 | async-start | bytes 6291456 | tf_op jit(solution)/shard_map/all_to_all | solution.py:638
  37.0 1.0 %copy-start.1 = (f32[512,128]{1,0:T(8,128)S(1)}, f32[512,128]{1,0:T(8,128)}, u32[]{:S(2)}) copy-start(f32[512,128]{1,0:T(8,128)} %refs_4_.3) | copy-start | bytes 786436
  50.4 21.1 %collective-permute-start = (f32[3,64,128]{2,1,0:T(8,128)S(1)}, f32[3,64,128]{2,1,0:T(8,128)S(1)}, u32[]{:S(2)}, u32[]{:S(2)}) collective-permute-start(f32[3,64,128]{2,1,0:T(8,128)S(1)} %get-tuple-element.30), channel_id=1, source_target_pairs={{0,8},{1,9},{2,10},{3,11},{4,12},{5,13},{6,14},{7,15},{8,16},{9,17... | collective-permute-start | bytes 294920 | tf_op jit(solution)/shard_map/ppermute | solution.py:566
  53.1 19.6 %collective-permute-start.1 = (f32[3,64,128]{2,1,0:T(8,128)S(1)}, f32[3,64,128]{2,1,0:T(8,128)S(1)}, u32[]{:S(2)}, u32[]{:S(2)}) collective-permute-start(f32[3,64,128]{2,1,0:T(8,128)S(1)} %get-tuple-element.31), channel_id=1, source_target_pairs={{8,0},{9,1},{10,2},{11,3},{12,4},{13,5},{14,6},{15,7},{16,8},{17,9... | collective-permute-start | bytes 294920 | tf_op jit(solution)/shard_map/ppermute | solution.py:566
  54.4 18.3 %collective-permute-start.2 = (f32[3,64,128]{2,1,0:T(8,128)S(1)}, f32[3,64,128]{2,1,0:T(8,128)S(1)}, u32[]{:S(2)}, u32[]{:S(2)}) collective-permute-start(f32[3,64,128]{2,1,0:T(8,128)S(1)} %get-tuple-element.33), channel_id=1, source_target_pairs={{0,1},{1,2},{2,3},{3,4},{4,5},{5,6},{6,7},{8,9},{9,10},{10,11},{11... | collective-permute-start | bytes 294920 | tf_op jit(solution)/shard_map/ppermute | solution.py:566
  56.2 15.2 %collective-permute-start.3 = (f32[3,8,128]{2,1,0:T(8,128)S(1)}, f32[3,8,128]{2,1,0:T(8,128)S(1)}, u32[]{:S(2)}, u32[]{:S(2)}) collective-permute-start(f32[3,8,128]{2,1,0:T(8,128)S(1)} %get-tuple-element.34), channel_id=1, source_target_pairs={{0,9},{1,10},{2,11},{3,12},{4,13},{5,14},{6,15},{8,17},{9,18},{10,... | collective-permute-start | bytes 36872 | tf_op jit(solution)/shard_map/ppermute | solution.py:566
  62.1 9.4 %collective-permute-start.4 = (f32[3,8,128]{2,1,0:T(8,128)S(1)}, f32[3,8,128]{2,1,0:T(8,128)S(1)}, u32[]{:S(2)}, u32[]{:S(2)}) collective-permute-start(f32[3,8,128]{2,1,0:T(8,128)S(1)} %get-tuple-element.35), channel_id=1, source_target_pairs={{8,1},{9,2},{10,3},{11,4},{12,5},{13,6},{14,7},{16,9},{17,10},{18,... | collective-permute-start | bytes 36872 | tf_op jit(solution)/shard_map/ppermute | solution.py:566
  72.8 9.3 %collective-permute-start.5 = (f32[3,64,128]{2,1,0:T(8,128)S(1)}, f32[3,64,128]{2,1,0:T(8,128)S(1)}, u32[]{:S(2)}, u32[]{:S(2)}) collective-permute-start(f32[3,64,128]{2,1,0:T(8,128)S(1)} %get-tuple-element.39), channel_id=1, source_target_pairs={{1,0},{2,1},{3,2},{4,3},{5,4},{6,5},{7,6},{9,8},{10,9},{11,10},{12... | collective-permute-start | bytes 294920 | tf_op jit(solution)/shard_map/ppermute | solution.py:566

commit v8 on v6

--- a/solution.py
+++ b/solution.py
@@ -111,7 +111,8 @@
     rank_ref, place_ref, count_ref, fields_ref, part_ref = refs[:5]
     out_refs = refs[5:7]
     tp_ref, push_ref, basis_ref, t_ref, work_ref, count_row_ref, held_ref = refs[7:14]
-    place_held, count_held, part_held, arrived = refs[14:]
+    place_held, count_held, part_held, arrived = refs[14:18]
+    node_refs = refs[18:]
     tiles = MOVERS // LANES
     pairs = [(place_ref, place_held), (count_ref, count_held), (part_ref, part_held)]
     pairs += [(fields_ref.at[f], held_ref.at[f]) for f in range(3)]
@@ -159,7 +160,7 @@
         for t in range(tiles):
             for j in range(NODES // LANES):
                 cols = slice(j * LANES, (j + 1) * LANES)
-                t_ref[f, t, cols, :] = rows[t * LANES : (t + 1) * LANES, cols].T
+                node_refs[f][t, cols, :] = rows[t * LANES : (t + 1) * LANES, cols].T
 
     for t in range(tiles):
         make_basis(t, 0)
@@ -172,7 +173,7 @@
         total = [None] * SLOTS
         for pair in range(NP // 2):
             nodes = [
-                [t_ref[f, t, pl.ds(a * 64 + (2 * pair + i) * 8, 8), :] for a in range(NP)]
+                [node_refs[f][t, pl.ds(a * 64 + (2 * pair + i) * 8, 8), :] for a in range(NP)]
                 for i in range(2)
             ]
             for p in range(SLOTS):
@@ -202,9 +203,10 @@
         return f
 
     for f in range(3):
-        if f:
-            gather(f)
-        lax.fori_loop(0, tiles, step, f)
+        step(0, f)
+        if f < 2:
+            gather(f + 1)
+        step(1, f)
 
     heads = []
     for t in range(tiles):
@@ -610,7 +612,8 @@
                 pltpu.VMEM((1, EL), jnp.int32),
                 pltpu.VMEM((EL, PARTS), F32),
                 pltpu.SemaphoreType.DMA((6,)),
-            ],
+            ]
+            + [pltpu.VMEM((half, NODES, LANES), F32)] * 3,
             compiler_params=params(mib),
             cost_estimate=cost(6),
             name=name,

time: 83.8 us -> 83.8 us (level)
  no operation moved by 1% of the time
where the time goes in v8:
time: 83.8 us; the launch traced here: 82.4 us
  Pallas kernels  33.1 us (39%)
  starting transfers between devices  30.5 us (36%)
  waiting for transfers between devices  16.9 us (20%)
  local copies, waits for them, and re-layouts  0.96 us (1%)
  between operations  0.93 us (1%)
    ppermute x6, starting transfers between devices, passed_along(): return lax.ppermute(x, AXES, pairs)  13.4 us
    pallas_call x2, Pallas kernels, interp(): pl.pallas_call(functools.partial(interp_kernel, moves), out_shape=out_sha...  12.2 us
    all_to_all x1, starting transfers between devices, body(): lax.all_to_all(send_head.reshape(-1), ORDER, split_axis=0, concat_axis=0,...  11.1 us
    ppermute x6, waiting for transfers between devices, passed_along(): return lax.ppermute(x, AXES, pairs)  8.82 us
    pallas_call x1, Pallas kernels, body(): pl.pallas_call(force_kernel, out_shape=(struct((3, tiles, NODES, LANES),...  7.36 us
    all_to_all x1, waiting for transfers between devices, body(): lax.all_to_all(send_head.reshape(-1), ORDER, split_axis=0, concat_axis=0,...  6.86 us
    all_to_all x1, starting transfers between devices, body(): recv = lax.all_to_all(send, ORDER, split_axis=0, concat_axis=0, tiled=True)  5.93 us
    pallas_call x1, Pallas kernels, body(): pl.pallas_call(pack_kernel, out_shape=struct((devices, 3 * COMP, LANES),...  5.38 us
  transfers between devices with their start and end apart: 8, of which 4 were waited for; matrix products, arithmetic and copies ran while one was open for 0% of the time, Pallas kernels for 30%

profile of v8, /device:TPU:0, one launch (start us, length us, event | category | flops | bytes accessed | tf_op | source)
XLA Modules:
  0.0 82.4 jit_solution(2769143985633549662)
XLA Ops:
  0.6 7.1 %moving.1 = (f32[768,128]{1,0:T(8,128)}, s32[1,512]{1,0:T(1,128)}) custom-call(s32[1]{0:T(128)} %bitcast.refs_0_.rank_ref, s32[1,512]{1,0:T(1,128)} %bitcast.12, s32[1,512]{1,0:T(1,128)} %bitcast.15, f32[3,512,512]{2,1,0:T(8,128)} %bitcast.7, f32[512,128]{1,0:T(8,128)} %refs_4_.3), custom_call_target="tpu_custom_call" | custom-call | bytes 18000000 | tf_op jit(solution)/shard_map/moving/pallas_call | solution.py:598
  7.7 11.1 %all-to-all-start = ((f32[128,768,1]{1,2,0:T(1,128)}), f32[128,768,1]{1,2,0:T(1,128)S(1)}, u32[]{:S(2)}, u32[]{:S(2)}) async-start(f32[128,768,1]{1,2,0:T(1,128)} %bitcast.18), calls=%async_computation | async-start | bytes 786432 | tf_op jit(solution)/shard_map/all_to_all | solution.py:628
  18.9 5.4 %pack.1 = f32[128,48,128]{2,1,0:T(8,128)} custom-call(s32[1,512]{1,0:T(1,128)} %get-tuple-element.27.position_ref, f32[3,512,512]{2,1,0:T(8,128)} %bitcast.8), custom_call_target="tpu_custom_call" | custom-call | bytes 15000000 | tf_op jit(solution)/shard_map/pack/pallas_call | solution.py:630
  24.2 0.0 copy-start
  24.3 0.0 copy-start.2
  24.3 0.0 copy-start.3
  24.3 6.9 %all-to-all-done = f32[128,768,1]{1,2,0:T(1,128)S(1)} async-done(((f32[128,768,1]{1,2,0:T(1,128)}), f32[128,768,1]{1,2,0:T(1,128)S(1)}, u32[]{:S(2)}, u32[]{:S(2)}) %all-to-all-start) | async-done | bytes 393248 | tf_op jit(solution)/shard_map/all_to_all | solution.py:628
  31.1 5.9 %all-to-all-start.1 = ((f32[128,48,128]{2,1,0:T(8,128)}), f32[128,48,128]{2,1,0:T(8,128)}, u32[]{:S(2)}, u32[]{:S(2)}) async-start(f32[128,48,128]{2,1,0:T(8,128)} %pack.1), calls=%async_computation.1 | async-start | bytes 6291456 | tf_op jit(solution)/shard_map/all_to_all | solution.py:639
  37.1 0.0 copy-done
  37.1 0.0 copy-done.2
  37.1 0.0 copy-done.3
  37.1 0.0 copy-start.1
  37.1 0.9 %copy-done.1 = f32[512,128]{1,0:T(8,128)S(1)} copy-done((f32[512,128]{1,0:T(8,128)S(1)}, f32[512,128]{1,0:T(8,128)}, u32[]{:S(2)}) %copy-start.1) | copy-done | bytes 262168
  38.0 5.1 %staying.1 = (f32[256,256]{1,0:T(8,128)S(1)}, s32[1,256]{1,0:T(1,128)S(1)}) custom-call(s32[1]{0:T(128)} %bitcast.refs_0_.rank_ref, s32[1,512]{1,0:T(1,128)S(1)} %bitcast.13, s32[1,512]{1,0:T(1,128)S(1)} %bitcast.16, f32[3,512,512]{2,1,0:T(8,128)S(1)} %bitcast.9, f32[512,128]{1,0:T(8,128)S(1)} %copy-done.1), custom_call_target="tpu_custom_call" | custom-call | bytes 18000000 | tf_op jit(solution)/shard_map/staying/pallas_call | solution.py:598
  43.2 7.4 %force.1 = (f32[3,4,512,128]{3,2,1,0:T(8,128)S(1)}, f32[3,64,128]{2,1,0:T(8,128)S(1)}, f32[3,64,128]{2,1,0:T(8,128)S(1)}, f32[3,64,128]{2,1,0:T(8,128)S(1)}, f32...) custom-call(f32[256,256]{1,0:T(8,128)S(1)} %get-tuple-element.22.hea, ...), custom_call_target="tpu_custom_call" | custom-call | bytes 24000000 | tf_op jit(solution)/shard_map/force/pallas_call | solution.py:642
  50.5 2.5 %collective-permute-start = (f32[3,64,128]{2,1,0:T(8,128)S(1)}, f32[3,64,128]{2,1,0:T(8,128)S(1)}, u32[]{:S(2)}, u32[]{:S(2)}) collective-permute-start(f32[3,64,128]{2,1,0:T(8,128)S(1)} %get-tuple-element.30), channel_id=1, source_target_pairs={{0,8},{1,9},{2,10},{3,11},{4,12},{5,13},{6,14},{7,15},{8,16},{9,17... | collective-permute-start | bytes 294920 | tf_op jit(solution)/shard_map/ppermute | solution.py:566
  53.1 1.3 %collective-permute-start.1 = (f32[3,64,128]{2,1,0:T(8,128)S(1)}, f32[3,64,128]{2,1,0:T(8,128)S(1)}, u32[]{:S(2)}, u32[]{:S(2)}) collective-permute-start(f32[3,64,128]{2,1,0:T(8,128)S(1)} %get-tuple-element.31), channel_id=1, source_target_pairs={{8,0},{9,1},{10,2},{11,3},{12,4},{13,5},{14,6},{15,7},{16,8},{17,9... | collective-permute-start | bytes 294920 | tf_op jit(solution)/shard_map/ppermute | solution.py:566
  54.4 1.8 %collective-permute-start.2 = (f32[3,64,128]{2,1,0:T(8,128)S(1)}, f32[3,64,128]{2,1,0:T(8,128)S(1)}, u32[]{:S(2)}, u32[]{:S(2)}) collective-permute-start(f32[3,64,128]{2,1,0:T(8,128)S(1)} %get-tuple-element.33), channel_id=1, source_target_pairs={{0,1},{1,2},{2,3},{3,4},{4,5},{5,6},{6,7},{8,9},{9,10},{10,11},{11... | collective-permute-start | bytes 294920 | tf_op jit(solution)/shard_map/ppermute | solution.py:566
  56.2 5.9 %collective-permute-start.3 = (f32[3,8,128]{2,1,0:T(8,128)S(1)}, f32[3,8,128]{2,1,0:T(8,128)S(1)}, u32[]{:S(2)}, u32[]{:S(2)}) collective-permute-start(f32[3,8,128]{2,1,0:T(8,128)S(1)} %get-tuple-element.34), channel_id=1, source_target_pairs={{0,9},{1,10},{2,11},{3,12},{4,13},{5,14},{6,15},{8,17},{9,18},{10,... | collective-permute-start | bytes 36872 | tf_op jit(solution)/shard_map/ppermute | solution.py:566
  62.1 0.7 collective-permute-start.4
  62.7 2.7 %base.1 = (f32[3,512,512]{2,1,0:T(8,128)}, f32[8,128]{1,0:T(8,128)S(1)}) custom-call(s32[1]{0:T(128)} %bitcast.refs_0_.rank_ref, s32[1,512]{1,0:T(1,128)S(1)} %bitcast.14, f32[3,512,512]{2,1,0:T(8,128)S(1)} %bitcast.10, f32[3,4,512,128]{3,2,1,0:T(8,128)S(1)} %get-tuple-element.28.force_ref), custom_call_target="tpu_custom_call" | custom-call | bytes 15000000 | tf_op jit(solution)/shard_map/base/pallas_call | solution.py:663
  65.4 6.5 %collective-permute-done.3.cb_ref = f32[3,8,128]{2,1,0:T(8,128)S(1)} collective-permute-done((f32[3,8,128]{2,1,0:T(8,128)S(1)}, f32[3,8,128]{2,1,0:T(8,128)S(1)}, u32[]{:S(2)}, u32[]{:S(2)}) %collective-permute-start.3) | collective-permute-done | bytes 12320 | tf_op jit(solution)/shard_map/ppermute | solution.py:566
  71.9 0.0 collective-permute-done.4.ca_ref
  71.9 0.0 collective-permute-done.below_ref.xb_ref
  71.9 2.3 %collective-permute-done.1.above_ref.xa_ref = f32[3,64,128]{2,1,0:T(8,128)S(1)} collective-permute-done((f32[3,64,128]{2,1,0:T(8,128)S(1)}, f32[3,64,128]{2,1,0:T(8,128)S(1)}, u32[]{:S(2)}, u32[]{:S(2)}) %collective-permute-start.1) | collective-permute-done | bytes 98336 | tf_op jit(solution)/shard_map/ppermute | solution.py:566
  74.2 0.0 collective-permute-done.2.yb_ref
  74.2 0.1 edge.1
  74.3 1.3 %collective-permute-start.5 = (f32[3,64,128]{2,1,0:T(8,128)S(1)}, f32[3,64,128]{2,1,0:T(8,128)S(1)}, u32[]{:S(2)}, u32[]{:S(2)}) collective-permute-start(f32[3,64,128]{2,1,0:T(8,128)S(1)} %get-tuple-element.39), channel_id=1, source_target_pairs={{1,0},{2,1},{3,2},{4,3},{5,4},{6,5},{7,6},{9,8},{10,9},{11,10},{12... | collective-permute-start | bytes 294920 | tf_op jit(solution)/shard_map/ppermute | solution.py:566
  75.6 1.2 %all-to-all-done.1.recv_ref = f32[128,48,128]{2,1,0:T(8,128)} async-done(((f32[128,48,128]{2,1,0:T(8,128)}), f32[128,48,128]{2,1,0:T(8,128)}, u32[]{:S(2)}, u32[]{:S(2)}) %all-to-all-start.1) | async-done | bytes 3145760 | tf_op jit(solution)/shard_map/all_to_all | solution.py:639
  76.8 4.3 %place.1 = (f32[3,512,512]{2,1,0:T(8,128)}, f32[3,64,512]{2,1,0:T(8,128)S(1)}) custom-call(s32[1,256]{1,0:T(1,128)S(1)} %get-tuple-element.25.peers_ref, s32[1,256]{1,0:T(1,128)S(1)} %get-tuple-element.26.slot_ref, f32[128,48,128]{2,1,0:T(8,128)} %all-to-all-done.1.recv_ref, f32[3,512,512]{2,1,0:T(8,128)} %get-tuple-element.29.base_ref, ...), custom_call_target="tpu_custom_call" | custom-call | bytes 9000000 | tf_op jit(solution)/shard_map/place/pallas_call | solution.py:688
  81.1 0.0 collective-permute-done.5.ya_ref
  81.1 1.1 %lines.1 = f32[3,512,512]{2,1,0:T(8,128)} custom-call(f32[3,64,512]{2,1,0:T(8,128)S(1)} %get-tuple-element.38.ends_ref, f32[3,64,128]{2,1,0:T(8,128)S(1)} %collective-permute-done.5.ya_ref, f32[3,512,512]{2,1,0:T(8,128)} %get-tuple-element.40.inner_ref), custom_call_target="tpu_custom_call", output_to_operand_aliasing={{}: (2, {})} | custom-call | bytes 3000000 | tf_op jit(solution)/shard_map/lines/pallas_call | solution.py:713
Async XLA Ops:
  7.7 23.4 %all-to-all-start = ((f32[128,768,1]{1,2,0:T(1,128)}), f32[128,768,1]{1,2,0:T(1,128)S(1)}, u32[]{:S(2)}, u32[]{:S(2)}) async-start(f32[128,768,1]{1,2,0:T(1,128)} %bitcast.18), calls=%async_computation | async-start | bytes 786432 | tf_op jit(solution)/shard_map/all_to_all | solution.py:628
  24.2 12.8 %copy-start = (f32[512,3,512]{2,0,1:T(8,128)S(1)}, f32[512,3,512]{2,0,1:T(8,128)}, u32[]{:S(2)}) copy-start(f32[512,3,512]{2,0,1:T(8,128)} %param.4) | copy-start | bytes 9437188
  24.3 12.8 %copy-start.2 = (s32[512]{0:T(512)S(1)}, s32[512]{0:T(512)}, u32[]{:S(2)}) copy-start(s32[512]{0:T(512)} %param.7) | copy-start | bytes 6148
  24.3 12.8 %copy-start.3 = (s32[512]{0:T(512)S(1)}, s32[512]{0:T(512)}, u32[]{:S(2)}) copy-start(s32[512]{0:T(512)} %param.6) | copy-start | bytes 6148
  31.1 45.7 %all-to-all-start.1 = ((f32[128,48,128]{2,1,0:T(8,128)}), f32[128,48,128]{2,1,0:T(8,128)}, u32[]{:S(2)}, u32[]{:S(2)}) async-start(f32[128,48,128]{2,1,0:T(8,128)} %pack.1), calls=%async_computation.1 | async-start | bytes 6291456 | tf_op jit(solution)/shard_map/all_to_all | solution.py:639
  37.1 1.0 %copy-start.1 = (f32[512,128]{1,0:T(8,128)S(1)}, f32[512,128]{1,0:T(8,128)}, u32[]{:S(2)}) copy-start(f32[512,128]{1,0:T(8,128)} %refs_4_.3) | copy-start | bytes 786436
  50.5 21.4 %collective-permute-start = (f32[3,64,128]{2,1,0:T(8,128)S(1)}, f32[3,64,128]{2,1,0:T(8,128)S(1)}, u32[]{:S(2)}, u32[]{:S(2)}) collective-permute-start(f32[3,64,128]{2,1,0:T(8,128)S(1)} %get-tuple-element.30), channel_id=1, source_target_pairs={{0,8},{1,9},{2,10},{3,11},{4,12},{5,13},{6,14},{7,15},{8,16},{9,17... | collective-permute-start | bytes 294920 | tf_op jit(solution)/shard_map/ppermute | solution.py:566
  53.1 21.2 %collective-permute-start.1 = (f32[3,64,128]{2,1,0:T(8,128)S(1)}, f32[3,64,128]{2,1,0:T(8,128)S(1)}, u32[]{:S(2)}, u32[]{:S(2)}) collective-permute-start(f32[3,64,128]{2,1,0:T(8,128)S(1)} %get-tuple-element.31), channel_id=1, source_target_pairs={{8,0},{9,1},{10,2},{11,3},{12,4},{13,5},{14,6},{15,7},{16,8},{17,9... | collective-permute-start | bytes 294920 | tf_op jit(solution)/shard_map/ppermute | solution.py:566
  54.4 19.9 %collective-permute-start.2 = (f32[3,64,128]{2,1,0:T(8,128)S(1)}, f32[3,64,128]{2,1,0:T(8,128)S(1)}, u32[]{:S(2)}, u32[]{:S(2)}) collective-permute-start(f32[3,64,128]{2,1,0:T(8,128)S(1)} %get-tuple-element.33), channel_id=1, source_target_pairs={{0,1},{1,2},{2,3},{3,4},{4,5},{5,6},{6,7},{8,9},{9,10},{10,11},{11... | collective-permute-start | bytes 294920 | tf_op jit(solution)/shard_map/ppermute | solution.py:566
  56.2 15.7 %collective-permute-start.3 = (f32[3,8,128]{2,1,0:T(8,128)S(1)}, f32[3,8,128]{2,1,0:T(8,128)S(1)}, u32[]{:S(2)}, u32[]{:S(2)}) collective-permute-start(f32[3,8,128]{2,1,0:T(8,128)S(1)} %get-tuple-element.34), channel_id=1, source_target_pairs={{0,9},{1,10},{2,11},{3,12},{4,13},{5,14},{6,15},{8,17},{9,18},{10,... | collective-permute-start | bytes 36872 | tf_op jit(solution)/shard_map/ppermute | solution.py:566
  62.1 9.9 %collective-permute-start.4 = (f32[3,8,128]{2,1,0:T(8,128)S(1)}, f32[3,8,128]{2,1,0:T(8,128)S(1)}, u32[]{:S(2)}, u32[]{:S(2)}) collective-permute-start(f32[3,8,128]{2,1,0:T(8,128)S(1)} %get-tuple-element.35), channel_id=1, source_target_pairs={{8,1},{9,2},{10,3},{11,4},{12,5},{13,6},{14,7},{16,9},{17,10},{18,... | collective-permute-start | bytes 36872 | tf_op jit(solution)/shard_map/ppermute | solution.py:566
  74.3 6.8 %collective-permute-start.5 = (f32[3,64,128]{2,1,0:T(8,128)S(1)}, f32[3,64,128]{2,1,0:T(8,128)S(1)}, u32[]{:S(2)}, u32[]{:S(2)}) collective-permute-start(f32[3,64,128]{2,1,0:T(8,128)S(1)} %get-tuple-element.39), channel_id=1, source_target_pairs={{1,0},{2,1},{3,2},{4,3},{5,4},{6,5},{7,6},{9,8},{10,9},{11,10},{12... | collective-permute-start | bytes 294920 | tf_op jit(solution)/shard_map/ppermute | solution.py:566
